TPU v7x, 32 devices: a whole 2x2x4 slice. The times are simulated.
32 devices in a mesh: grp: 2 (over x), tile: 4 (over z), tm: 4 (over y, core).
Axes of the slice: x: 2, y: 2, z: 4, core: 2. Of those that a mesh axis runs over, the one named last changes fastest.
Arguments:
- pixels: bfloat16 [6, 96, 400, 800], P('grp', 'tm', 'tile'), parts along dimension 0, may hold values from 0.049804688 to 1
- offsets: int32 [6, 20, 40, 2], P('grp'), parts along dimension 0, may hold values from -6 to 6
- subaperture_valid_mask: int32 [6, 96, 20, 40], P('grp', 'tm', 'tile'), parts along dimension 0, may hold values 0 or 1
- frame_count: int32 [8], P(('grp', 'tm')), parts along dimension 0, may hold values from 12 to 24, as said below
- slope_to_modes: bfloat16 [2, 3, 20, 40, 256], P(None, None, 'tile'), may hold values from -0.59765625 to 0.59765625
- process_noise: float32 [256], replicated, may hold values from 0.0002 to 0.2
- mode_gain: float32 [256], replicated, may hold values from 0.5 to 2
Outputs:
- smoothed_modes: float32 [192, 256], P(('grp', 'tm'), 'tile'), parts along dimension 0
- smoothed_variance: float32 [192, 256], P(('grp', 'tm'), 'tile'), parts along dimension 0
There are 2 independent parts, one for each index of `grp`. A program takes and returns all parts, laid end to end along the dimension named above; an argument that names none is the same for every part. Nothing has to cross between parts.
Inputs may be any that keep to these rules, and one draw needn't show every extreme that they name: `frame_count`: some block has all 24 frames live.
All inputs are finite; a program needn't handle non-finite values. No bound on the sum of `subaperture_valid_mask` on one device may be relied on, other than what follows from the above.
Results may differ from a plain program's by a relative error of at most 0.00094.
Values may be sent and summed in bfloat16 or wider, within the bound.
No kernel may reach another device: no remote copies, remote signals or barrier semaphores. Data moves between devices by JAX's collectives and lax.ppermute only.
A program may use at most 128 MiB of HBM per device.

v0:
```python
import functools

import jax
import jax.numpy as jnp
from jax import lax
from jax.experimental import pallas as pl
from jax.experimental.pallas import tpu as pltpu
from jax.sharding import PartitionSpec as P

SIDE = 20
CENTRE = (SIDE - 1) / 2.0
LANES = 128
VMEM_LIMIT = 56 * 1024 * 1024
VMEM = pl.BlockSpec(memory_space=pltpu.VMEM)
HBM = pl.BlockSpec(memory_space=pl.ANY)


def slot_of(strip, sensor):
    return (strip + 1 + sensor) % 3


def lane_iota(rows=1):
    return lax.broadcasted_iota(jnp.int32, (rows, LANES), 1)


def in_slot(lane, slot, cols):
    return (lane >= slot * cols) & (lane < (slot + 1) * cols)


def by_slot(lane, cols, values):
    out = jnp.zeros_like(values[0])
    for q, v in enumerate(values):
        out = jnp.where(in_slot(lane, q, cols), v, out)
    return out


def spread(v, cols):
    rows = v.shape[0]
    return jnp.concatenate([v, v, v, jnp.zeros((rows, LANES - 3 * cols), v.dtype)], axis=1)


def side_by_side(a, b, c):
    rows, cols = a.shape
    return jnp.concatenate([a, b, c, jnp.zeros((rows, LANES - 3 * cols), a.dtype)], axis=1)


def rotate(x, slots, cols):
    lane = lane_iota()
    shift = slots * cols
    near = pltpu.roll(x, shift, axis=1)
    far = pltpu.roll(x, LANES - 3 * cols + shift, axis=1)
    return jnp.where(lane >= shift, near, far)


def chunk_moments(x_ref, geo, w_ref, frames):
    rows, width = x_ref.shape
    col_pos = geo[0:1, :]
    row_pos = geo[1:2, :]
    base = lax.broadcasted_iota(jnp.int32, (16, LANES), 0).astype(jnp.float32) - col_pos
    for t in range(width // 16):
        d = base + float(16 * t)
        inside = jnp.abs(d) < 10.0
        w_ref[16 * t : 16 * t + 16, 0:LANES] = jnp.where(inside, 1.0, 0.0).astype(jnp.bfloat16)
        w_ref[16 * t : 16 * t + 16, LANES:] = jnp.where(inside, d, 0.0).astype(jnp.bfloat16)
    r = jnp.dot(x_ref[...], w_ref[...], preferred_element_type=jnp.float32)
    flux = jnp.zeros((frames, LANES), jnp.float32)
    cols = jnp.zeros((frames, LANES), jnp.float32)
    lines = jnp.zeros((frames, LANES), jnp.float32)
    for y in range(rows // frames):
        d = float(y) - row_pos
        inside = jnp.abs(d) < 10.0
        one = jnp.where(inside, 1.0, 0.0)
        centred = jnp.where(inside, d, 0.0)
        rf = r[y * frames : (y + 1) * frames, 0:LANES]
        rc = r[y * frames : (y + 1) * frames, LANES:]
        flux = flux + one * rf
        cols = cols + one * rc
        lines = lines + centred * rf
    return flux, cols, lines


def kernel_edge(sub_rows, sub_cols, frames, x_hbm, off_ref, p_ref, geo_ref, up_ref, down_ref, buf, w_ref, sem):
    sensors = x_hbm.shape[0]
    block = SIDE * frames
    last = sub_rows - 1

    def copy(s, e):
        start = pl.multiple_of(e * last * block, block)
        return pltpu.make_async_copy(
            x_hbm.at[s, pl.ds(start, block)], buf.at[2 * s + e], sem.at[2 * s + e]
        )

    for s in range(sensors):
        for e in range(2):
            copy(s, e).start()

    lane = lane_iota()
    index = lane - sub_cols * (lane >= sub_cols).astype(jnp.int32)
    index = index - sub_cols * (lane >= 2 * sub_cols).astype(jnp.int32)
    col_base = (SIDE * index).astype(jnp.float32) + CENTRE
    tile = lax.axis_index("tile")
    total_rows = off_ref.shape[1]
    for s in range(sensors):
        spread_rows = []
        for k in range(-1, sub_rows + 1):
            row = jnp.clip(tile * sub_rows + k, 0, total_rows - 1)
            v = off_ref[s, row].astype(jnp.float32)
            spread_rows.append(spread(v, sub_cols))
        for i in range(sub_rows):
            cs = [None] * 3
            rs = [None] * 3
            for k in (i - 1, i, i + 1):
                q = slot_of(k, s)
                v = spread_rows[k + 1]
                cs[q] = v[1:2] + col_base
                rs[q] = v[0:1] + (SIDE * (k - i) + CENTRE)
            used = lane < 3 * sub_cols
            col_pos = jnp.where(used, by_slot(lane, sub_cols, cs), -1000.0)
            row_pos = jnp.where(used, by_slot(lane, sub_cols, rs), -1000.0)
            geo_ref[s * sub_rows + i, 0:1, :] = col_pos
            geo_ref[s * sub_rows + i, 1:2, :] = row_pos

    def step(n, carry):
        s = n // 2
        e = n - 2 * s
        copy(s, e).wait()
        flux, cols, lines = chunk_moments(
            buf.at[n], geo_ref[s * sub_rows + e * last], w_ref, frames
        )
        p_ref[n, 0] = flux
        p_ref[n, 1] = cols
        p_ref[n, 2] = lines
        return carry

    lax.fori_loop(0, 2 * sensors, step, 0)
    for m in range(3):
        down = [None] * 3
        up = [None] * 3
        for s in range(sensors):
            down[slot_of(-1, s)] = p_ref[2 * s, m]
            up[slot_of(sub_rows, s)] = p_ref[2 * s + 1, m]
        down_ref[m] = by_slot(lane, sub_cols, down)
        up_ref[m] = by_slot(lane, sub_cols, up)


def slope_pair(flux, cols, lines, mask):
    live = mask > 0.0
    safe = jnp.where(live, flux, 1.0)
    sx = jnp.where(live, cols / safe, 0.0) * mask
    sy = jnp.where(live, lines / safe, 0.0) * mask
    return sx.astype(jnp.bfloat16), sy.astype(jnp.bfloat16)


def stacked(modes_ref, x, picks):
    parts = [modes_ref[x, s, k].astype(jnp.float32) for s, k in picks]
    used = sum(p.shape[0] for p in parts)
    parts.append(jnp.zeros((LANES - used, parts[0].shape[1]), jnp.float32))
    return jnp.concatenate(parts, axis=0).astype(jnp.bfloat16)


def kernel_inner(
    sub_rows, sub_cols, frames, x_hbm, geo_ref, pe_ref, mask_ref, modes_ref,
    pm_ref, edge_ref, em_ref, count_ref, buf, w_ref, acc_ref, sem,
):
    sensors = x_hbm.shape[0]
    block = SIDE * frames
    inner = sub_rows - 2
    last = sub_rows - 1

    def copy(s, i):
        start = pl.multiple_of((i + 1) * block, block)
        return pltpu.make_async_copy(
            x_hbm.at[s, pl.ds(start, block)], buf.at[inner * s + i], sem.at[inner * s + i]
        )

    for s in range(sensors):
        for i in range(inner):
            copy(s, i).start()

    lane = lane_iota()

    def step(n, carry):
        s = n // inner
        i = n - inner * s
        copy(s, i).wait()
        flux, cols, lines = chunk_moments(
            buf.at[n], geo_ref[s * sub_rows + i + 1], w_ref, frames
        )
        acc_ref[n, 0] = flux
        acc_ref[n, 1] = cols
        acc_ref[n, 2] = lines
        return carry

    lax.fori_loop(0, inner * sensors, step, 0)

    def partial(s, i, m):
        if i == 0:
            return pe_ref[2 * s, m]
        if i == last:
            return pe_ref[2 * s + 1, m]
        return acc_ref[inner * s + i - 1, m]

    def strip_total(s, k, m):
        total = None
        for i in (k - 1, k, k + 1):
            if 0 <= i <= last:
                v = partial(s, i, m)
                total = v if total is None else total + v
        return total

    masks = {}
    for s in range(sensors):
        for k in range(sub_rows):
            masks[s, k] = mask_ref[s, k].astype(jnp.float32)
    count = None
    for e, k in enumerate((0, last)):
        order = [None] * 3
        for s in range(sensors):
            order[slot_of(k, s)] = s
        m = side_by_side(*[masks[s, k] for s in order])
        em_ref[e] = m
        count = m if count is None else count + m
        for mom in range(3):
            edge_ref[e, mom] = by_slot(lane, sub_cols, [strip_total(s, k, mom) for s in order])
    modes = jnp.zeros((frames, modes_ref.shape[-1]), jnp.float32)
    for s in range(sensors):
        for g in range(1, last, 3):
            strips = list(range(g, min(g + 3, last)))
            order = sorted(strips, key=lambda k: slot_of(k, s))
            mask = side_by_side(*[masks[s, k] for k in order])
            count = count + mask
            mom = [
                by_slot(lane, sub_cols, [strip_total(s, k, m) for k in order]) for m in range(3)
            ]
            pair = slope_pair(mom[0], mom[1], mom[2], mask)
            for x in range(2):
                modes = modes + jnp.dot(
                    pair[x],
                    stacked(modes_ref, x, [(s, k) for k in order]),
                    preferred_element_type=jnp.float32,
                )
    pm_ref[...] = modes
    count_ref[...] = jnp.broadcast_to(jnp.sum(count, axis=1, keepdims=True), count_ref.shape)


def kernel_join(
    sub_rows, sub_cols, frames, tiles, blocks, total_subaps,
    live_ref, from_before_ref, from_after_ref, pm_ref, edge_ref, em_ref, count_ref, modes_ref, gain_ref,
    out_ref,
):
    sensors = modes_ref.shape[1]
    last = sub_rows - 1
    modes = pm_ref[...]
    for e, k in enumerate((0, last)):
        halo_ref = (from_before_ref, from_after_ref)[e]
        halo_strip = (sub_rows, -1)[e]
        turn = (slot_of(k, 0) - slot_of(halo_strip, 0)) % 3
        order = [None] * 3
        for s in range(sensors):
            order[slot_of(k, s)] = s
        mom = [edge_ref[e, m] + rotate(halo_ref[m], turn, sub_cols) for m in range(3)]
        pair = slope_pair(mom[0], mom[1], mom[2], em_ref[e])
        for x in range(2):
            modes = modes + jnp.dot(
                pair[x],
                stacked(modes_ref, x, [(s, k) for s in order]),
                preferred_element_type=jnp.float32,
            )
    gain = gain_ref[...]
    frame = lax.broadcasted_iota(jnp.int32, (frames, 1), 0)
    live = (frame < live_ref[0]).astype(jnp.float32)
    info_mean = gain * modes * live
    count = count_ref[...]
    count = jnp.concatenate([count] * (modes.shape[1] // LANES), axis=1)
    info_prec = gain * count * live / total_subaps
    share = modes.shape[1] // tiles
    for t in range(tiles):
        piece = jnp.concatenate(
            [info_mean[:, t * share : (t + 1) * share], info_prec[:, t * share : (t + 1) * share]],
            axis=1,
        )
        for b in range(blocks):
            out_ref[t * blocks + b] = piece


def shifted(x, by, fill, back):
    rows = x.shape[0]
    if by % 8 == 0:
        pad = jnp.full((by, x.shape[1]), fill, x.dtype)
        if back:
            return jnp.concatenate([x[by:], pad], axis=0)
        return jnp.concatenate([pad, x[: rows - by]], axis=0)
    row = lax.broadcasted_iota(jnp.int32, (rows, 1), 0)
    if back:
        return jnp.where(row < rows - by, pltpu.roll(x, rows - by, axis=0), fill)
    return jnp.where(row >= by, pltpu.roll(x, by, axis=0), fill)


def kernel_smooth(tiles, blocks, frames, in_ref, noise_ref, mean_ref, var_ref, mean_scr, var_scr):
    share = mean_ref.shape[1]
    total = blocks * frames
    tile = lax.axis_index("tile")
    time = lax.axis_index("tm")
    noise_all = noise_ref[...]
    q = jnp.zeros((1, share), jnp.float32)
    for t in range(tiles):
        q = jnp.where(tile == t, noise_all[:, t * share : (t + 1) * share], q)
    summed = []
    for b in range(blocks):
        v = in_ref[b]
        for t in range(1, tiles):
            v = v + in_ref[t * blocks + b]
        summed.append(v)
    both = jnp.concatenate(summed, axis=0)
    info_mean = both[:, :share]
    prec = both[:, share:]
    row = lax.broadcasted_iota(jnp.int32, (total, 1), 0)
    first = row == 0
    retain = 1.0 / (1.0 + q * prec)
    a = jnp.where(first, 0.0, retain)
    c = jnp.where(first, 1.0 / (1.0 + prec), q * retain)
    b = c * info_mean
    e = a * info_mean
    j = a * prec
    by = 1
    while by < total:
        a1 = shifted(a, by, 1.0, False)
        b1 = shifted(b, by, 0.0, False)
        c1 = shifted(c, by, 0.0, False)
        e1 = shifted(e, by, 0.0, False)
        j1 = shifted(j, by, 0.0, False)
        damp = 1.0 / (1.0 + c1 * j)
        left = a * damp
        right = a1 * damp
        b = left * (b1 + c1 * e) + b
        c = left * a * c1 + c
        e, j = right * (e - j * b1) + e1, right * a1 * j + j1
        a = left * a1
        by *= 2
    g = jnp.where(row == total - 1, 0.0, c / (c + q))
    m = (1.0 - g) * b
    v = c * (1.0 - g)
    by = 1
    while by < total:
        g1 = shifted(g, by, 1.0, True)
        m1 = shifted(m, by, 0.0, True)
        v1 = shifted(v, by, 0.0, True)
        m = g * m1 + m
        v = g * g * v1 + v
        g = g * g1
        by *= 2
    mean_scr[...] = m
    var_scr[...] = v
    start = pl.multiple_of(time * frames, 8)
    mean_ref[...] = mean_scr[pl.ds(start, frames), :]
    var_ref[...] = var_scr[pl.ds(start, frames), :]


def body(pixels, offsets, mask, frame_count, slope_to_modes, process_noise, mode_gain):
    sensors, frames, lines, width = pixels.shape
    sub_rows, sub_cols = mask.shape[2], mask.shape[3]
    modes = process_noise.shape[0]
    tiles = lax.axis_size("tile")
    blocks = lax.axis_size("tm")
    share = modes // tiles
    total_subaps = sensors * sub_rows * tiles * sub_cols
    f32 = jnp.float32
    x = jnp.transpose(pixels, (0, 2, 1, 3)).reshape(sensors, lines * frames, width)
    off = jnp.transpose(offsets, (0, 1, 3, 2))
    msk = jnp.transpose(mask, (0, 2, 1, 3))
    block = SIDE * frames
    inner = sub_rows - 2
    params = pltpu.CompilerParams(vmem_limit_bytes=VMEM_LIMIT)

    def cost(chunks):
        return pl.CostEstimate(
            flops=2 * chunks * block * width * 256, bytes_accessed=chunks * block * width * 2, transcendentals=0
        )

    parts, geo, up, down = pl.pallas_call(
        functools.partial(kernel_edge, sub_rows, sub_cols, frames),
        out_shape=(
            jax.ShapeDtypeStruct((2 * sensors, 3, frames, LANES), f32),
            jax.ShapeDtypeStruct((sensors * sub_rows, 8, LANES), f32),
            jax.ShapeDtypeStruct((3, frames, LANES), f32),
            jax.ShapeDtypeStruct((3, frames, LANES), f32),
        ),
        in_specs=[HBM, VMEM],
        out_specs=(VMEM, VMEM, VMEM, VMEM),
        scratch_shapes=[
            pltpu.VMEM((2 * sensors, block, width), jnp.bfloat16),
            pltpu.VMEM((width, 2 * LANES), jnp.bfloat16),
            pltpu.SemaphoreType.DMA((2 * sensors,)),
        ],
        compiler_params=params,
        cost_estimate=cost(2 * sensors),
        name="edge_moments",
    )(x, off)
    onward = [(i, i + 1) for i in range(tiles - 1)]
    backward = [(j, i) for i, j in onward]
    from_before = lax.ppermute(up, "tile", onward)
    from_after = lax.ppermute(down, "tile", backward)
    partial_modes, edge, edge_mask, count = pl.pallas_call(
        functools.partial(kernel_inner, sub_rows, sub_cols, frames),
        out_shape=(
            jax.ShapeDtypeStruct((frames, modes), f32),
            jax.ShapeDtypeStruct((2, 3, frames, LANES), f32),
            jax.ShapeDtypeStruct((2, frames, LANES), f32),
            jax.ShapeDtypeStruct((frames, LANES), f32),
        ),
        in_specs=[HBM, VMEM, VMEM, VMEM, VMEM],
        out_specs=(VMEM, VMEM, VMEM, VMEM),
        scratch_shapes=[
            pltpu.VMEM((inner * sensors, block, width), jnp.bfloat16),
            pltpu.VMEM((width, 2 * LANES), jnp.bfloat16),
            pltpu.VMEM((inner * sensors, 3, frames, LANES), f32),
            pltpu.SemaphoreType.DMA((inner * sensors,)),
        ],
        compiler_params=params,
        cost_estimate=cost(inner * sensors),
        name="inner_moments",
    )(x, geo, parts, msk, slope_to_modes)
    payload = pl.pallas_call(
        functools.partial(kernel_join, sub_rows, sub_cols, frames, tiles, blocks, float(total_subaps)),
        out_shape=jax.ShapeDtypeStruct((tiles * blocks, frames, 2 * share), f32),
        in_specs=[pl.BlockSpec(memory_space=pltpu.SMEM)] + [VMEM] * 8,
        out_specs=VMEM,
        compiler_params=params,
        name="join_halo",
    )(
        frame_count, from_before, from_after, partial_modes, edge, edge_mask, count,
        slope_to_modes, mode_gain.reshape(1, modes),
    )
    info = lax.all_to_all(payload, ("tile", "tm"), 0, 0)
    return pl.pallas_call(
        functools.partial(kernel_smooth, tiles, blocks, frames),
        out_shape=(
            jax.ShapeDtypeStruct((frames, share), f32),
            jax.ShapeDtypeStruct((frames, share), f32),
        ),
        in_specs=[VMEM, VMEM],
        out_specs=(VMEM, VMEM),
        scratch_shapes=[
            pltpu.VMEM((blocks * frames, share), f32),
            pltpu.VMEM((blocks * frames, share), f32),
        ],
        compiler_params=params,
        name="smooth",
    )(info, process_noise.reshape(1, modes))


def solution(mesh):
    return jax.shard_map(
        body,
        mesh=mesh,
        in_specs=(
            P("grp", "tm", "tile", None),
            P("grp", None, None, None),
            P("grp", "tm", "tile", None),
            P(("grp", "tm")),
            P(None, None, "tile", None, None),
            P(),
            P(),
        ),
        out_specs=(P(("grp", "tm"), "tile"), P(("grp", "tm"), "tile")),
        check_vma=False,
    )
```

profile of v0, /device:TPU:0, one launch (start us, length us, event | category | flops | bytes accessed | tf_op | source)
XLA Modules:
  0.0 42.6 jit_solution(14951668424906388811)
XLA Ops:
  0.6 5.9 %edge_moments.1 = (f32[6,3,24,128]{3,2,1,0:T(8,128)}, f32[15,8,128]{2,1,0:T(8,128)}, f32[3,24,128]{2,1,0:T(8,128)}, f32[3,24,128]{2,1,0:T(8,128)}) custom-call(bf16[3,2400,800]{2,1,0:T(8,128)(2,1)} %bitcast.7, s32[3,20,2,40]{3,2,1,0:T(2,128)} %bitcast.10), custom_call_target="tpu_custom_call" | custom-call | flops 1179648000 | bytes 4608000 | tf_op jit(solution)/shard_map/edge_moments/pallas_call | solution.py:380
  6.5 4.9 %collective-permute-start = (f32[3,24,128]{2,1,0:T(8,128)}, f32[3,24,128]{2,1,0:T(8,128)S(1)}, u32[]{:S(2)}, u32[]{:S(2)}) collective-permute-start(f32[3,24,128]{2,1,0:T(8,128)} %get-tuple-element.10), channel_id=1, source_target_pairs={{0,4},{4,8},{8,12},{1,5},{5,9},{9,13},{2,6},{6,10},{10,14},{3,7},{... | collective-permute-start | bytes 110600 | tf_op jit(solution)/shard_map/ppermute | solution.py:401
  11.4 1.3 %collective-permute-start.1 = (f32[3,24,128]{2,1,0:T(8,128)}, f32[3,24,128]{2,1,0:T(8,128)S(1)}, u32[]{:S(2)}, u32[]{:S(2)}) collective-permute-start(f32[3,24,128]{2,1,0:T(8,128)} %get-tuple-element.11), channel_id=1, source_target_pairs={{4,0},{8,4},{12,8},{5,1},{9,5},{13,9},{6,2},{10,6},{14,10},{7,3},{... | collective-permute-start | bytes 110600 | tf_op jit(solution)/shard_map/ppermute | solution.py:402
  12.7 8.1 %inner_moments.1 = (f32[24,256]{1,0:T(8,128)}, f32[2,3,24,128]{3,2,1,0:T(8,128)}, f32[2,24,128]{2,1,0:T(8,128)}, f32[24,128]{1,0:T(8,128)}) custom-call(bf16[3,2400,800]{2,1,0:T(8,128)(2,1)} %bitcast.8, f32[15,8,128]{2,1,0:T(8,128)} %get-tuple-element.12.geo_ref, f32[6,3,24,128]{3,2,1,0:T(8,128)} %get-tuple-element.13.pe_ref, s32[3,5,24,40]{3,2,1,0:T(8,128)} %bitcast.9, ...), custom_call_target="tpu_custom_call" | custom-call | flops 1769472000 | bytes 6912000 | tf_op jit(solution)/shard_map/inner_moments/pallas_call | solution.py:403
  21.5 0.0 collective-permute-done.from_before_ref
  21.5 0.0 copy-start
  21.5 0.0 collective-permute-done.1.from_after_ref
  21.5 0.0 copy-start.1
  21.5 0.6 %copy-done = f32[3,24,128]{2,1,0:T(8,128)} copy-done((f32[3,24,128]{2,1,0:T(8,128)}, f32[3,24,128]{2,1,0:T(8,128)S(1)}, u32[]{:S(2)}) %copy-start) | copy-done | bytes 36888
  22.1 0.0 copy-done.1
  22.1 2.2 %join_halo.1 = f32[16,24,128]{2,1,0:T(8,128)} custom-call(s32[1]{0:T(128)S(6)} %copy.9.live_ref, f32[3,24,128]{2,1,0:T(8,128)} %copy-done, f32[3,24,128]{2,1,0:T(8,128)} %copy-done.1, f32[24,256]{1,0:T(8,128)} %get-tuple-element.14.pm_ref, f32[2,3,24,128]{3,2,1,0:T(8,128)} %get-tuple-element.15.edge_ref, f32[2,24,128]{2,1,0:T(8,128)} %get-tuple-element.16.em_ref, ...), custom_call_target="tpu_custom_call" | custom-call | tf_op jit(solution)/shard_map/join_halo/pallas_call | solution.py:423
  24.3 16.1 %all_to_all.5.in_ref = f32[16,24,128]{2,1,0:T(8,128)} all-to-all(f32[16,24,128]{2,1,0:T(8,128)} %join_halo.1), channel_id=1, replica_groups=mesh['grp'=2,'tile'=4,'tm'=4] {'tile','tm'}, dimensions={0} | all-to-all | bytes 393216 | tf_op jit(solution)/shard_map/all_to_all | solution.py:434
  40.4 2.2 %smooth.1 = (f32[24,64]{1,0:T(8,128)}, f32[24,64]{1,0:T(8,128)}) custom-call(f32[16,24,128]{2,1,0:T(8,128)} %all_to_all.5.in_ref, f32[1,256]{1,0:T(1,128)} %bitcast.11), custom_call_target="tpu_custom_call" | custom-call | tf_op jit(solution)/shard_map/smooth/pallas_call | solution.py:435
Async XLA Ops:
  6.5 15.0 %collective-permute-start = (f32[3,24,128]{2,1,0:T(8,128)}, f32[3,24,128]{2,1,0:T(8,128)S(1)}, u32[]{:S(2)}, u32[]{:S(2)}) collective-permute-start(f32[3,24,128]{2,1,0:T(8,128)} %get-tuple-element.10), channel_id=1, source_target_pairs={{0,4},{4,8},{8,12},{1,5},{5,9},{9,13},{2,6},{6,10},{10,14},{3,7},{... | collective-permute-start | bytes 110600 | tf_op jit(solution)/shard_map/ppermute | solution.py:401
  11.4 10.1 %collective-permute-start.1 = (f32[3,24,128]{2,1,0:T(8,128)}, f32[3,24,128]{2,1,0:T(8,128)S(1)}, u32[]{:S(2)}, u32[]{:S(2)}) collective-permute-start(f32[3,24,128]{2,1,0:T(8,128)} %get-tuple-element.11), channel_id=1, source_target_pairs={{4,0},{8,4},{12,8},{5,1},{9,5},{13,9},{6,2},{10,6},{14,10},{7,3},{... | collective-permute-start | bytes 110600 | tf_op jit(solution)/shard_map/ppermute | solution.py:402
  21.5 0.6 %copy-start = (f32[3,24,128]{2,1,0:T(8,128)}, f32[3,24,128]{2,1,0:T(8,128)S(1)}, u32[]{:S(2)}) copy-start(f32[3,24,128]{2,1,0:T(8,128)S(1)} %collective-permute-done.from_before_ref) | copy-start | bytes 110596
  21.5 0.6 %copy-start.1 = (f32[3,24,128]{2,1,0:T(8,128)}, f32[3,24,128]{2,1,0:T(8,128)S(1)}, u32[]{:S(2)}) copy-start(f32[3,24,128]{2,1,0:T(8,128)S(1)} %collective-permute-done.1.from_after_ref) | copy-start | bytes 110596
where the time goes:
time: 43 us; the launch traced here: 42.6 us
  Pallas kernels  18.3 us (43%)
  blocking collectives  16.1 us (37%)
  starting transfers between devices  6.21 us (14%)
  between operations  1.34 us (3%)
  local copies, waits for them, and re-layouts  0.61 us (1%)
    all_to_all x1, blocking collectives, body(): info = lax.all_to_all(payload, ('tile', 'tm'), 0, 0)  16.1 us
    pallas_call x1, Pallas kernels, body(): pl.pallas_call(functools.partial(kernel_inner, sub_rows, sub_cols, frames...  8.08 us
    pallas_call x1, Pallas kernels, body(): pl.pallas_call(functools.partial(kernel_edge, sub_rows, sub_cols, frames)...  5.87 us
    ppermute x1, starting transfers between devices, body(): from_before = lax.ppermute(up, 'tile', onward)  4.92 us
    pallas_call x1, Pallas kernels, body(): pl.pallas_call(functools.partial(kernel_smooth, tiles, blocks, frames), o...  2.2 us
    pallas_call x1, Pallas kernels, body(): pl.pallas_call(functools.partial(kernel_join, sub_rows, sub_cols, frames,...  2.18 us
    ppermute x1, starting transfers between devices, body(): from_after = lax.ppermute(down, 'tile', backward)  1.29 us
  transfers between devices with their start and end apart: 2, of which 0 were waited for; matrix products, arithmetic and copies ran while one was open for 0% of the time, Pallas kernels for 19%

commit v1 on v0

v1 whole, which is shorter than its diff:
```python
import functools

import jax
import jax.numpy as jnp
from jax import lax
from jax.experimental import pallas as pl
from jax.experimental.pallas import tpu as pltpu
from jax.sharding import PartitionSpec as P

SIDE = 20
CENTRE = (SIDE - 1) / 2.0
LANES = 128
VMEM_LIMIT = 56 * 1024 * 1024
VMEM = pl.BlockSpec(memory_space=pltpu.VMEM)
HBM = pl.BlockSpec(memory_space=pl.ANY)


def slot_of(strip, sensor):
    return (strip + 1 + sensor) % 3


def lane_iota(rows=1):
    return lax.broadcasted_iota(jnp.int32, (rows, LANES), 1)


def in_slot(lane, slot, cols):
    return (lane >= slot * cols) & (lane < (slot + 1) * cols)


def by_slot(lane, cols, values):
    out = jnp.zeros_like(values[0])
    for q, v in enumerate(values):
        out = jnp.where(in_slot(lane, q, cols), v, out)
    return out


def spread(v, cols):
    rows = v.shape[0]
    return jnp.concatenate([v, v, v, jnp.zeros((rows, LANES - 3 * cols), v.dtype)], axis=1)


def side_by_side(a, b, c):
    rows, cols = a.shape
    return jnp.concatenate([a, b, c, jnp.zeros((rows, LANES - 3 * cols), a.dtype)], axis=1)


def rotate(x, slots, cols):
    lane = lane_iota()
    shift = slots * cols
    near = pltpu.roll(x, shift, axis=1)
    far = pltpu.roll(x, LANES - 3 * cols + shift, axis=1)
    return jnp.where(lane >= shift, near, far)


def build_weights(geo, w_ref):
    base = lax.broadcasted_iota(jnp.int32, (16, LANES), 0).astype(jnp.float32) - geo[0:1, :]
    for t in range(w_ref.shape[0] // 16):
        d = base + float(16 * t)
        inside = jnp.abs(d) < 10.0
        w_ref[16 * t : 16 * t + 16, 0:LANES] = jnp.where(inside, 1.0, 0.0).astype(jnp.bfloat16)
        w_ref[16 * t : 16 * t + 16, LANES:] = jnp.where(inside, d, 0.0).astype(jnp.bfloat16)


def row_sums(geo, r_ref, p_ref, frames):
    row_pos = geo[1:2, :]
    flux = jnp.zeros((frames, LANES), jnp.float32)
    cols = jnp.zeros((frames, LANES), jnp.float32)
    lines = jnp.zeros((frames, LANES), jnp.float32)
    for y in range(r_ref.shape[0] // frames):
        d = float(y) - row_pos
        inside = jnp.abs(d) < 10.0
        one = jnp.where(inside, 1.0, 0.0)
        centred = jnp.where(inside, d, 0.0)
        rf = r_ref[y * frames : (y + 1) * frames, 0:LANES]
        rc = r_ref[y * frames : (y + 1) * frames, LANES:]
        flux = flux + one * rf
        cols = cols + one * rc
        lines = lines + centred * rf
    p_ref[0] = flux
    p_ref[1] = cols
    p_ref[2] = lines


def geometry(geo_ref, off_ref, sensors, sub_rows, sub_cols):
    lane = lane_iota()
    index = lane - sub_cols * (lane >= sub_cols).astype(jnp.int32)
    index = index - sub_cols * (lane >= 2 * sub_cols).astype(jnp.int32)
    col_base = (SIDE * index).astype(jnp.float32) + CENTRE
    used = lane < 3 * sub_cols
    tile = lax.axis_index("tile")
    total_rows = off_ref.shape[1]
    for s in range(sensors):
        spread_rows = []
        for k in range(-1, sub_rows + 1):
            row = jnp.clip(tile * sub_rows + k, 0, total_rows - 1)
            v = off_ref[s, row].astype(jnp.float32)
            spread_rows.append(spread(v, sub_cols))
        for i in range(sub_rows):
            cs = [None] * 3
            rs = [None] * 3
            for k in (i - 1, i, i + 1):
                q = slot_of(k, s)
                v = spread_rows[k + 1]
                cs[q] = v[1:2] + col_base
                rs[q] = v[0:1] + (SIDE * (k - i) + CENTRE)
            geo_ref[s, i, 0:1, :] = jnp.where(used, by_slot(lane, sub_cols, cs), -1000.0)
            geo_ref[s, i, 1:2, :] = jnp.where(used, by_slot(lane, sub_cols, rs), -1000.0)


def slope_pair(flux, cols, lines, mask):
    live = mask > 0.0
    safe = jnp.where(live, flux, 1.0)
    sx = jnp.where(live, cols / safe, 0.0) * mask
    sy = jnp.where(live, lines / safe, 0.0) * mask
    return sx.astype(jnp.bfloat16), sy.astype(jnp.bfloat16)


def stacked(modes_ref, x, picks):
    parts = [modes_ref[x, s, k].astype(jnp.float32) for s, k in picks]
    used = sum(p.shape[0] for p in parts)
    parts.append(jnp.zeros((LANES - used, parts[0].shape[1]), jnp.float32))
    return jnp.concatenate(parts, axis=0).astype(jnp.bfloat16)


def kernel_moments(
    sub_rows, sub_cols, frames, x_hbm, off_hbm, mask_hbm, modes_hbm,
    pm_ref, edge_ref, em_ref, count_ref, halo_ref,
    buf, w_ref, r_ref, p_ref, geo_ref, off_ref, mask_ref, modes_ref, sem, side_sem,
):
    sensors = x_hbm.shape[0]
    block = SIDE * frames
    last = sub_rows - 1

    def copy(s, i):
        return pltpu.make_async_copy(
            x_hbm.at[s, pl.ds(i * block, block)], buf.at[s, i], sem.at[s, i]
        )

    off_copy = pltpu.make_async_copy(off_hbm, off_ref, side_sem.at[0])
    mask_copy = pltpu.make_async_copy(mask_hbm, mask_ref, side_sem.at[1])
    modes_copy = pltpu.make_async_copy(modes_hbm, modes_ref, side_sem.at[2])
    off_copy.start()
    for s in range(sensors):
        for i in range(sub_rows):
            copy(s, i).start()
    mask_copy.start()
    modes_copy.start()
    off_copy.wait()
    geometry(geo_ref, off_ref, sensors, sub_rows, sub_cols)
    build_weights(geo_ref[0, 0], w_ref.at[0])

    def step(s, carry):
        for i in range(sub_rows):
            copy(s, i).wait()
            if i < last:
                build_weights(geo_ref[s, i + 1], w_ref.at[i + 1])
            else:
                build_weights(geo_ref[jnp.minimum(s + 1, sensors - 1), 0], w_ref.at[0])
            r_ref[i] = jnp.dot(buf[s, i], w_ref[i], preferred_element_type=jnp.float32)
            if i > 0:
                row_sums(geo_ref[s, i - 1], r_ref.at[i - 1], p_ref.at[s, i - 1], frames)
        row_sums(geo_ref[s, last], r_ref.at[last], p_ref.at[s, last], frames)
        return carry

    lax.fori_loop(0, sensors, step, 0)
    lane = lane_iota()

    def strip_total(s, k, m):
        total = None
        for i in (k - 1, k, k + 1):
            if 0 <= i <= last:
                v = p_ref[s, i, m]
                total = v if total is None else total + v
        return total

    for m in range(3):
        down = [None] * 3
        up = [None] * 3
        for s in range(sensors):
            down[slot_of(-1, s)] = p_ref[s, 0, m]
            up[slot_of(sub_rows, s)] = p_ref[s, last, m]
        halo_ref[0, m] = by_slot(lane, sub_cols, up)
        halo_ref[1, m] = by_slot(lane, sub_cols, down)
    mask_copy.wait()
    modes_copy.wait()
    masks = {}
    for s in range(sensors):
        for k in range(sub_rows):
            masks[s, k] = mask_ref[s, k].astype(jnp.float32)
    count = None
    for e, k in enumerate((0, last)):
        order = [None] * 3
        for s in range(sensors):
            order[slot_of(k, s)] = s
        m = side_by_side(*[masks[s, k] for s in order])
        em_ref[e] = m
        count = m if count is None else count + m
        for mom in range(3):
            edge_ref[e, mom] = by_slot(lane, sub_cols, [strip_total(s, k, mom) for s in order])
    modes = jnp.zeros((frames, modes_ref.shape[-1]), jnp.float32)
    for s in range(sensors):
        for g in range(1, last, 3):
            strips = list(range(g, min(g + 3, last)))
            order = sorted(strips, key=lambda k: slot_of(k, s))
            mask = side_by_side(*[masks[s, k] for k in order])
            count = count + mask
            mom = [
                by_slot(lane, sub_cols, [strip_total(s, k, m) for k in order]) for m in range(3)
            ]
            pair = slope_pair(mom[0], mom[1], mom[2], mask)
            for x in range(2):
                modes = modes + jnp.dot(
                    pair[x],
                    stacked(modes_ref, x, [(s, k) for k in order]),
                    preferred_element_type=jnp.float32,
                )
    pm_ref[...] = modes
    count_ref[...] = jnp.broadcast_to(jnp.sum(count, axis=1, keepdims=True), count_ref.shape)


def kernel_join(
    sub_rows, sub_cols, frames, tiles,
    live_ref, halo_ref, pm_ref, edge_ref, em_ref, count_ref, modes_ref, gain_ref, out_ref,
):
    sensors = modes_ref.shape[1]
    last = sub_rows - 1
    modes = pm_ref[...]
    tile = lax.axis_index("tile")
    for e, k in enumerate((0, last)):
        halo_strip = (sub_rows, -1)[e]
        near = (jnp.maximum(tile - 1, 0), jnp.minimum(tile + 1, tiles - 1))[e]
        there = (tile > 0, tile < tiles - 1)[e]
        turn = (slot_of(k, 0) - slot_of(halo_strip, 0)) % 3
        order = [None] * 3
        for s in range(sensors):
            order[slot_of(k, s)] = s
        mom = [
            edge_ref[e, m] + rotate(jnp.where(there, halo_ref[near, e, m], 0.0), turn, sub_cols)
            for m in range(3)
        ]
        pair = slope_pair(mom[0], mom[1], mom[2], em_ref[e])
        for x in range(2):
            modes = modes + jnp.dot(
                pair[x],
                stacked(modes_ref, x, [(s, k) for s in order]),
                preferred_element_type=jnp.float32,
            )
    frame = lax.broadcasted_iota(jnp.int32, (frames, 1), 0)
    live = (frame < live_ref[0]).astype(jnp.float32)
    out_ref[0:frames, :] = gain_ref[...] * modes * live
    lane = lane_iota(frames)
    own = lane == lax.broadcasted_iota(jnp.int32, (frames, LANES), 0)
    count_row = jnp.sum(jnp.where(own, count_ref[...] * live, 0.0), axis=0, keepdims=True)
    out_ref[frames : frames + 8, :] = jnp.zeros((8, modes.shape[1]), jnp.float32)
    out_ref[frames : frames + 1, 0:LANES] = count_row


def shifted(x, by, fill, back):
    rows = x.shape[0]
    if by % 8 == 0:
        pad = jnp.full((by, x.shape[1]), fill, x.dtype)
        if back:
            return jnp.concatenate([x[by:], pad], axis=0)
        return jnp.concatenate([pad, x[: rows - by]], axis=0)
    row = lax.broadcasted_iota(jnp.int32, (rows, 1), 0)
    if back:
        return jnp.where(row < rows - by, pltpu.roll(x, rows - by, axis=0), fill)
    return jnp.where(row >= by, pltpu.roll(x, by, axis=0), fill)


def kernel_smooth(tiles, blocks, frames, total_subaps, in_ref, noise_ref, gain_ref, mean_ref, var_ref, mean_scr, var_scr):
    share = mean_ref.shape[1]
    total = blocks * frames
    tile = lax.axis_index("tile")
    time = lax.axis_index("tm")
    def own_modes(v):
        out = v[:, 0:share]
        for t in range(1, tiles):
            out = jnp.where(tile == t, v[:, t * share : (t + 1) * share], out)
        return out

    q = own_modes(noise_ref[...])
    gain = own_modes(gain_ref[...])
    own = lane_iota(frames) == lax.broadcasted_iota(jnp.int32, (frames, LANES), 0)
    summed = []
    counts = []
    for b in range(blocks):
        v = in_ref[b]
        for t in range(1, tiles):
            v = v + in_ref[t * blocks + b]
        summed.append(v[0:frames])
        count_row = v[frames : frames + 1, 0:LANES]
        counts.append(jnp.sum(jnp.where(own, count_row, 0.0), axis=1, keepdims=True))
    info_mean = own_modes(jnp.concatenate(summed, axis=0))
    prec = gain * jnp.concatenate(counts, axis=0) / total_subaps
    row = lax.broadcasted_iota(jnp.int32, (total, 1), 0)
    first = row == 0
    retain = 1.0 / (1.0 + q * prec)
    a = jnp.where(first, 0.0, retain)
    c = jnp.where(first, 1.0 / (1.0 + prec), q * retain)
    b = c * info_mean
    e = a * info_mean
    j = a * prec
    by = 1
    while by < total:
        a1 = shifted(a, by, 1.0, False)
        b1 = shifted(b, by, 0.0, False)
        c1 = shifted(c, by, 0.0, False)
        e1 = shifted(e, by, 0.0, False)
        j1 = shifted(j, by, 0.0, False)
        damp = 1.0 / (1.0 + c1 * j)
        left = a * damp
        right = a1 * damp
        b = left * (b1 + c1 * e) + b
        c = left * a * c1 + c
        e, j = right * (e - j * b1) + e1, right * a1 * j + j1
        a = left * a1
        by *= 2
    g = jnp.where(row == total - 1, 0.0, c / (c + q))
    m = (1.0 - g) * b
    v = c * (1.0 - g)
    by = 1
    while by < total:
        g1 = shifted(g, by, 1.0, True)
        m1 = shifted(m, by, 0.0, True)
        v1 = shifted(v, by, 0.0, True)
        m = g * m1 + m
        v = g * g * v1 + v
        g = g * g1
        by *= 2
    mean_scr[...] = m
    var_scr[...] = v
    start = pl.multiple_of(time * frames, 8)
    mean_ref[...] = mean_scr[pl.ds(start, frames), :]
    var_ref[...] = var_scr[pl.ds(start, frames), :]


def body(pixels, offsets, mask, frame_count, slope_to_modes, process_noise, mode_gain):
    sensors, frames, lines, width = pixels.shape
    sub_rows, sub_cols = mask.shape[2], mask.shape[3]
    modes = process_noise.shape[0]
    tiles = lax.axis_size("tile")
    blocks = lax.axis_size("tm")
    share = modes // tiles
    total_subaps = sensors * sub_rows * tiles * sub_cols
    f32 = jnp.float32
    x = jnp.transpose(pixels, (0, 2, 1, 3)).reshape(sensors, lines * frames, width)
    off = jnp.transpose(offsets, (0, 1, 3, 2))
    msk = jnp.transpose(mask, (0, 2, 1, 3))
    block = SIDE * frames
    params = pltpu.CompilerParams(vmem_limit_bytes=VMEM_LIMIT)

    def cost(chunks):
        return pl.CostEstimate(
            flops=2 * chunks * block * width * 256, bytes_accessed=chunks * block * width * 2, transcendentals=0
        )

    bf16 = jnp.bfloat16
    partial_modes, edge, edge_mask, count, halo = pl.pallas_call(
        functools.partial(kernel_moments, sub_rows, sub_cols, frames),
        out_shape=(
            jax.ShapeDtypeStruct((frames, modes), f32),
            jax.ShapeDtypeStruct((2, 3, frames, LANES), f32),
            jax.ShapeDtypeStruct((2, frames, LANES), f32),
            jax.ShapeDtypeStruct((frames, LANES), f32),
            jax.ShapeDtypeStruct((2, 3, frames, LANES), f32),
        ),
        in_specs=[HBM] * 4,
        out_specs=(VMEM,) * 5,
        scratch_shapes=[
            pltpu.VMEM((sensors, sub_rows, block, width), bf16),
            pltpu.VMEM((sub_rows, width, 2 * LANES), bf16),
            pltpu.VMEM((sub_rows, block, 2 * LANES), f32),
            pltpu.VMEM((sensors, sub_rows, 3, frames, LANES), f32),
            pltpu.VMEM((sensors, sub_rows, 8, LANES), f32),
            pltpu.VMEM(off.shape, off.dtype),
            pltpu.VMEM(msk.shape, msk.dtype),
            pltpu.VMEM(slope_to_modes.shape, bf16),
            pltpu.SemaphoreType.DMA((sensors, sub_rows)),
            pltpu.SemaphoreType.DMA((3,)),
        ],
        compiler_params=params,
        cost_estimate=cost(sensors * sub_rows),
        name="moments",
    )(x, off, msk, slope_to_modes)
    halos = lax.all_gather(halo, "tile")
    gain = mode_gain.reshape(1, modes)
    payload = pl.pallas_call(
        functools.partial(kernel_join, sub_rows, sub_cols, frames, tiles),
        out_shape=jax.ShapeDtypeStruct((frames + 8, modes), f32),
        in_specs=[pl.BlockSpec(memory_space=pltpu.SMEM)] + [VMEM] * 7,
        out_specs=VMEM,
        compiler_params=params,
        name="join_halo",
    )(frame_count, halos, partial_modes, edge, edge_mask, count, slope_to_modes, gain)
    info = lax.all_gather(payload, ("tile", "tm"))
    return pl.pallas_call(
        functools.partial(kernel_smooth, tiles, blocks, frames, float(total_subaps)),
        out_shape=(
            jax.ShapeDtypeStruct((frames, share), f32),
            jax.ShapeDtypeStruct((frames, share), f32),
        ),
        in_specs=[VMEM] * 3,
        out_specs=(VMEM, VMEM),
        scratch_shapes=[
            pltpu.VMEM((blocks * frames, share), f32),
            pltpu.VMEM((blocks * frames, share), f32),
        ],
        compiler_params=params,
        name="smooth",
    )(info, process_noise.reshape(1, modes), gain)


def solution(mesh):
    return jax.shard_map(
        body,
        mesh=mesh,
        in_specs=(
            P("grp", "tm", "tile", None),
            P("grp", None, None, None),
            P("grp", "tm", "tile", None),
            P(("grp", "tm")),
            P(None, None, "tile", None, None),
            P(),
            P(),
        ),
        out_specs=(P(("grp", "tm"), "tile"), P(("grp", "tm"), "tile")),
        check_vma=False,
    )
```

time: 43 us -> 61.7 us (1.43)
  blocking collectives: 16.1 us -> 41.1 us
  starting transfers between devices: 6.21 us -> 0 us
  Pallas kernels: 18.3 us -> 19.1 us
    all_gather x0 -> x2, blocking collectives: none -> 41.1 us  [the longest x1 23.6 us: body(): info = lax.all_gather(payload, ('tile', 'tm'))]
    all_to_all x1 -> x0, blocking collectives: 16.1 us -> none  [body(): info = lax.all_to_all(payload, ('tile', 'tm'), 0, 0)]
    ppermute x2 -> x0, starting transfers between devices: 6.21 us -> none  [the longest x1 4.92 us: body(): from_before = lax.ppermute(up, 'tile', onward)]
    pallas_call x3 -> x2, Pallas kernels: 16.2 us -> 17 us  [the longest x1 14.8 us: body(): pl.pallas_call(functools.partial(kernel_moments, sub_rows, sub_cols, fram...]
  transfers between devices with their start and end apart: 2 -> 0, of which waited for: 0 -> 0; matrix products, arithmetic and copies ran while one was open for 0% -> 0% of each run, Pallas kernels for 19% -> 0%
where the time goes in v1:
time: 61.7 us; the launch traced here: 61.5 us
  blocking collectives  41.1 us (67%)
  Pallas kernels  19.1 us (31%)
  between operations  1.29 us (2%)
    all_gather x1, blocking collectives, body(): info = lax.all_gather(payload, ('tile', 'tm'))  23.6 us
    all_gather x1, blocking collectives, body(): halos = lax.all_gather(halo, 'tile')  17.6 us
    pallas_call x1, Pallas kernels, body(): pl.pallas_call(functools.partial(kernel_moments, sub_rows, sub_cols, fram...  14.8 us
    pallas_call x1, Pallas kernels, body(): pl.pallas_call(functools.partial(kernel_smooth, tiles, blocks, frames, fl...  2.28 us
    pallas_call x1, Pallas kernels, body(): pl.pallas_call(functools.partial(kernel_join, sub_rows, sub_cols, frames,...  2.05 us

profile of v1, /device:TPU:0, one launch (start us, length us, event | category | flops | bytes accessed | tf_op | source)
XLA Modules:
  0.0 61.5 jit_solution(13856360861951927395)
XLA Ops:
  1.3 14.8 %moments.1 = (f32[24,256]{1,0:T(8,128)}, f32[2,3,24,128]{3,2,1,0:T(8,128)}, f32[2,24,128]{2,1,0:T(8,128)}, f32[24,128]{1,0:T(8,128)}, f32[2,3,24,128]{3,2,1,0:T(8,128)}) custom-call(bf16[3,2400,800]{2,1,0:T(8,128)(2,1)} %bitcast.9, s32[3,20,2,40]{3,2,1,0:T(2,128)} %bitcast.13, s32[3,5,24,40]{3,2,1,0:T(8,128)} %bitcast.12, bf16[2,3,5,40,256]{4,3,2,1,0:T(8,128)(2,1)} %modes_ref.1), custom_call_target="tpu_custom_call" | custom-call | flops 2949120000 | bytes 11520000 | tf_op jit(solution)/shard_map/moments/pallas_call | solution.py:359
  16.0 17.6 %all-gather = f32[8,3,24,128]{3,2,1,0:T(8,128)} all-gather(f32[2,3,24,128]{3,2,1,0:T(8,128)} %get-tuple-element.7), channel_id=2, replica_groups=mesh['grp'=2,'tile'=4,'tm'=4] {'tile'}, dimensions={0}, use_global_device_ids=true | all-gather | bytes 368640 | tf_op jit(solution)/shard_map/all_gather | solution.py:386
  33.6 2.1 %join_halo.1 = f32[32,256]{1,0:T(8,128)} custom-call(s32[1]{0:T(128)S(6)} %copy.9.live_ref, f32[4,2,3,24,128]{4,3,2,1,0:T(8,128)} %bitcast.11, f32[24,256]{1,0:T(8,128)} %get-tuple-element.8.pm_ref, f32[2,3,24,128]{3,2,1,0:T(8,128)} %get-tuple-element.9.edge_ref, f32[2,24,128]{2,1,0:T(8,128)} %get-tuple-element.10.em_ref, ...), custom_call_target="tpu_custom_call" | custom-call | tf_op jit(solution)/shard_map/join_halo/pallas_call | solution.py:388
  35.7 23.6 %all-gather.1 = f32[512,256]{1,0:T(8,128)} all-gather(f32[32,256]{1,0:T(8,128)} %join_halo.1), channel_id=3, replica_groups=mesh['grp'=2,'tile'=4,'tm'=4] {'tile','tm'}, dimensions={0}, use_global_device_ids=true | all-gather | bytes 557056 | tf_op jit(solution)/shard_map/all_gather | solution.py:396
  59.2 2.3 %smooth.1 = (f32[24,64]{1,0:T(8,128)}, f32[24,64]{1,0:T(8,128)}) custom-call(f32[16,32,256]{2,1,0:T(8,128)} %bitcast.10, f32[1,256]{1,0:T(1,128)} %bitcast.16, f32[1,256]{1,0:T(1,128)} %bitcast.15), custom_call_target="tpu_custom_call" | custom-call | tf_op jit(solution)/shard_map/smooth/pallas_call | solution.py:397

commit v2 on v1

v2 whole, which is shorter than its diff:
```python
import functools

import jax
import jax.numpy as jnp
from jax import lax
from jax.experimental import pallas as pl
from jax.experimental.pallas import tpu as pltpu
from jax.sharding import PartitionSpec as P

SIDE = 20
SHIFT = 6
CENTRE = (SIDE - 1) / 2.0
LANES = 128
HALF = LANES // 2
VMEM_LIMIT = 24 * 1024 * 1024
VMEM = pl.BlockSpec(memory_space=pltpu.VMEM)
HBM = pl.BlockSpec(memory_space=pl.ANY)


def slot_of(strip, sensor):
    return (strip + 1 + sensor) % 3


def half_columns(half, sub_cols, width):
    cols = sub_cols // 2
    first = max(0, half * cols * SIDE - SHIFT) // LANES * LANES
    end = min(width, -(-((half + 1) * cols * SIDE + SHIFT) // 16) * 16)
    return first, end - first


def lane_iota(rows=1):
    return lax.broadcasted_iota(jnp.int32, (rows, LANES), 1)


def half_lane(rows=1):
    lane = lane_iota(rows)
    return jnp.where(lane >= HALF, lane - HALF, lane)


def by_slot(values, cols):
    lane = half_lane()
    out = jnp.zeros_like(values[0])
    for q, v in enumerate(values):
        if v is not None:
            out = jnp.where((lane >= q * cols) & (lane < (q + 1) * cols), v, out)
    return out


def side_by_side(pieces):
    rows, cols = pieces[0].shape
    pad = jnp.zeros((rows, HALF - 3 * cols), pieces[0].dtype)
    return jnp.concatenate([*pieces, pad, *pieces, pad], axis=1)


def rotate(x, slots, cols):
    shift = slots * cols
    if shift == 0:
        return x
    near = pltpu.roll(x, shift, axis=1)
    far = pltpu.roll(x, LANES - 3 * cols + shift, axis=1)
    return jnp.where(half_lane() >= shift, near, far)


def geometry(geo_ref, off_ref, sensors, sub_rows, sub_cols, width):
    cols = sub_cols // 2
    lane = half_lane()
    index = lane - cols * (lane >= cols).astype(jnp.int32)
    index = index - cols * (lane >= 2 * cols).astype(jnp.int32)
    used = lane < 3 * cols
    tile = lax.axis_index("tile")
    total_rows = off_ref.shape[1]
    for s in range(sensors):
        spread_rows = []
        for k in range(-1, sub_rows + 1):
            row = jnp.clip(tile * sub_rows + k, 0, total_rows - 1)
            v = off_ref[s, row].astype(jnp.float32)
            spread_rows.append([side_by_side([v[:, h * cols : (h + 1) * cols]] * 3) for h in range(2)])
        for i in range(sub_rows):
            for h in range(2):
                first, _ = half_columns(h, sub_cols, width)
                col_base = (SIDE * (index + h * cols) - first).astype(jnp.float32) + CENTRE
                cs = [None] * 3
                rs = [None] * 3
                for k in (i - 1, i, i + 1):
                    q = slot_of(k, s)
                    v = spread_rows[k + 1][h]
                    cs[q] = v[1:2] + col_base
                    rs[q] = v[0:1] + (SIDE * (k - i) + CENTRE)
                geo_ref[s, i, 2 * h : 2 * h + 1, :] = jnp.where(used, by_slot(cs, cols), -1000.0)
                geo_ref[s, i, 2 * h + 1 : 2 * h + 2, :] = jnp.where(used, by_slot(rs, cols), -1000.0)


def build_weights(col_pos, w_ref):
    base = lax.broadcasted_iota(jnp.int32, (16, LANES), 0).astype(jnp.float32) - col_pos
    left = lane_iota(16) < HALF
    for t in range(w_ref.shape[0] // 16):
        d = base + float(16 * t)
        value = jnp.where(left, 1.0, d)
        w_ref[16 * t : 16 * t + 16, :] = jnp.where(jnp.abs(d) < 10.0, value, 0.0).astype(jnp.bfloat16)


def row_sums(row_pos, r, frames):
    plain = jnp.zeros((frames, LANES), jnp.float32)
    lines = jnp.zeros((frames, LANES), jnp.float32)
    for y in range(r.shape[0] // frames):
        d = float(y) - row_pos
        inside = jnp.abs(d) < 10.0
        one = jnp.where(inside, 1.0, 0.0)
        centred = jnp.where(inside, d, 0.0)
        piece = r[y * frames : (y + 1) * frames, :]
        plain = plain + one * piece
        lines = lines + centred * piece
    return plain, lines


def block_moments(x_ref, geo_ref, w_ref, p_ref, sub_cols, frames):
    count = len(x_ref)
    for n in range(count):
        for h in range(2):
            build_weights(geo_ref[n][2 * h : 2 * h + 1, :], w_ref.at[n, h])
    for n in range(count):
        for h in range(2):
            first, size = half_columns(h, sub_cols, x_ref[n].shape[1])
            r = jnp.dot(
                x_ref[n][:, first : first + size],
                w_ref[n, h, 0:size, :],
                preferred_element_type=jnp.float32,
            )
            plain, lines = row_sums(geo_ref[n][2 * h + 1 : 2 * h + 2, :], r, frames)
            p_ref[n][h, 0] = plain
            p_ref[n][h, 1] = lines


def kernel_edge(
    sub_rows, sub_cols, frames, x_hbm, off_hbm, mask_hbm, modes_hbm,
    up_ref, down_ref, p_ref, geo_ref, buf, mask_ref, modes_ref,
    w_ref, off_ref, sem, side_sem,
):
    sensors = x_hbm.shape[0]
    block = SIDE * frames
    last = sub_rows - 1
    cols = sub_cols // 2

    def copy(s, i):
        return pltpu.make_async_copy(
            x_hbm.at[s, pl.ds(i * block, block)], buf.at[s, i], sem.at[s, i]
        )

    off_copy = pltpu.make_async_copy(off_hbm, off_ref, side_sem.at[0])
    mask_copy = pltpu.make_async_copy(mask_hbm, mask_ref, side_sem.at[1])
    modes_copy = pltpu.make_async_copy(modes_hbm, modes_ref, side_sem.at[2])
    off_copy.start()
    for s in range(sensors):
        for i in (0, last):
            copy(s, i).start()
    for s in range(sensors):
        for i in range(1, last):
            copy(s, i).start()
    mask_copy.start()
    modes_copy.start()
    off_copy.wait()
    geometry(geo_ref, off_ref, sensors, sub_rows, sub_cols, x_hbm.shape[2])

    def step(s, carry):
        copy(s, 0).wait()
        copy(s, last).wait()
        block_moments(
            [buf.at[s, 0], buf.at[s, last]],
            [geo_ref.at[s, 0], geo_ref.at[s, last]],
            w_ref,
            [p_ref.at[s, 0], p_ref.at[s, 1]],
            sub_cols,
            frames,
        )
        return carry

    lax.fori_loop(0, sensors, step, 0)
    left = lane_iota() < HALF
    for ref, e, strip in ((down_ref, 0, -1), (up_ref, 1, sub_rows)):
        pair = []
        for h in range(2):
            both = []
            for a in range(2):
                order = [None] * 3
                for s in range(sensors):
                    order[slot_of(strip, s)] = p_ref[s, e, h, a]
                both.append(by_slot(order, cols))
            ref[h] = both[0]
            pair.append(both[1])
        ref[2] = jnp.where(left, pair[0], pltpu.roll(pair[1], HALF, axis=1))
    for s in range(sensors):
        for i in range(1, last):
            copy(s, i).wait()
    mask_copy.wait()
    modes_copy.wait()


def slope_terms(plain, lines, mask):
    left = lane_iota() < HALF
    live = mask > 0.0
    flux = jnp.where(left, plain, pltpu.roll(plain, HALF, axis=1))
    moment = jnp.where(left, lines, plain)
    return jnp.where(live, moment / jnp.where(live, flux, 1.0) * mask, 0.0).astype(jnp.bfloat16)


def stacked(modes_ref, picks, half, cols):
    parts = []
    for x in (1, 0):
        used = 0
        for pick in picks:
            if pick is None:
                parts.append(jnp.zeros((cols, modes_ref.shape[-1]), jnp.float32))
            else:
                s, k = pick
                rows = modes_ref[x, s, k].astype(jnp.float32)
                parts.append(rows[half * cols : (half + 1) * cols])
            used += cols
        parts.append(jnp.zeros((HALF - used, modes_ref.shape[-1]), jnp.float32))
    return jnp.concatenate(parts, axis=0).astype(jnp.bfloat16)


def kernel_inner(
    sub_rows, sub_cols, frames, x_ref, geo_ref, pe_ref, mask_ref, modes_ref,
    pm_ref, edge_ref, em_ref, count_ref, w_ref, p_ref,
):
    sensors = x_ref.shape[0]
    last = sub_rows - 1
    cols = sub_cols // 2

    def step(s, carry):
        block_moments(
            [x_ref.at[s, i] for i in range(1, last)],
            [geo_ref.at[s, i] for i in range(1, last)],
            w_ref,
            [p_ref.at[s, i - 1] for i in range(1, last)],
            sub_cols,
            frames,
        )
        return carry

    lax.fori_loop(0, sensors, step, 0)

    def partial(s, i, h, a):
        if i == 0:
            return pe_ref[s, 0, h, a]
        if i == last:
            return pe_ref[s, 1, h, a]
        return p_ref[s, i - 1, h, a]

    def strip_total(s, k, h, a):
        total = None
        for i in (k - 1, k, k + 1):
            if 0 <= i <= last:
                v = partial(s, i, h, a)
                total = v if total is None else total + v
        return total

    def mask_of(s, k, h):
        return mask_ref[s, k].astype(jnp.float32)[:, h * cols : (h + 1) * cols]

    count = jnp.zeros((frames, LANES), jnp.float32)
    for e, k in enumerate((0, last)):
        order = [None] * 3
        for s in range(sensors):
            order[slot_of(k, s)] = s
        for h in range(2):
            m = side_by_side([mask_of(s, k, h) for s in order])
            em_ref[e, h] = m
            count = count + m
            for a in range(2):
                edge_ref[e, h, a] = by_slot([strip_total(s, k, h, a) for s in order], cols)
    modes = jnp.zeros((frames, modes_ref.shape[-1]), jnp.float32)
    for s in range(sensors):
        for g in range(1, last, 3):
            order = [None] * 3
            for k in range(g, min(g + 3, last)):
                order[slot_of(k, s)] = k
            for h in range(2):
                none = jnp.zeros((frames, cols), jnp.float32)
                mask = side_by_side([none if k is None else mask_of(s, k, h) for k in order])
                count = count + mask
                plain, lines = (
                    by_slot([None if k is None else strip_total(s, k, h, a) for k in order], cols)
                    for a in range(2)
                )
                modes = modes + jnp.dot(
                    slope_terms(plain, lines, mask),
                    stacked(modes_ref, [None if k is None else (s, k) for k in order], h, cols),
                    preferred_element_type=jnp.float32,
                )
    pm_ref[...] = modes
    count_ref[...] = jnp.broadcast_to(0.5 * jnp.sum(count, axis=1, keepdims=True), count_ref.shape)


def kernel_join(
    sub_rows, sub_cols, frames, tiles, blocks,
    live_ref, before_ref, after_ref, pm_ref, edge_ref, em_ref, count_ref, modes_ref, gain_ref, out_ref,
):
    sensors = modes_ref.shape[1]
    last = sub_rows - 1
    cols = sub_cols // 2
    modes = pm_ref[...]
    for e, k in enumerate((0, last)):
        halo_ref = (before_ref, after_ref)[e]
        halo_strip = (sub_rows, -1)[e]
        turn = (slot_of(k, 0) - slot_of(halo_strip, 0)) % 3
        order = [None] * 3
        for s in range(sensors):
            order[slot_of(k, s)] = s
        both = halo_ref[2]
        for h in range(2):
            lines = both if h == 0 else pltpu.roll(both, HALF, axis=1)
            plain = edge_ref[e, h, 0] + rotate(halo_ref[h], turn, cols)
            lines = edge_ref[e, h, 1] + rotate(lines, turn, cols)
            modes = modes + jnp.dot(
                slope_terms(plain, lines, em_ref[e, h]),
                stacked(modes_ref, [None if s is None else (s, k) for s in order], h, cols),
                preferred_element_type=jnp.float32,
            )
    frame = lax.broadcasted_iota(jnp.int32, (frames, 1), 0)
    live = (frame < live_ref[0]).astype(jnp.float32)
    info = gain_ref[...] * modes * live
    own = lane_iota(frames) == lax.broadcasted_iota(jnp.int32, (frames, LANES), 0)
    counts = jnp.sum(jnp.where(own, count_ref[...] * live, 0.0), axis=0, keepdims=True)
    share = modes.shape[1] // tiles
    pack = LANES // share
    rows = frames // pack
    pad = jnp.zeros((out_ref.shape[1] - rows - 1, LANES), jnp.float32)
    for t in range(tiles):
        piece = jnp.concatenate(
            [info[g * rows : (g + 1) * rows, t * share : (t + 1) * share] for g in range(pack)], axis=1
        )
        piece = jnp.concatenate([piece, counts, pad], axis=0)
        for b in range(blocks):
            out_ref[t * blocks + b] = piece


def shifted(x, by, fill, back):
    rows = x.shape[0]
    if by % 8 == 0:
        pad = jnp.full((by, x.shape[1]), fill, x.dtype)
        if back:
            return jnp.concatenate([x[by:], pad], axis=0)
        return jnp.concatenate([pad, x[: rows - by]], axis=0)
    row = lax.broadcasted_iota(jnp.int32, (rows, 1), 0)
    if back:
        return jnp.where(row < rows - by, pltpu.roll(x, rows - by, axis=0), fill)
    return jnp.where(row >= by, pltpu.roll(x, by, axis=0), fill)


def kernel_smooth(
    tiles, blocks, frames, total_subaps, in_ref, noise_ref, gain_ref, mean_ref, var_ref, mean_scr, var_scr
):
    share = mean_ref.shape[1]
    total = blocks * frames
    tile = lax.axis_index("tile")
    time = lax.axis_index("tm")
    pack = LANES // share
    rows = frames // pack

    def own_modes(v):
        out = v[:, 0:share]
        for t in range(1, tiles):
            out = jnp.where(tile == t, v[:, t * share : (t + 1) * share], out)
        return out

    q = own_modes(noise_ref[...])
    gain = own_modes(gain_ref[...])
    own = lane_iota(frames) == lax.broadcasted_iota(jnp.int32, (frames, LANES), 0)
    infos = []
    counts = []
    for b in range(blocks):
        v = in_ref[b]
        for t in range(1, tiles):
            v = v + in_ref[t * blocks + b]
        for g in range(pack):
            infos.append(v[0:rows, g * share : (g + 1) * share])
        counts.append(jnp.sum(jnp.where(own, v[rows : rows + 1], 0.0), axis=1, keepdims=True))
    info_mean = jnp.concatenate(infos, axis=0)
    prec = gain * jnp.concatenate(counts, axis=0) / total_subaps
    row = lax.broadcasted_iota(jnp.int32, (total, 1), 0)
    first = row == 0
    retain = 1.0 / (1.0 + q * prec)
    a = jnp.where(first, 0.0, retain)
    c = jnp.where(first, 1.0 / (1.0 + prec), q * retain)
    b = c * info_mean
    e = a * info_mean
    j = a * prec
    by = 1
    while by < total:
        a1 = shifted(a, by, 1.0, False)
        b1 = shifted(b, by, 0.0, False)
        c1 = shifted(c, by, 0.0, False)
        e1 = shifted(e, by, 0.0, False)
        j1 = shifted(j, by, 0.0, False)
        damp = 1.0 / (1.0 + c1 * j)
        left = a * damp
        right = a1 * damp
        b = left * (b1 + c1 * e) + b
        c = left * a * c1 + c
        e, j = right * (e - j * b1) + e1, right * a1 * j + j1
        a = left * a1
        by *= 2
    g = jnp.where(row == total - 1, 0.0, c / (c + q))
    m = (1.0 - g) * b
    v = c * (1.0 - g)
    by = 1
    while by < total:
        g1 = shifted(g, by, 1.0, True)
        m1 = shifted(m, by, 0.0, True)
        v1 = shifted(v, by, 0.0, True)
        m = g * m1 + m
        v = g * g * v1 + v
        g = g * g1
        by *= 2
    mean_scr[...] = m
    var_scr[...] = v
    start = pl.multiple_of(time * frames, 8)
    mean_ref[...] = mean_scr[pl.ds(start, frames), :]
    var_ref[...] = var_scr[pl.ds(start, frames), :]


def body(pixels, offsets, mask, frame_count, slope_to_modes, process_noise, mode_gain):
    sensors, frames, lines, width = pixels.shape
    sub_rows, sub_cols = mask.shape[2], mask.shape[3]
    modes = process_noise.shape[0]
    tiles = lax.axis_size("tile")
    blocks = lax.axis_size("tm")
    share = modes // tiles
    total_subaps = sensors * sub_rows * tiles * sub_cols
    f32 = jnp.float32
    bf16 = jnp.bfloat16
    x = jnp.transpose(pixels, (0, 2, 1, 3)).reshape(sensors, lines * frames, width)
    off = jnp.transpose(offsets, (0, 1, 3, 2))
    msk = jnp.transpose(mask, (0, 2, 1, 3))
    x, off, msk, slope_to_modes = (
        pltpu.with_memory_space_constraint(v, pltpu.HBM) for v in (x, off, msk, slope_to_modes)
    )
    block = SIDE * frames
    inner = sub_rows - 2
    depth = max(half_columns(h, sub_cols, width)[1] for h in range(2))
    params = pltpu.CompilerParams(vmem_limit_bytes=VMEM_LIMIT)

    def cost(chunks):
        return pl.CostEstimate(
            flops=2 * chunks * block * width * 256, bytes_accessed=chunks * block * width * 2, transcendentals=0
        )

    up, down, parts, geo, buf, mask_v, modes_v = pl.pallas_call(
        functools.partial(kernel_edge, sub_rows, sub_cols, frames),
        out_shape=(
            jax.ShapeDtypeStruct((3, frames, LANES), f32),
            jax.ShapeDtypeStruct((3, frames, LANES), f32),
            pltpu.VMEM((sensors, 2, 2, 2, frames, LANES), f32),
            pltpu.VMEM((sensors, sub_rows, 8, LANES), f32),
            pltpu.VMEM((sensors, sub_rows, block, width), bf16),
            pltpu.VMEM(msk.shape, msk.dtype),
            pltpu.VMEM(slope_to_modes.shape, bf16),
        ),
        in_specs=[HBM] * 4,
        out_specs=(VMEM,) * 7,
        scratch_shapes=[
            pltpu.VMEM((2, 2, depth, LANES), bf16),
            pltpu.VMEM(off.shape, off.dtype),
            pltpu.SemaphoreType.DMA((sensors, sub_rows)),
            pltpu.SemaphoreType.DMA((3,)),
        ],
        compiler_params=params,
        cost_estimate=cost(2 * sensors),
        name="edge_moments",
    )(x, off, msk, slope_to_modes)
    onward = [(i, i + 1) for i in range(tiles - 1)]
    backward = [(j, i) for i, j in onward]
    from_before = lax.ppermute(up, "tile", onward)
    from_after = lax.ppermute(down, "tile", backward)
    partial_modes, edge, edge_mask, count = pl.pallas_call(
        functools.partial(kernel_inner, sub_rows, sub_cols, frames),
        out_shape=(
            pltpu.VMEM((frames, modes), f32),
            pltpu.VMEM((2, 2, 2, frames, LANES), f32),
            pltpu.VMEM((2, 2, frames, LANES), f32),
            pltpu.VMEM((frames, LANES), f32),
        ),
        in_specs=[VMEM] * 5,
        out_specs=(VMEM,) * 4,
        scratch_shapes=[
            pltpu.VMEM((inner, 2, depth, LANES), bf16),
            pltpu.VMEM((sensors, inner, 2, 2, frames, LANES), f32),
        ],
        compiler_params=params,
        cost_estimate=cost(inner * sensors),
        name="inner_moments",
    )(buf, geo, parts, mask_v, modes_v)
    gain = mode_gain.reshape(1, modes)
    packed = -(-(frames * share // LANES + 1) // 8) * 8
    payload = pl.pallas_call(
        functools.partial(kernel_join, sub_rows, sub_cols, frames, tiles, blocks),
        out_shape=jax.ShapeDtypeStruct((tiles * blocks, packed, LANES), f32),
        in_specs=[pl.BlockSpec(memory_space=pltpu.SMEM)] + [VMEM] * 8,
        out_specs=VMEM,
        compiler_params=params,
        name="join_halo",
    )(frame_count, from_before, from_after, partial_modes, edge, edge_mask, count, modes_v, gain)
    info = lax.all_to_all(payload, ("tile", "tm"), 0, 0)
    return pl.pallas_call(
        functools.partial(kernel_smooth, tiles, blocks, frames, float(total_subaps)),
        out_shape=(
            jax.ShapeDtypeStruct((frames, share), f32),
            jax.ShapeDtypeStruct((frames, share), f32),
        ),
        in_specs=[VMEM] * 3,
        out_specs=(VMEM, VMEM),
        scratch_shapes=[
            pltpu.VMEM((blocks * frames, share), f32),
            pltpu.VMEM((blocks * frames, share), f32),
        ],
        compiler_params=params,
        name="smooth",
    )(info, process_noise.reshape(1, modes), gain)


def solution(mesh):
    return jax.shard_map(
        body,
        mesh=mesh,
        in_specs=(
            P("grp", "tm", "tile", None),
            P("grp", None, None, None),
            P("grp", "tm", "tile", None),
            P(("grp", "tm")),
            P(None, None, "tile", None, None),
            P(),
            P(),
        ),
        out_specs=(P(("grp", "tm"), "tile"), P(("grp", "tm"), "tile")),
        check_vma=False,
    )
```

time: 61.7 us -> 34.2 us (0.55)
  blocking collectives: 41.1 us -> 14.3 us
  Pallas kernels: 19.1 us -> 11.6 us
  starting transfers between devices: 0 us -> 6.22 us
    all_gather x2 -> x0, blocking collectives: 41.1 us -> none  [the longest x1 23.6 us: body(): info = lax.all_gather(payload, ('tile', 'tm'))]
    all_to_all x0 -> x1, blocking collectives: none -> 14.3 us  [body(): info = lax.all_to_all(payload, ('tile', 'tm'), 0, 0)]
    ppermute x0 -> x2, starting transfers between devices: none -> 6.22 us  [the longest x1 4.93 us: body(): from_before = lax.ppermute(up, 'tile', onward)]
    pallas_call x1 -> x2, Pallas kernels: 14.8 us -> 10.1 us  [the longest x1 6.61 us: body(): pl.pallas_call(functools.partial(kernel_edge, sub_rows, sub_cols, frames)...]
    pallas_call x1, Pallas kernels: 2.05 us -> 0.38 us  [body(): pl.pallas_call(functools.partial(kernel_join, sub_rows, sub_cols, frames,...]
    pallas_call x1, Pallas kernels: 2.28 us -> 1.19 us  [body(): pl.pallas_call(functools.partial(kernel_smooth, tiles, blocks, frames, fl...]
  transfers between devices with their start and end apart: 0 -> 2, of which waited for: 0 -> 1; matrix products, arithmetic and copies ran while one was open for 0% -> 0% of each run, Pallas kernels for 0% -> 10%
where the time goes in v2:
time: 34.2 us; the launch traced here: 34 us
  blocking collectives  14.3 us (42%)
  Pallas kernels  11.6 us (34%)
  starting transfers between devices  6.22 us (18%)
  between operations  1.35 us (4%)
  waiting for transfers between devices  0.44 us (1%)
    all_to_all x1, blocking collectives, body(): info = lax.all_to_all(payload, ('tile', 'tm'), 0, 0)  14.3 us
    pallas_call x1, Pallas kernels, body(): pl.pallas_call(functools.partial(kernel_edge, sub_rows, sub_cols, frames)...  6.61 us
    ppermute x1, starting transfers between devices, body(): from_before = lax.ppermute(up, 'tile', onward)  4.93 us
    pallas_call x1, Pallas kernels, body(): pl.pallas_call(functools.partial(kernel_inner, sub_rows, sub_cols, frames...  3.44 us
    ppermute x1, starting transfers between devices, body(): from_after = lax.ppermute(down, 'tile', backward)  1.29 us
    pallas_call x1, Pallas kernels, body(): pl.pallas_call(functools.partial(kernel_smooth, tiles, blocks, frames, fl...  1.19 us
  transfers between devices with their start and end apart: 2, of which 1 were waited for; matrix products, arithmetic and copies ran while one was open for 0% of the time, Pallas kernels for 10%

profile of v2, /device:TPU:0, one launch (start us, length us, event | category | flops | bytes accessed | tf_op | source)
XLA Modules:
  0.0 34.0 jit_solution(9206013695689092022)
XLA Ops:
  0.6 0.0 copy-start
  0.6 0.0 copy-start.1
  0.7 6.6 %edge_moments.1 = (f32[3,24,128]{2,1,0:T(8,128)S(1)}, f32[3,24,128]{2,1,0:T(8,128)S(1)}, f32[3,2,2,2,24,128]{5,4,3,2,1,0:T(8,128)S(1)}, f32[3,5,8,128]{3,2,1,0:T...) custom-call(bf16[3,2400,800]{2,1,0:T(8,128)(2,1)} %bitcast.10, ...), custom_call_target="tpu_custom_call" | custom-call | flops 1179648000 | bytes 4608000 | tf_op jit(solution)/shard_map/edge_moments/pallas_call | solution.py:449
  7.3 4.9 %collective-permute-start = (f32[3,24,128]{2,1,0:T(8,128)S(1)}, f32[3,24,128]{2,1,0:T(8,128)S(1)}, u32[]{:S(2)}, u32[]{:S(2)}) collective-permute-start(f32[3,24,128]{2,1,0:T(8,128)S(1)} %get-tuple-element.13), channel_id=1, source_target_pairs={{0,4},{4,8},{8,12},{1,5},{5,9},{9,13},{2,6},{6,10},{10,14},{3,7},{... | collective-permute-start | bytes 110600 | tf_op jit(solution)/shard_map/ppermute | solution.py:474
  12.2 1.3 %collective-permute-start.1 = (f32[3,24,128]{2,1,0:T(8,128)S(1)}, f32[3,24,128]{2,1,0:T(8,128)S(1)}, u32[]{:S(2)}, u32[]{:S(2)}) collective-permute-start(f32[3,24,128]{2,1,0:T(8,128)S(1)} %get-tuple-element.14), channel_id=1, source_target_pairs={{4,0},{8,4},{12,8},{5,1},{9,5},{13,9},{6,2},{10,6},{14,10},{7,3},{... | collective-permute-start | bytes 110600 | tf_op jit(solution)/shard_map/ppermute | solution.py:475
  13.5 3.4 %inner_moments.1 = (f32[24,256]{1,0:T(8,128)S(1)}, f32[2,2,2,24,128]{4,3,2,1,0:T(8,128)S(1)}, f32[2,2,24,128]{3,2,1,0:T(8,128)S(1)}, f32[24,128]{1,0:T(8,128)S(1)}) custom-call(bf16[3,5,480,800]{3,2,1,0:T(8,128)(2,1)S(1)} %get-tuple-element.15.x_ref, f32[3,5,8,128]{3,2,1,0:T(8,128)S(1)} %get-tuple-element.16.geo_ref, ...), custom_call_target="tpu_custom_call" | custom-call | flops 1769472000 | bytes 6912000 | tf_op jit(solution)/shard_map/inner_moments/pallas_call | solution.py:476
  17.6 0.0 collective-permute-done.before_ref
  17.6 0.4 %collective-permute-done.1.after_ref = f32[3,24,128]{2,1,0:T(8,128)S(1)} collective-permute-done((f32[3,24,128]{2,1,0:T(8,128)S(1)}, f32[3,24,128]{2,1,0:T(8,128)S(1)}, u32[]{:S(2)}, u32[]{:S(2)}) %collective-permute-start.1) | collective-permute-done | bytes 36896 | tf_op jit(solution)/shard_map/ppermute | solution.py:475
  18.1 0.0 copy-done
  18.1 0.4 %join_halo.1 = f32[16,16,128]{2,1,0:T(8,128)S(1)} custom-call(s32[1]{0:T(128)S(6)} %copy.9.live_ref, f32[3,24,128]{2,1,0:T(8,128)S(1)} %collective-permute-done.before_ref, f32[3,24,128]{2,1,0:T(8,128)S(1)} %collective-permute-done.1.after_ref, f32[24,256]{1,0:T(8,128)S(1)} %get-tuple-element.20.pm_ref, ...), custom_call_target="tpu_custom_call" | custom-call | tf_op jit(solution)/shard_map/join_halo/pallas_call | solution.py:496
  18.4 14.3 %all_to_all.5.in_ref = f32[16,16,128]{2,1,0:T(8,128)S(1)} all-to-all(f32[16,16,128]{2,1,0:T(8,128)S(1)} %join_halo.1), channel_id=1, replica_groups=mesh['grp'=2,'tile'=4,'tm'=4] {'tile','tm'}, dimensions={0} | all-to-all | bytes 262144 | tf_op jit(solution)/shard_map/all_to_all | solution.py:504
  32.8 0.0 copy-done.1
  32.8 1.2 %smooth.1 = (f32[24,64]{1,0:T(8,128)}, f32[24,64]{1,0:T(8,128)}) custom-call(f32[16,16,128]{2,1,0:T(8,128)S(1)} %all_to_all.5.in_ref, f32[1,256]{1,0:T(1,128)S(1)} %bitcast.9, f32[1,256]{1,0:T(1,128)S(1)} %bitcast.8), custom_call_target="tpu_custom_call" | custom-call | tf_op jit(solution)/shard_map/smooth/pallas_call | solution.py:505
Async XLA Ops:
  0.6 17.4 %copy-start = (f32[256]{0:T(256)S(1)}, f32[256]{0:T(256)}, u32[]{:S(2)}) copy-start(f32[256]{0:T(256)} %param.13) | copy-start | bytes 3076
  0.6 32.1 %copy-start.1 = (f32[256]{0:T(256)S(1)}, f32[256]{0:T(256)}, u32[]{:S(2)}) copy-start(f32[256]{0:T(256)} %param.12) | copy-start | bytes 3076
  7.3 10.3 %collective-permute-start = (f32[3,24,128]{2,1,0:T(8,128)S(1)}, f32[3,24,128]{2,1,0:T(8,128)S(1)}, u32[]{:S(2)}, u32[]{:S(2)}) collective-permute-start(f32[3,24,128]{2,1,0:T(8,128)S(1)} %get-tuple-element.13), channel_id=1, source_target_pairs={{0,4},{4,8},{8,12},{1,5},{5,9},{9,13},{2,6},{6,10},{10,14},{3,7},{... | collective-permute-start | bytes 110600 | tf_op jit(solution)/shard_map/ppermute | solution.py:474
  12.2 5.9 %collective-permute-start.1 = (f32[3,24,128]{2,1,0:T(8,128)S(1)}, f32[3,24,128]{2,1,0:T(8,128)S(1)}, u32[]{:S(2)}, u32[]{:S(2)}) collective-permute-start(f32[3,24,128]{2,1,0:T(8,128)S(1)} %get-tuple-element.14), channel_id=1, source_target_pairs={{4,0},{8,4},{12,8},{5,1},{9,5},{13,9},{6,2},{10,6},{14,10},{7,3},{... | collective-permute-start | bytes 110600 | tf_op jit(solution)/shard_map/ppermute | solution.py:475

commit v3 on v2

--- a/solution.py
+++ b/solution.py
@@ -132,30 +132,31 @@
 
 
 def kernel_edge(
-    sub_rows, sub_cols, frames, x_hbm, off_hbm, mask_hbm, modes_hbm,
-    up_ref, down_ref, p_ref, geo_ref, buf, mask_ref, modes_ref,
-    w_ref, off_ref, sem, side_sem,
+    sub_rows, sub_cols, frames, x_hbm, off_hbm, mask_hbm, frames_ref, modes_hbm,
+    up_ref, down_ref, p_ref, geo_ref, mask_ref, live_ref, modes_ref, ahead_ref,
+    buf, w_ref, off_ref, sem, side_sem,
 ):
     sensors = x_hbm.shape[0]
     block = SIDE * frames
     last = sub_rows - 1
     cols = sub_cols // 2
 
-    def copy(s, i):
+    def copy(s, e):
         return pltpu.make_async_copy(
-            x_hbm.at[s, pl.ds(i * block, block)], buf.at[s, i], sem.at[s, i]
+            x_hbm.at[s, pl.ds(e * last * block, block)], buf.at[s, e], sem.at[s, e]
         )
 
     off_copy = pltpu.make_async_copy(off_hbm, off_ref, side_sem.at[0])
     mask_copy = pltpu.make_async_copy(mask_hbm, mask_ref, side_sem.at[1])
     modes_copy = pltpu.make_async_copy(modes_hbm, modes_ref, side_sem.at[2])
+    ahead_copy = pltpu.make_async_copy(
+        x_hbm.at[0, pl.ds(block, ahead_ref.shape[0])], ahead_ref, side_sem.at[3]
+    )
     off_copy.start()
     for s in range(sensors):
-        for i in (0, last):
-            copy(s, i).start()
-    for s in range(sensors):
-        for i in range(1, last):
-            copy(s, i).start()
+        for e in range(2):
+            copy(s, e).start()
+    ahead_copy.start()
     mask_copy.start()
     modes_copy.start()
     off_copy.wait()
@@ -163,9 +164,9 @@
 
     def step(s, carry):
         copy(s, 0).wait()
-        copy(s, last).wait()
+        copy(s, 1).wait()
         block_moments(
-            [buf.at[s, 0], buf.at[s, last]],
+            [buf.at[s, 0], buf.at[s, 1]],
             [geo_ref.at[s, 0], geo_ref.at[s, last]],
             w_ref,
             [p_ref.at[s, 0], p_ref.at[s, 1]],
@@ -188,9 +189,9 @@
             ref[h] = both[0]
             pair.append(both[1])
         ref[2] = jnp.where(left, pair[0], pltpu.roll(pair[1], HALF, axis=1))
-    for s in range(sensors):
-        for i in range(1, last):
-            copy(s, i).wait()
+    frame = lax.broadcasted_iota(jnp.int32, (frames, LANES), 0)
+    live_ref[...] = (frame < frames_ref[0]).astype(jnp.float32)
+    ahead_copy.wait()
     mask_copy.wait()
     modes_copy.wait()
 
@@ -220,25 +221,36 @@
 
 
 def kernel_inner(
-    sub_rows, sub_cols, frames, x_ref, geo_ref, pe_ref, mask_ref, modes_ref,
-    pm_ref, edge_ref, em_ref, count_ref, w_ref, p_ref,
+    sub_rows, sub_cols, frames, ahead, x_hbm, ahead_ref, geo_ref, pe_ref, mask_ref, modes_ref,
+    pm_ref, edge_ref, em_ref, count_ref, buf, w_ref, p_ref, sem,
 ):
-    sensors = x_ref.shape[0]
+    sensors = x_hbm.shape[0]
+    block = SIDE * frames
     last = sub_rows - 1
     cols = sub_cols // 2
 
-    def step(s, carry):
-        block_moments(
-            [x_ref.at[s, i] for i in range(1, last)],
-            [geo_ref.at[s, i] for i in range(1, last)],
-            w_ref,
-            [p_ref.at[s, i - 1] for i in range(1, last)],
-            sub_cols,
-            frames,
+    def copy(s, i):
+        return pltpu.make_async_copy(
+            x_hbm.at[s, pl.ds(i * block, block)], buf.at[s, i - 1], sem.at[s, i - 1]
         )
-        return carry
-
-    lax.fori_loop(0, sensors, step, 0)
+
+    def done(s, i):
+        return s == 0 and i <= ahead
+
+    for s in range(sensors):
+        for i in range(1, last):
+            if not done(s, i):
+                copy(s, i).start()
+    for s in range(sensors):
+        for i in range(1, last):
+            if done(s, i):
+                pixels = ahead_ref.at[(i - 1) * block : i * block]
+            else:
+                copy(s, i).wait()
+                pixels = buf.at[s, i - 1]
+            block_moments(
+                [pixels], [geo_ref.at[s, i]], w_ref.at[pl.ds(i - 1, 1)], [p_ref.at[s, i - 1]], sub_cols, frames
+            )
 
     def partial(s, i, h, a):
         if i == 0:
@@ -293,7 +305,7 @@
 
 
 def kernel_join(
-    sub_rows, sub_cols, frames, tiles, blocks,
+    sub_rows, sub_cols, frames, tiles,
     live_ref, before_ref, after_ref, pm_ref, edge_ref, em_ref, count_ref, modes_ref, gain_ref, out_ref,
 ):
     sensors = modes_ref.shape[1]
@@ -317,9 +329,8 @@
                 stacked(modes_ref, [None if s is None else (s, k) for s in order], h, cols),
                 preferred_element_type=jnp.float32,
             )
-    frame = lax.broadcasted_iota(jnp.int32, (frames, 1), 0)
-    live = (frame < live_ref[0]).astype(jnp.float32)
-    info = gain_ref[...] * modes * live
+    live = live_ref[...]
+    info = gain_ref[...] * modes * jnp.concatenate([live] * (modes.shape[1] // LANES), axis=1)
     own = lane_iota(frames) == lax.broadcasted_iota(jnp.int32, (frames, LANES), 0)
     counts = jnp.sum(jnp.where(own, count_ref[...] * live, 0.0), axis=0, keepdims=True)
     share = modes.shape[1] // tiles
@@ -331,8 +342,15 @@
             [info[g * rows : (g + 1) * rows, t * share : (t + 1) * share] for g in range(pack)], axis=1
         )
         piece = jnp.concatenate([piece, counts, pad], axis=0)
-        for b in range(blocks):
-            out_ref[t * blocks + b] = piece
+        out_ref[t] = piece
+
+
+def kernel_sum(blocks, in_ref, out_ref):
+    total = in_ref[0]
+    for t in range(1, in_ref.shape[0]):
+        total = total + in_ref[t]
+    for b in range(blocks):
+        out_ref[b] = total
 
 
 def shifted(x, by, fill, back):
@@ -371,8 +389,6 @@
     counts = []
     for b in range(blocks):
         v = in_ref[b]
-        for t in range(1, tiles):
-            v = v + in_ref[t * blocks + b]
         for g in range(pack):
             infos.append(v[0:rows, g * share : (g + 1) * share])
         counts.append(jnp.sum(jnp.where(own, v[rows : rows + 1], 0.0), axis=1, keepdims=True))
@@ -433,11 +449,12 @@
     x = jnp.transpose(pixels, (0, 2, 1, 3)).reshape(sensors, lines * frames, width)
     off = jnp.transpose(offsets, (0, 1, 3, 2))
     msk = jnp.transpose(mask, (0, 2, 1, 3))
+    block = SIDE * frames
     x, off, msk, slope_to_modes = (
         pltpu.with_memory_space_constraint(v, pltpu.HBM) for v in (x, off, msk, slope_to_modes)
     )
-    block = SIDE * frames
     inner = sub_rows - 2
+    ahead = min(2, inner)
     depth = max(half_columns(h, sub_cols, width)[1] for h in range(2))
     params = pltpu.CompilerParams(vmem_limit_bytes=VMEM_LIMIT)
 
@@ -446,62 +463,75 @@
             flops=2 * chunks * block * width * 256, bytes_accessed=chunks * block * width * 2, transcendentals=0
         )
 
-    up, down, parts, geo, buf, mask_v, modes_v = pl.pallas_call(
+    up, down, parts, geo, mask_v, live, modes_v, pixels_ahead = pl.pallas_call(
         functools.partial(kernel_edge, sub_rows, sub_cols, frames),
         out_shape=(
             jax.ShapeDtypeStruct((3, frames, LANES), f32),
             jax.ShapeDtypeStruct((3, frames, LANES), f32),
             pltpu.VMEM((sensors, 2, 2, 2, frames, LANES), f32),
             pltpu.VMEM((sensors, sub_rows, 8, LANES), f32),
-            pltpu.VMEM((sensors, sub_rows, block, width), bf16),
             pltpu.VMEM(msk.shape, msk.dtype),
+            pltpu.VMEM((frames, LANES), f32),
             pltpu.VMEM(slope_to_modes.shape, bf16),
+            pltpu.VMEM((ahead * block, width), bf16),
         ),
-        in_specs=[HBM] * 4,
-        out_specs=(VMEM,) * 7,
+        in_specs=[HBM, HBM, HBM, pl.BlockSpec(memory_space=pltpu.SMEM), HBM],
+        out_specs=(VMEM,) * 8,
         scratch_shapes=[
+            pltpu.VMEM((sensors, 2, block, width), bf16),
             pltpu.VMEM((2, 2, depth, LANES), bf16),
             pltpu.VMEM(off.shape, off.dtype),
-            pltpu.SemaphoreType.DMA((sensors, sub_rows)),
-            pltpu.SemaphoreType.DMA((3,)),
+            pltpu.SemaphoreType.DMA((sensors, 2)),
+            pltpu.SemaphoreType.DMA((4,)),
         ],
         compiler_params=params,
         cost_estimate=cost(2 * sensors),
         name="edge_moments",
-    )(x, off, msk, slope_to_modes)
+    )(x, off, msk, frame_count, slope_to_modes)
     onward = [(i, i + 1) for i in range(tiles - 1)]
     backward = [(j, i) for i, j in onward]
     from_before = lax.ppermute(up, "tile", onward)
     from_after = lax.ppermute(down, "tile", backward)
     partial_modes, edge, edge_mask, count = pl.pallas_call(
-        functools.partial(kernel_inner, sub_rows, sub_cols, frames),
+        functools.partial(kernel_inner, sub_rows, sub_cols, frames, ahead),
         out_shape=(
             pltpu.VMEM((frames, modes), f32),
             pltpu.VMEM((2, 2, 2, frames, LANES), f32),
             pltpu.VMEM((2, 2, frames, LANES), f32),
             pltpu.VMEM((frames, LANES), f32),
         ),
-        in_specs=[VMEM] * 5,
+        in_specs=[HBM] + [VMEM] * 5,
         out_specs=(VMEM,) * 4,
         scratch_shapes=[
+            pltpu.VMEM((sensors, inner, block, width), bf16),
             pltpu.VMEM((inner, 2, depth, LANES), bf16),
             pltpu.VMEM((sensors, inner, 2, 2, frames, LANES), f32),
+            pltpu.SemaphoreType.DMA((sensors, inner)),
         ],
         compiler_params=params,
         cost_estimate=cost(inner * sensors),
         name="inner_moments",
-    )(buf, geo, parts, mask_v, modes_v)
+    )(x, pixels_ahead, geo, parts, mask_v, modes_v)
     gain = mode_gain.reshape(1, modes)
     packed = -(-(frames * share // LANES + 1) // 8) * 8
     payload = pl.pallas_call(
-        functools.partial(kernel_join, sub_rows, sub_cols, frames, tiles, blocks),
-        out_shape=jax.ShapeDtypeStruct((tiles * blocks, packed, LANES), f32),
-        in_specs=[pl.BlockSpec(memory_space=pltpu.SMEM)] + [VMEM] * 8,
+        functools.partial(kernel_join, sub_rows, sub_cols, frames, tiles),
+        out_shape=jax.ShapeDtypeStruct((tiles, packed, LANES), f32),
+        in_specs=[VMEM] * 9,
         out_specs=VMEM,
         compiler_params=params,
         name="join_halo",
-    )(frame_count, from_before, from_after, partial_modes, edge, edge_mask, count, modes_v, gain)
-    info = lax.all_to_all(payload, ("tile", "tm"), 0, 0)
+    )(live, from_before, from_after, partial_modes, edge, edge_mask, count, modes_v, gain)
+    own_share = lax.all_to_all(payload, "tile", 0, 0)
+    summed = pl.pallas_call(
+        functools.partial(kernel_sum, blocks),
+        out_shape=jax.ShapeDtypeStruct((blocks, packed, LANES), f32),
+        in_specs=[VMEM],
+        out_specs=VMEM,
+        compiler_params=params,
+        name="sum_tiles",
+    )(own_share)
+    info = lax.all_to_all(summed, "tm", 0, 0)
     return pl.pallas_call(
         functools.partial(kernel_smooth, tiles, blocks, frames, float(total_subaps)),
         out_shape=(

time: 34.2 us -> 36.2 us (1.058)
  blocking collectives: 14.3 us -> 17.9 us
  Pallas kernels: 11.6 us -> 10.4 us
  waiting for transfers between devices: 0.44 us -> 0.01 us
    all_to_all x1 -> x2, blocking collectives: 14.3 us -> 17.9 us  [the longest x1 11.4 us: body(): own_share = lax.all_to_all(payload, 'tile', 0, 0)]
    pallas_call x1, Pallas kernels: 6.61 us -> 4.03 us  [body(): pl.pallas_call(functools.partial(kernel_edge, sub_rows, sub_cols, frames)...]
    pallas_call x1, Pallas kernels: 3.44 us -> 4.83 us  [body(): pl.pallas_call(functools.partial(kernel_inner, sub_rows, sub_cols, frames...]
    ppermute x1, waiting for transfers between devices: 0.44 us -> 0.01 us  [body(): from_after = lax.ppermute(down, 'tile', backward)]
  transfers between devices with their start and end apart: 2 -> 2, of which waited for: 1 -> 0; matrix products, arithmetic and copies ran while one was open for 0% -> 0% of each run, Pallas kernels for 10% -> 13%
where the time goes in v3:
time: 36.2 us; the launch traced here: 36 us
  blocking collectives  17.9 us (49%)
  Pallas kernels  10.4 us (29%)
  starting transfers between devices  6.22 us (17%)
  between operations  1.36 us (4%)
    all_to_all x1, blocking collectives, body(): own_share = lax.all_to_all(payload, 'tile', 0, 0)  11.4 us
    all_to_all x1, blocking collectives, body(): info = lax.all_to_all(summed, 'tm', 0, 0)  6.53 us
    ppermute x1, starting transfers between devices, body(): from_before = lax.ppermute(up, 'tile', onward)  4.93 us
    pallas_call x1, Pallas kernels, body(): pl.pallas_call(functools.partial(kernel_inner, sub_rows, sub_cols, frames...  4.83 us
    pallas_call x1, Pallas kernels, body(): pl.pallas_call(functools.partial(kernel_edge, sub_rows, sub_cols, frames)...  4.03 us
    ppermute x1, starting transfers between devices, body(): from_after = lax.ppermute(down, 'tile', backward)  1.29 us
    pallas_call x1, Pallas kernels, body(): pl.pallas_call(functools.partial(kernel_smooth, tiles, blocks, frames, fl...  1.2 us
  transfers between devices with their start and end apart: 2, of which 0 were waited for; matrix products, arithmetic and copies ran while one was open for 0% of the time, Pallas kernels for 13%

profile of v3, /device:TPU:0, one launch (start us, length us, event | category | flops | bytes accessed | tf_op | source)
XLA Modules:
  0.0 36.0 jit_solution(11315110479097826418)
XLA Ops:
  1.3 0.0 copy-start
  1.3 0.0 copy-start.1
  1.3 4.0 %edge_moments.1 = (f32[3,24,128]{2,1,0:T(8,128)S(1)}, f32[3,24,128]{2,1,0:T(8,128)S(1)}, f32[3,2,2,2,24,128]{5,4,3,2,1,0:T(8,128)S(1)}, f32[3,5,8,128]{3,2,1,0:T...) custom-call(bf16[3,2400,800]{2,1,0:T(8,128)(2,1)} %bitcast.10, ...), custom_call_target="tpu_custom_call" | custom-call | flops 1179648000 | bytes 4608000 | tf_op jit(solution)/shard_map/edge_moments/pallas_call | solution.py:466
  5.3 4.9 %collective-permute-start = (f32[3,24,128]{2,1,0:T(8,128)S(1)}, f32[3,24,128]{2,1,0:T(8,128)S(1)}, u32[]{:S(2)}, u32[]{:S(2)}) collective-permute-start(f32[3,24,128]{2,1,0:T(8,128)S(1)} %get-tuple-element.15), channel_id=1, source_target_pairs={{0,4},{4,8},{8,12},{1,5},{5,9},{9,13},{2,6},{6,10},{10,14},{3,7},{... | collective-permute-start | bytes 110600 | tf_op jit(solution)/shard_map/ppermute | solution.py:493
  10.3 1.3 %collective-permute-start.1 = (f32[3,24,128]{2,1,0:T(8,128)S(1)}, f32[3,24,128]{2,1,0:T(8,128)S(1)}, u32[]{:S(2)}, u32[]{:S(2)}) collective-permute-start(f32[3,24,128]{2,1,0:T(8,128)S(1)} %get-tuple-element.16), channel_id=1, source_target_pairs={{4,0},{8,4},{12,8},{5,1},{9,5},{13,9},{6,2},{10,6},{14,10},{7,3},{... | collective-permute-start | bytes 110600 | tf_op jit(solution)/shard_map/ppermute | solution.py:494
  11.6 4.8 %inner_moments.1 = (f32[24,256]{1,0:T(8,128)S(1)}, f32[2,2,2,24,128]{4,3,2,1,0:T(8,128)S(1)}, f32[2,2,24,128]{3,2,1,0:T(8,128)S(1)}, f32[24,128]{1,0:T(8,128)S(1)}) custom-call(bf16[3,2400,800]{2,1,0:T(8,128)(2,1)} %bitcast.11, bf16[960,800]{1,0:T(8,128)(2,1)S(1)} %get-tuple-element.17.ahead_ref, f32[3,5,8,128]{3,2,1,0:T(8,128)S(1)} %get-tuple-element.18.geo_ref, ...), custom_call_target="tpu_custom_call" | custom-call | flops 1769472000 | bytes 6912000 | tf_op jit(solution)/shard_map/inner_moments/pallas_call | solution.py:495
  16.4 0.0 collective-permute-done.before_ref
  16.4 0.0 collective-permute-done.1.after_ref
  16.4 0.0 copy-done
  16.4 0.4 %join_halo.1 = f32[4,16,128]{2,1,0:T(8,128)S(1)} custom-call(f32[24,128]{1,0:T(8,128)S(1)} %get-tuple-element.14.live_ref, f32[3,24,128]{2,1,0:T(8,128)S(1)} %collective-permute-done.before_ref, f32[3,24,128]{2,1,0:T(8,128)S(1)} %collective-permute-done.1.after_ref, f32[24,256]{1,0:T(8,128)S(1)} %get-tuple-element.22.pm_ref, ...), custom_call_target="tpu_custom_call" | custom-call | tf_op jit(solution)/shard_map/join_halo/pallas_call | solution.py:517
  16.8 11.4 %all_to_all.10.in_ref = f32[4,16,128]{2,1,0:T(8,128)S(1)} all-to-all(f32[4,16,128]{2,1,0:T(8,128)S(1)} %join_halo.1), channel_id=1, replica_groups=mesh['grp'=2,'tile'=4,'tm'=4] {'tile'}, dimensions={0} | all-to-all | bytes 65536 | tf_op jit(solution)/shard_map/all_to_all | solution.py:525
  28.2 6.5 %all_to_all.11.in_ref = f32[4,16,128]{2,1,0:T(8,128)S(1)} all-to-all(f32[4,16,128]{2,1,0:T(8,128)S(1)} %sum_tiles.1), channel_id=1, replica_groups=mesh['grp'=2,'tile'=4,'tm'=4] {'tm'}, dimensions={0} | all-to-all | bytes 65536 | tf_op jit(solution)/shard_map/all_to_all | solution.py:534
  34.8 0.0 copy-done.1
  34.8 1.2 %smooth.1 = (f32[24,64]{1,0:T(8,128)}, f32[24,64]{1,0:T(8,128)}) custom-call(f32[4,16,128]{2,1,0:T(8,128)S(1)} %all_to_all.11.in_ref, f32[1,256]{1,0:T(1,128)S(1)} %bitcast.9, f32[1,256]{1,0:T(1,128)S(1)} %bitcast.8), custom_call_target="tpu_custom_call" | custom-call | tf_op jit(solution)/shard_map/smooth/pallas_call | solution.py:535
  (1 shorter events, 0.0 us)
Async XLA Ops:
  1.3 15.2 %copy-start = (f32[256]{0:T(256)S(1)}, f32[256]{0:T(256)}, u32[]{:S(2)}) copy-start(f32[256]{0:T(256)} %param.13) | copy-start | bytes 3076
  1.3 33.5 %copy-start.1 = (f32[256]{0:T(256)S(1)}, f32[256]{0:T(256)}, u32[]{:S(2)}) copy-start(f32[256]{0:T(256)} %param.12) | copy-start | bytes 3076
  5.3 11.1 %collective-permute-start = (f32[3,24,128]{2,1,0:T(8,128)S(1)}, f32[3,24,128]{2,1,0:T(8,128)S(1)}, u32[]{:S(2)}, u32[]{:S(2)}) collective-permute-start(f32[3,24,128]{2,1,0:T(8,128)S(1)} %get-tuple-element.15), channel_id=1, source_target_pairs={{0,4},{4,8},{8,12},{1,5},{5,9},{9,13},{2,6},{6,10},{10,14},{3,7},{... | collective-permute-start | bytes 110600 | tf_op jit(solution)/shard_map/ppermute | solution.py:493
  10.3 6.1 %collective-permute-start.1 = (f32[3,24,128]{2,1,0:T(8,128)S(1)}, f32[3,24,128]{2,1,0:T(8,128)S(1)}, u32[]{:S(2)}, u32[]{:S(2)}) collective-permute-start(f32[3,24,128]{2,1,0:T(8,128)S(1)} %get-tuple-element.16), channel_id=1, source_target_pairs={{4,0},{8,4},{12,8},{5,1},{9,5},{13,9},{6,2},{10,6},{14,10},{7,3},{... | collective-permute-start | bytes 110600 | tf_op jit(solution)/shard_map/ppermute | solution.py:494

commit v4 on v2

--- a/solution.py
+++ b/solution.py
@@ -113,86 +113,155 @@
     return plain, lines
 
 
-def block_moments(x_ref, geo_ref, w_ref, p_ref, sub_cols, frames):
-    count = len(x_ref)
-    for n in range(count):
+def block_moments(pixels, row_pos, w_ref, p_ref, sub_cols, frames):
+    for h in range(2):
+        first, size = half_columns(h, sub_cols, pixels.shape[1])
+        r = jnp.dot(
+            pixels[:, first : first + size], w_ref[h, 0:size, :], preferred_element_type=jnp.float32
+        )
+        plain, lines = row_sums(row_pos[h], r, frames)
+        p_ref[h, 0] = plain
+        p_ref[h, 1] = lines
+
+
+def block_weights(geo_ref, w_ref):
+    for h in range(2):
+        build_weights(geo_ref[2 * h : 2 * h + 1, :], w_ref.at[h])
+
+
+def row_positions(geo_ref):
+    return [geo_ref[2 * h + 1 : 2 * h + 2, :] for h in range(2)]
+
+
+def strip_total(p_ref, s, k, h, a):
+    total = None
+    for i in (k - 1, k, k + 1):
+        if 0 <= i < p_ref.shape[1]:
+            v = p_ref[s, i, h, a]
+            total = v if total is None else total + v
+    return total
+
+
+def mask_of(mask_ref, s, k, h):
+    cols = mask_ref.shape[3] // 2
+    return mask_ref[s, k].astype(jnp.float32)[:, h * cols : (h + 1) * cols]
+
+
+def inner_projection(p_ref, mask_ref, modes_ref, s):
+    last = p_ref.shape[1] - 1
+    frames, sub_cols = mask_ref.shape[2:]
+    cols = sub_cols // 2
+    modes = jnp.zeros((frames, modes_ref.shape[-1]), jnp.float32)
+    count = jnp.zeros((frames, LANES), jnp.float32)
+    none = jnp.zeros((frames, cols), jnp.float32)
+    for g in range(1, last, 3):
+        order = [None] * 3
+        for k in range(g, min(g + 3, last)):
+            order[slot_of(k, s)] = k
         for h in range(2):
-            build_weights(geo_ref[n][2 * h : 2 * h + 1, :], w_ref.at[n, h])
-    for n in range(count):
-        for h in range(2):
-            first, size = half_columns(h, sub_cols, x_ref[n].shape[1])
-            r = jnp.dot(
-                x_ref[n][:, first : first + size],
-                w_ref[n, h, 0:size, :],
+            mask = side_by_side([none if k is None else mask_of(mask_ref, s, k, h) for k in order])
+            count = count + mask
+            plain, lines = (
+                by_slot([None if k is None else strip_total(p_ref, s, k, h, a) for k in order], cols)
+                for a in range(2)
+            )
+            modes = modes + jnp.dot(
+                slope_terms(plain, lines, mask),
+                stacked(modes_ref, [None if k is None else (s, k) for k in order], h, cols),
                 preferred_element_type=jnp.float32,
             )
-            plain, lines = row_sums(geo_ref[n][2 * h + 1 : 2 * h + 2, :], r, frames)
-            p_ref[n][h, 0] = plain
-            p_ref[n][h, 1] = lines
-
-
-def kernel_edge(
+    return modes, count
+
+
+def kernel_first(
     sub_rows, sub_cols, frames, x_hbm, off_hbm, mask_hbm, modes_hbm,
-    up_ref, down_ref, p_ref, geo_ref, buf, mask_ref, modes_ref,
-    w_ref, off_ref, sem, side_sem,
+    up_ref, down_ref, p_ref, geo_ref, mask_ref, modes_ref, ahead_ref, pm_ref, count_ref,
+    buf, edge_buf, w_ref, off_ref, sem, side_sem,
 ):
     sensors = x_hbm.shape[0]
     block = SIDE * frames
+    piece = block // 2
     last = sub_rows - 1
     cols = sub_cols // 2
-
-    def copy(s, i):
-        return pltpu.make_async_copy(
-            x_hbm.at[s, pl.ds(i * block, block)], buf.at[s, i], sem.at[s, i]
-        )
+    final = sensors - 1
+    order = (0, last, *range(1, last))
+
+    def place(s, i):
+        if isinstance(s, int) and s == final:
+            return ahead_ref.at[i - 1] if 0 < i < last else edge_buf.at[min(i, 1)]
+        return buf.at[s, i]
+
+    def copies(s, i):
+        return [
+            pltpu.make_async_copy(
+                x_hbm.at[s, pl.ds(i * block + z * piece, piece)],
+                place(s, i).at[pl.ds(z * piece, piece)],
+                sem.at[s, i, z],
+            )
+            for z in range(2)
+        ]
+
+    def wait(s, i):
+        for c in copies(s, i):
+            c.wait()
 
     off_copy = pltpu.make_async_copy(off_hbm, off_ref, side_sem.at[0])
     mask_copy = pltpu.make_async_copy(mask_hbm, mask_ref, side_sem.at[1])
     modes_copy = pltpu.make_async_copy(modes_hbm, modes_ref, side_sem.at[2])
     off_copy.start()
     for s in range(sensors):
-        for i in (0, last):
-            copy(s, i).start()
-    for s in range(sensors):
-        for i in range(1, last):
-            copy(s, i).start()
-    mask_copy.start()
-    modes_copy.start()
+        for i in order:
+            for c in copies(s, i):
+                c.start()
+        if s == 0:
+            mask_copy.start()
+            modes_copy.start()
     off_copy.wait()
     geometry(geo_ref, off_ref, sensors, sub_rows, sub_cols, x_hbm.shape[2])
+    block_weights(geo_ref.at[0, order[0]], w_ref.at[0])
 
     def step(s, carry):
-        copy(s, 0).wait()
-        copy(s, last).wait()
+        for n, i in enumerate(order):
+            wait(s, i)
+            after = (s, order[n + 1]) if n + 1 < sub_rows else (s + 1, order[0])
+            block_weights(geo_ref.at[after], w_ref.at[(n + 1) % sub_rows])
+            block_moments(
+                buf.at[s, i], row_positions(geo_ref.at[s, i]), w_ref.at[n], p_ref.at[s, i], sub_cols, frames
+            )
+        return carry
+
+    lax.fori_loop(0, final, step, 0)
+    mask_copy.wait()
+    modes_copy.wait()
+    modes = jnp.zeros(pm_ref.shape, jnp.float32)
+    count = jnp.zeros(count_ref.shape, jnp.float32)
+    for s in range(final):
+        part, number = inner_projection(p_ref, mask_ref, modes_ref, s)
+        modes = modes + part
+        count = count + number
+    pm_ref[...] = modes
+    count_ref[...] = count
+    block_weights(geo_ref.at[final, last], w_ref.at[1])
+    for n, i in enumerate((0, last)):
+        wait(final, i)
         block_moments(
-            [buf.at[s, 0], buf.at[s, last]],
-            [geo_ref.at[s, 0], geo_ref.at[s, last]],
-            w_ref,
-            [p_ref.at[s, 0], p_ref.at[s, 1]],
-            sub_cols,
-            frames,
+            place(final, i), row_positions(geo_ref.at[final, i]), w_ref.at[n], p_ref.at[final, i], sub_cols, frames
         )
-        return carry
-
-    lax.fori_loop(0, sensors, step, 0)
     left = lane_iota() < HALF
-    for ref, e, strip in ((down_ref, 0, -1), (up_ref, 1, sub_rows)):
+    for ref, i, strip in ((down_ref, 0, -1), (up_ref, last, sub_rows)):
         pair = []
         for h in range(2):
             both = []
             for a in range(2):
-                order = [None] * 3
+                pieces = [None] * 3
                 for s in range(sensors):
-                    order[slot_of(strip, s)] = p_ref[s, e, h, a]
-                both.append(by_slot(order, cols))
+                    pieces[slot_of(strip, s)] = p_ref[s, i, h, a]
+                both.append(by_slot(pieces, cols))
             ref[h] = both[0]
             pair.append(both[1])
         ref[2] = jnp.where(left, pair[0], pltpu.roll(pair[1], HALF, axis=1))
-    for s in range(sensors):
-        for i in range(1, last):
-            copy(s, i).wait()
-    mask_copy.wait()
-    modes_copy.wait()
+    for i in range(1, last):
+        wait(final, i)
 
 
 def slope_terms(plain, lines, mask):
@@ -219,82 +288,52 @@
     return jnp.concatenate(parts, axis=0).astype(jnp.bfloat16)
 
 
-def kernel_inner(
-    sub_rows, sub_cols, frames, x_ref, geo_ref, pe_ref, mask_ref, modes_ref,
+class OneSensor:
+    def __init__(self, ref):
+        self.ref = ref
+        self.shape = ref.shape
+
+    def __getitem__(self, at):
+        return self.ref[0, at[1], at[2], at[3]]
+
+
+def kernel_second(
+    sub_rows, sub_cols, frames, ahead_ref, geo_ref, pf_ref, mask_ref, modes_ref, pm_in_ref, count_in_ref,
     pm_ref, edge_ref, em_ref, count_ref, w_ref, p_ref,
 ):
-    sensors = x_ref.shape[0]
+    sensors = pf_ref.shape[0]
     last = sub_rows - 1
     cols = sub_cols // 2
-
-    def step(s, carry):
+    final = sensors - 1
+    for i in range(1, last):
+        block_weights(geo_ref.at[final, i], w_ref.at[i - 1])
+    for i in range(1, last):
         block_moments(
-            [x_ref.at[s, i] for i in range(1, last)],
-            [geo_ref.at[s, i] for i in range(1, last)],
-            w_ref,
-            [p_ref.at[s, i - 1] for i in range(1, last)],
-            sub_cols,
-            frames,
+            ahead_ref.at[i - 1], row_positions(geo_ref.at[final, i]), w_ref.at[i - 1], p_ref.at[0, i], sub_cols, frames
         )
-        return carry
-
-    lax.fori_loop(0, sensors, step, 0)
-
-    def partial(s, i, h, a):
-        if i == 0:
-            return pe_ref[s, 0, h, a]
-        if i == last:
-            return pe_ref[s, 1, h, a]
-        return p_ref[s, i - 1, h, a]
-
-    def strip_total(s, k, h, a):
-        total = None
-        for i in (k - 1, k, k + 1):
-            if 0 <= i <= last:
-                v = partial(s, i, h, a)
-                total = v if total is None else total + v
-        return total
-
-    def mask_of(s, k, h):
-        return mask_ref[s, k].astype(jnp.float32)[:, h * cols : (h + 1) * cols]
-
-    count = jnp.zeros((frames, LANES), jnp.float32)
+    for i in (0, last):
+        p_ref[0, i] = pf_ref[final, i]
+    modes, count = inner_projection(OneSensor(p_ref), mask_ref, modes_ref, final)
+    count = count + count_in_ref[...]
     for e, k in enumerate((0, last)):
         order = [None] * 3
         for s in range(sensors):
             order[slot_of(k, s)] = s
         for h in range(2):
-            m = side_by_side([mask_of(s, k, h) for s in order])
+            m = side_by_side([mask_of(mask_ref, s, k, h) for s in order])
             em_ref[e, h] = m
             count = count + m
             for a in range(2):
-                edge_ref[e, h, a] = by_slot([strip_total(s, k, h, a) for s in order], cols)
-    modes = jnp.zeros((frames, modes_ref.shape[-1]), jnp.float32)
-    for s in range(sensors):
-        for g in range(1, last, 3):
-            order = [None] * 3
-            for k in range(g, min(g + 3, last)):
-                order[slot_of(k, s)] = k
-            for h in range(2):
-                none = jnp.zeros((frames, cols), jnp.float32)
-                mask = side_by_side([none if k is None else mask_of(s, k, h) for k in order])
-                count = count + mask
-                plain, lines = (
-                    by_slot([None if k is None else strip_total(s, k, h, a) for k in order], cols)
-                    for a in range(2)
+                edge_ref[e, h, a] = by_slot(
+                    [strip_total(OneSensor(p_ref) if s == final else pf_ref, s, k, h, a) for s in order], cols
                 )
-                modes = modes + jnp.dot(
-                    slope_terms(plain, lines, mask),
-                    stacked(modes_ref, [None if k is None else (s, k) for k in order], h, cols),
-                    preferred_element_type=jnp.float32,
-                )
-    pm_ref[...] = modes
+    pm_ref[...] = pm_in_ref[...] + modes
     count_ref[...] = jnp.broadcast_to(0.5 * jnp.sum(count, axis=1, keepdims=True), count_ref.shape)
 
 
 def kernel_join(
     sub_rows, sub_cols, frames, tiles, blocks,
-    live_ref, before_ref, after_ref, pm_ref, edge_ref, em_ref, count_ref, modes_ref, gain_ref, out_ref,
+    live_ref, after_ref, before_ref, pm_ref, edge_ref, em_ref, count_ref, modes_ref, gain_ref, out_ref,
 ):
     sensors = modes_ref.shape[1]
     last = sub_rows - 1
@@ -317,9 +356,8 @@
                 stacked(modes_ref, [None if s is None else (s, k) for s in order], h, cols),
                 preferred_element_type=jnp.float32,
             )
-    frame = lax.broadcasted_iota(jnp.int32, (frames, 1), 0)
-    live = (frame < live_ref[0]).astype(jnp.float32)
-    info = gain_ref[...] * modes * live
+    live = (lax.broadcasted_iota(jnp.int32, (frames, LANES), 0) < live_ref[0]).astype(jnp.float32)
+    info = gain_ref[...] * modes * jnp.concatenate([live] * (modes.shape[1] // LANES), axis=1)
     own = lane_iota(frames) == lax.broadcasted_iota(jnp.int32, (frames, LANES), 0)
     counts = jnp.sum(jnp.where(own, count_ref[...] * live, 0.0), axis=0, keepdims=True)
     share = modes.shape[1] // tiles
@@ -433,10 +471,10 @@
     x = jnp.transpose(pixels, (0, 2, 1, 3)).reshape(sensors, lines * frames, width)
     off = jnp.transpose(offsets, (0, 1, 3, 2))
     msk = jnp.transpose(mask, (0, 2, 1, 3))
+    block = SIDE * frames
     x, off, msk, slope_to_modes = (
         pltpu.with_memory_space_constraint(v, pltpu.HBM) for v in (x, off, msk, slope_to_modes)
     )
-    block = SIDE * frames
     inner = sub_rows - 2
     depth = max(half_columns(h, sub_cols, width)[1] for h in range(2))
     params = pltpu.CompilerParams(vmem_limit_bytes=VMEM_LIMIT)
@@ -446,51 +484,55 @@
             flops=2 * chunks * block * width * 256, bytes_accessed=chunks * block * width * 2, transcendentals=0
         )
 
-    up, down, parts, geo, buf, mask_v, modes_v = pl.pallas_call(
-        functools.partial(kernel_edge, sub_rows, sub_cols, frames),
+    up, down, parts, geo, mask_v, modes_v, ahead, modes_first, count_first = pl.pallas_call(
+        functools.partial(kernel_first, sub_rows, sub_cols, frames),
         out_shape=(
             jax.ShapeDtypeStruct((3, frames, LANES), f32),
             jax.ShapeDtypeStruct((3, frames, LANES), f32),
-            pltpu.VMEM((sensors, 2, 2, 2, frames, LANES), f32),
+            pltpu.VMEM((sensors, sub_rows, 2, 2, frames, LANES), f32),
             pltpu.VMEM((sensors, sub_rows, 8, LANES), f32),
-            pltpu.VMEM((sensors, sub_rows, block, width), bf16),
             pltpu.VMEM(msk.shape, msk.dtype),
             pltpu.VMEM(slope_to_modes.shape, bf16),
+            pltpu.VMEM((inner, block, width), bf16),
+            pltpu.VMEM((frames, modes), f32),
+            pltpu.VMEM((frames, LANES), f32),
         ),
         in_specs=[HBM] * 4,
-        out_specs=(VMEM,) * 7,
+        out_specs=(VMEM,) * 9,
         scratch_shapes=[
-            pltpu.VMEM((2, 2, depth, LANES), bf16),
+            pltpu.VMEM((sensors - 1, sub_rows, block, width), bf16),
+            pltpu.VMEM((2, block, width), bf16),
+            pltpu.VMEM((sub_rows, 2, depth, LANES), bf16),
             pltpu.VMEM(off.shape, off.dtype),
-            pltpu.SemaphoreType.DMA((sensors, sub_rows)),
+            pltpu.SemaphoreType.DMA((sensors, sub_rows, 2)),
             pltpu.SemaphoreType.DMA((3,)),
         ],
         compiler_params=params,
-        cost_estimate=cost(2 * sensors),
-        name="edge_moments",
+        cost_estimate=cost(sensors * sub_rows - inner),
+        name="first_moments",
     )(x, off, msk, slope_to_modes)
     onward = [(i, i + 1) for i in range(tiles - 1)]
     backward = [(j, i) for i, j in onward]
+    from_after = lax.ppermute(down, "tile", backward)
     from_before = lax.ppermute(up, "tile", onward)
-    from_after = lax.ppermute(down, "tile", backward)
     partial_modes, edge, edge_mask, count = pl.pallas_call(
-        functools.partial(kernel_inner, sub_rows, sub_cols, frames),
+        functools.partial(kernel_second, sub_rows, sub_cols, frames),
         out_shape=(
             pltpu.VMEM((frames, modes), f32),
             pltpu.VMEM((2, 2, 2, frames, LANES), f32),
             pltpu.VMEM((2, 2, frames, LANES), f32),
             pltpu.VMEM((frames, LANES), f32),
         ),
-        in_specs=[VMEM] * 5,
+        in_specs=[VMEM] * 7,
         out_specs=(VMEM,) * 4,
         scratch_shapes=[
             pltpu.VMEM((inner, 2, depth, LANES), bf16),
-            pltpu.VMEM((sensors, inner, 2, 2, frames, LANES), f32),
+            pltpu.VMEM((1, sub_rows, 2, 2, frames, LANES), f32),
         ],
         compiler_params=params,
-        cost_estimate=cost(inner * sensors),
-        name="inner_moments",
-    )(buf, geo, parts, mask_v, modes_v)
+        cost_estimate=cost(inner),
+        name="second_moments",
+    )(ahead, geo, parts, mask_v, modes_v, modes_first, count_first)
     gain = mode_gain.reshape(1, modes)
     packed = -(-(frames * share // LANES + 1) // 8) * 8
     payload = pl.pallas_call(
@@ -500,7 +542,7 @@
         out_specs=VMEM,
         compiler_params=params,
         name="join_halo",
-    )(frame_count, from_before, from_after, partial_modes, edge, edge_mask, count, modes_v, gain)
+    )(frame_count, from_after, from_before, partial_modes, edge, edge_mask, count, modes_v, gain)
     info = lax.all_to_all(payload, ("tile", "tm"), 0, 0)
     return pl.pallas_call(
         functools.partial(kernel_smooth, tiles, blocks, frames, float(total_subaps)),

time: 34.2 us -> 36.4 us (1.064)
  Pallas kernels: 11.6 us -> 13.5 us
  starting transfers between devices: 6.22 us -> 6.84 us
  waiting for transfers between devices: 0.44 us -> 0.01 us
    pallas_call x2, Pallas kernels: 10.1 us -> 12 us  [the longest x1 10.7 us: body(): pl.pallas_call(functools.partial(kernel_first, sub_rows, sub_cols, frames...]
    ppermute x1, starting transfers between devices: 4.93 us -> 5.55 us  [body(): from_before = lax.ppermute(up, 'tile', onward)]
    ppermute x1, waiting for transfers between devices: 0.44 us -> 0.01 us  [body(): from_after = lax.ppermute(down, 'tile', backward)]
  transfers between devices with their start and end apart: 2 -> 2, of which waited for: 1 -> 0; matrix products, arithmetic and copies ran while one was open for 0% -> 0% of each run, Pallas kernels for 10% -> 4%
where the time goes in v4:
time: 36.4 us; the launch traced here: 36.2 us
  blocking collectives  14.5 us (40%)
  Pallas kernels  13.5 us (37%)
  starting transfers between devices  6.84 us (19%)
  between operations  1.34 us (4%)
    all_to_all x1, blocking collectives, body(): info = lax.all_to_all(payload, ('tile', 'tm'), 0, 0)  14.5 us
    pallas_call x1, Pallas kernels, body(): pl.pallas_call(functools.partial(kernel_first, sub_rows, sub_cols, frames...  10.7 us
    ppermute x1, starting transfers between devices, body(): from_before = lax.ppermute(up, 'tile', onward)  5.55 us
    pallas_call x1, Pallas kernels, body(): pl.pallas_call(functools.partial(kernel_second, sub_rows, sub_cols, frame...  1.3 us
    ppermute x1, starting transfers between devices, body(): from_after = lax.ppermute(down, 'tile', backward)  1.29 us
    pallas_call x1, Pallas kernels, body(): pl.pallas_call(functools.partial(kernel_smooth, tiles, blocks, frames, fl...  1.19 us
  transfers between devices with their start and end apart: 2, of which 0 were waited for; matrix products, arithmetic and copies ran while one was open for 0% of the time, Pallas kernels for 4%

profile of v4, /device:TPU:0, one launch (start us, length us, event | category | flops | bytes accessed | tf_op | source)
XLA Modules:
  0.0 36.2 jit_solution(4102822513002542848)
XLA Ops:
  0.6 0.0 copy-start
  0.6 0.0 copy-start.1
  0.7 10.7 %first_moments.1 = (f32[3,24,128]{2,1,0:T(8,128)S(1)}, f32[3,24,128]{2,1,0:T(8,128)S(1)}, f32[3,5,2,2,24,128]{5,4,3,2,1,0:T(8,128)S(1)}, f32[3,5,8,128]{3,2,1,0:...) custom-call(bf16[3,2400,800]{2,1,0:T(8,128)(2,1)} %bitcast.10, ...), custom_call_target="tpu_custom_call" | custom-call | flops 2359296000 | bytes 9216000 | tf_op jit(solution)/shard_map/first_moments/pallas_call | solution.py:487
  11.3 1.3 %collective-permute-start = (f32[3,24,128]{2,1,0:T(8,128)S(1)}, f32[3,24,128]{2,1,0:T(8,128)S(1)}, u32[]{:S(2)}, u32[]{:S(2)}) collective-permute-start(f32[3,24,128]{2,1,0:T(8,128)S(1)} %get-tuple-element.15), channel_id=1, source_target_pairs={{4,0},{8,4},{12,8},{5,1},{9,5},{13,9},{6,2},{10,6},{14,10},{7,3},{... | collective-permute-start | bytes 110600 | tf_op jit(solution)/shard_map/ppermute | solution.py:516
  12.6 5.6 %collective-permute-start.1 = (f32[3,24,128]{2,1,0:T(8,128)S(1)}, f32[3,24,128]{2,1,0:T(8,128)S(1)}, u32[]{:S(2)}, u32[]{:S(2)}) collective-permute-start(f32[3,24,128]{2,1,0:T(8,128)S(1)} %get-tuple-element.16), channel_id=1, source_target_pairs={{0,4},{4,8},{8,12},{1,5},{5,9},{9,13},{2,6},{6,10},{10,14},{3,7},{... | collective-permute-start | bytes 110600 | tf_op jit(solution)/shard_map/ppermute | solution.py:517
  18.8 1.3 %second_moments.1 = (f32[24,256]{1,0:T(8,128)S(1)}, f32[2,2,2,24,128]{4,3,2,1,0:T(8,128)S(1)}, f32[2,2,24,128]{3,2,1,0:T(8,128)S(1)}, f32[24,128]{1,0:T(8,128)S(1)}) custom-call(bf16[3,480,800]{2,1,0:T(8,128)(2,1)S(1)} %get-tuple-element.17.ahead_ref, f32[3,5,8,128]{3,2,1,0:T(8,128)S(1)} %get-tuple-element.18.geo_ref, ...), custom_call_target="tpu_custom_call" | custom-call | flops 589824000 | bytes 2304000 | tf_op jit(solution)/shard_map/second_moments/pallas_call | solution.py:518
  20.1 0.0 collective-permute-done.after_ref
  20.1 0.0 collective-permute-done.1.before_ref
  20.1 0.0 copy-done
  20.1 0.4 %join_halo.1 = f32[16,16,128]{2,1,0:T(8,128)S(1)} custom-call(s32[1]{0:T(128)S(6)} %copy.9.live_ref, f32[3,24,128]{2,1,0:T(8,128)S(1)} %collective-permute-done.after_ref, f32[3,24,128]{2,1,0:T(8,128)S(1)} %collective-permute-done.1.before_ref, f32[24,256]{1,0:T(8,128)S(1)} %get-tuple-element.24.pm_ref, ...), custom_call_target="tpu_custom_call" | custom-call | tf_op jit(solution)/shard_map/join_halo/pallas_call | solution.py:538
  20.5 14.5 %all_to_all.5.in_ref = f32[16,16,128]{2,1,0:T(8,128)S(1)} all-to-all(f32[16,16,128]{2,1,0:T(8,128)S(1)} %join_halo.1), channel_id=1, replica_groups=mesh['grp'=2,'tile'=4,'tm'=4] {'tile','tm'}, dimensions={0} | all-to-all | bytes 262144 | tf_op jit(solution)/shard_map/all_to_all | solution.py:546
  35.0 0.0 copy-done.1
  35.0 1.2 %smooth.1 = (f32[24,64]{1,0:T(8,128)}, f32[24,64]{1,0:T(8,128)}) custom-call(f32[16,16,128]{2,1,0:T(8,128)S(1)} %all_to_all.5.in_ref, f32[1,256]{1,0:T(1,128)S(1)} %bitcast.9, f32[1,256]{1,0:T(1,128)S(1)} %bitcast.8), custom_call_target="tpu_custom_call" | custom-call | tf_op jit(solution)/shard_map/smooth/pallas_call | solution.py:547
Async XLA Ops:
  0.6 19.5 %copy-start = (f32[256]{0:T(256)S(1)}, f32[256]{0:T(256)}, u32[]{:S(2)}) copy-start(f32[256]{0:T(256)} %param.13) | copy-start | bytes 3076
  0.6 34.4 %copy-start.1 = (f32[256]{0:T(256)S(1)}, f32[256]{0:T(256)}, u32[]{:S(2)}) copy-start(f32[256]{0:T(256)} %param.12) | copy-start | bytes 3076
  11.3 8.8 %collective-permute-start = (f32[3,24,128]{2,1,0:T(8,128)S(1)}, f32[3,24,128]{2,1,0:T(8,128)S(1)}, u32[]{:S(2)}, u32[]{:S(2)}) collective-permute-start(f32[3,24,128]{2,1,0:T(8,128)S(1)} %get-tuple-element.15), channel_id=1, source_target_pairs={{4,0},{8,4},{12,8},{5,1},{9,5},{13,9},{6,2},{10,6},{14,10},{7,3},{... | collective-permute-start | bytes 110600 | tf_op jit(solution)/shard_map/ppermute | solution.py:516
  12.6 7.5 %collective-permute-start.1 = (f32[3,24,128]{2,1,0:T(8,128)S(1)}, f32[3,24,128]{2,1,0:T(8,128)S(1)}, u32[]{:S(2)}, u32[]{:S(2)}) collective-permute-start(f32[3,24,128]{2,1,0:T(8,128)S(1)} %get-tuple-element.16), channel_id=1, source_target_pairs={{0,4},{4,8},{8,12},{1,5},{5,9},{9,13},{2,6},{6,10},{10,14},{3,7},{... | collective-permute-start | bytes 110600 | tf_op jit(solution)/shard_map/ppermute | solution.py:517

commit v5 on v4

--- a/solution.py
+++ b/solution.py
@@ -180,7 +180,6 @@
 ):
     sensors = x_hbm.shape[0]
     block = SIDE * frames
-    piece = block // 2
     last = sub_rows - 1
     cols = sub_cols // 2
     final = sensors - 1
@@ -191,19 +190,8 @@
             return ahead_ref.at[i - 1] if 0 < i < last else edge_buf.at[min(i, 1)]
         return buf.at[s, i]
 
-    def copies(s, i):
-        return [
-            pltpu.make_async_copy(
-                x_hbm.at[s, pl.ds(i * block + z * piece, piece)],
-                place(s, i).at[pl.ds(z * piece, piece)],
-                sem.at[s, i, z],
-            )
-            for z in range(2)
-        ]
-
-    def wait(s, i):
-        for c in copies(s, i):
-            c.wait()
+    def copy(s, i):
+        return pltpu.make_async_copy(x_hbm.at[s, pl.ds(i * block, block)], place(s, i), sem.at[s, i])
 
     off_copy = pltpu.make_async_copy(off_hbm, off_ref, side_sem.at[0])
     mask_copy = pltpu.make_async_copy(mask_hbm, mask_ref, side_sem.at[1])
@@ -211,23 +199,25 @@
     off_copy.start()
     for s in range(sensors):
         for i in order:
-            for c in copies(s, i):
-                c.start()
+            copy(s, i).start()
         if s == 0:
             mask_copy.start()
             modes_copy.start()
     off_copy.wait()
     geometry(geo_ref, off_ref, sensors, sub_rows, sub_cols, x_hbm.shape[2])
-    block_weights(geo_ref.at[0, order[0]], w_ref.at[0])
+
+    def blocks_of(s, which):
+        for i in which:
+            block_weights(geo_ref.at[s, i], w_ref.at[i])
+        for i in which:
+            copy(s, i).wait()
+        for i in which:
+            block_moments(
+                place(s, i), row_positions(geo_ref.at[s, i]), w_ref.at[i], p_ref.at[s, i], sub_cols, frames
+            )
 
     def step(s, carry):
-        for n, i in enumerate(order):
-            wait(s, i)
-            after = (s, order[n + 1]) if n + 1 < sub_rows else (s + 1, order[0])
-            block_weights(geo_ref.at[after], w_ref.at[(n + 1) % sub_rows])
-            block_moments(
-                buf.at[s, i], row_positions(geo_ref.at[s, i]), w_ref.at[n], p_ref.at[s, i], sub_cols, frames
-            )
+        blocks_of(s, order)
         return carry
 
     lax.fori_loop(0, final, step, 0)
@@ -241,12 +231,7 @@
         count = count + number
     pm_ref[...] = modes
     count_ref[...] = count
-    block_weights(geo_ref.at[final, last], w_ref.at[1])
-    for n, i in enumerate((0, last)):
-        wait(final, i)
-        block_moments(
-            place(final, i), row_positions(geo_ref.at[final, i]), w_ref.at[n], p_ref.at[final, i], sub_cols, frames
-        )
+    blocks_of(final, (0, last))
     left = lane_iota() < HALF
     for ref, i, strip in ((down_ref, 0, -1), (up_ref, last, sub_rows)):
         pair = []
@@ -261,7 +246,7 @@
             pair.append(both[1])
         ref[2] = jnp.where(left, pair[0], pltpu.roll(pair[1], HALF, axis=1))
     for i in range(1, last):
-        wait(final, i)
+        copy(final, i).wait()
 
 
 def slope_terms(plain, lines, mask):
@@ -333,7 +318,7 @@
 
 def kernel_join(
     sub_rows, sub_cols, frames, tiles, blocks,
-    live_ref, after_ref, before_ref, pm_ref, edge_ref, em_ref, count_ref, modes_ref, gain_ref, out_ref,
+    live_ref, before_ref, after_ref, pm_ref, edge_ref, em_ref, count_ref, modes_ref, gain_ref, out_ref,
 ):
     sensors = modes_ref.shape[1]
     last = sub_rows - 1
@@ -504,7 +489,7 @@
             pltpu.VMEM((2, block, width), bf16),
             pltpu.VMEM((sub_rows, 2, depth, LANES), bf16),
             pltpu.VMEM(off.shape, off.dtype),
-            pltpu.SemaphoreType.DMA((sensors, sub_rows, 2)),
+            pltpu.SemaphoreType.DMA((sensors, sub_rows)),
             pltpu.SemaphoreType.DMA((3,)),
         ],
         compiler_params=params,
@@ -513,8 +498,8 @@
     )(x, off, msk, slope_to_modes)
     onward = [(i, i + 1) for i in range(tiles - 1)]
     backward = [(j, i) for i, j in onward]
+    from_before = lax.ppermute(up, "tile", onward)
     from_after = lax.ppermute(down, "tile", backward)
-    from_before = lax.ppermute(up, "tile", onward)
     partial_modes, edge, edge_mask, count = pl.pallas_call(
         functools.partial(kernel_second, sub_rows, sub_cols, frames),
         out_shape=(
@@ -542,7 +527,7 @@
         out_specs=VMEM,
         compiler_params=params,
         name="join_halo",
-    )(frame_count, from_after, from_before, partial_modes, edge, edge_mask, count, modes_v, gain)
+    )(frame_count, from_before, from_after, partial_modes, edge, edge_mask, count, modes_v, gain)
     info = lax.all_to_all(payload, ("tile", "tm"), 0, 0)
     return pl.pallas_call(
         functools.partial(kernel_smooth, tiles, blocks, frames, float(total_subaps)),

time: 36.4 us -> 35 us (0.962)
  waiting for transfers between devices: 0.01 us -> 2.6 us
  blocking collectives: 14.5 us -> 12.7 us
  Pallas kernels: 13.5 us -> 11.9 us
  starting transfers between devices: 6.84 us -> 6.22 us
    ppermute x1, waiting for transfers between devices: 0.01 us -> 2.6 us  [body(): from_after = lax.ppermute(down, 'tile', backward)]
    all_to_all x1, blocking collectives: 14.5 us -> 12.7 us  [body(): info = lax.all_to_all(payload, ('tile', 'tm'), 0, 0)]
    pallas_call x1, Pallas kernels: 10.7 us -> 9.08 us  [body(): pl.pallas_call(functools.partial(kernel_first, sub_rows, sub_cols, frames...]
    ppermute x1, starting transfers between devices: 5.55 us -> 4.93 us  [body(): from_before = lax.ppermute(up, 'tile', onward)]
  transfers between devices with their start and end apart: 2 -> 2, of which waited for: 0 -> 1; matrix products, arithmetic and copies ran while one was open for 0% -> 0% of each run, Pallas kernels for 4% -> 4%
where the time goes in v5:
time: 35 us; the launch traced here: 34.8 us
  blocking collectives  12.7 us (36%)
  Pallas kernels  11.9 us (34%)
  starting transfers between devices  6.22 us (18%)
  waiting for transfers between devices  2.6 us (7%)
  between operations  1.33 us (4%)
    all_to_all x1, blocking collectives, body(): info = lax.all_to_all(payload, ('tile', 'tm'), 0, 0)  12.7 us
    pallas_call x1, Pallas kernels, body(): pl.pallas_call(functools.partial(kernel_first, sub_rows, sub_cols, frames...  9.08 us
    ppermute x1, starting transfers between devices, body(): from_before = lax.ppermute(up, 'tile', onward)  4.93 us
    ppermute x1, waiting for transfers between devices, body(): from_after = lax.ppermute(down, 'tile', backward)  2.6 us
    pallas_call x1, Pallas kernels, body(): pl.pallas_call(functools.partial(kernel_second, sub_rows, sub_cols, frame...  1.3 us
    ppermute x1, starting transfers between devices, body(): from_after = lax.ppermute(down, 'tile', backward)  1.29 us
    pallas_call x1, Pallas kernels, body(): pl.pallas_call(functools.partial(kernel_smooth, tiles, blocks, frames, fl...  1.19 us
  transfers between devices with their start and end apart: 2, of which 1 were waited for; matrix products, arithmetic and copies ran while one was open for 0% of the time, Pallas kernels for 4%

profile of v5, /device:TPU:0, one launch (start us, length us, event | category | flops | bytes accessed | tf_op | source)
XLA Modules:
  0.0 34.8 jit_solution(760806781314330854)
XLA Ops:
  0.6 0.0 copy-start
  0.6 0.0 copy-start.1
  0.7 9.1 %first_moments.1 = (f32[3,24,128]{2,1,0:T(8,128)S(1)}, f32[3,24,128]{2,1,0:T(8,128)S(1)}, f32[3,5,2,2,24,128]{5,4,3,2,1,0:T(8,128)S(1)}, f32[3,5,8,128]{3,2,1,0:...) custom-call(bf16[3,2400,800]{2,1,0:T(8,128)(2,1)} %bitcast.10, ...), custom_call_target="tpu_custom_call" | custom-call | flops 2359296000 | bytes 9216000 | tf_op jit(solution)/shard_map/first_moments/pallas_call | solution.py:472
  9.7 4.9 %collective-permute-start = (f32[3,24,128]{2,1,0:T(8,128)S(1)}, f32[3,24,128]{2,1,0:T(8,128)S(1)}, u32[]{:S(2)}, u32[]{:S(2)}) collective-permute-start(f32[3,24,128]{2,1,0:T(8,128)S(1)} %get-tuple-element.15), channel_id=1, source_target_pairs={{0,4},{4,8},{8,12},{1,5},{5,9},{9,13},{2,6},{6,10},{10,14},{3,7},{... | collective-permute-start | bytes 110600 | tf_op jit(solution)/shard_map/ppermute | solution.py:501
  14.7 1.3 %collective-permute-start.1 = (f32[3,24,128]{2,1,0:T(8,128)S(1)}, f32[3,24,128]{2,1,0:T(8,128)S(1)}, u32[]{:S(2)}, u32[]{:S(2)}) collective-permute-start(f32[3,24,128]{2,1,0:T(8,128)S(1)} %get-tuple-element.16), channel_id=1, source_target_pairs={{4,0},{8,4},{12,8},{5,1},{9,5},{13,9},{6,2},{10,6},{14,10},{7,3},{... | collective-permute-start | bytes 110600 | tf_op jit(solution)/shard_map/ppermute | solution.py:502
  16.6 1.3 %second_moments.1 = (f32[24,256]{1,0:T(8,128)S(1)}, f32[2,2,2,24,128]{4,3,2,1,0:T(8,128)S(1)}, f32[2,2,24,128]{3,2,1,0:T(8,128)S(1)}, f32[24,128]{1,0:T(8,128)S(1)}) custom-call(bf16[3,480,800]{2,1,0:T(8,128)(2,1)S(1)} %get-tuple-element.17.ahead_ref, f32[3,5,8,128]{3,2,1,0:T(8,128)S(1)} %get-tuple-element.18.geo_ref, ...), custom_call_target="tpu_custom_call" | custom-call | flops 589824000 | bytes 2304000 | tf_op jit(solution)/shard_map/second_moments/pallas_call | solution.py:503
  17.9 0.0 collective-permute-done.before_ref
  17.9 2.6 %collective-permute-done.1.after_ref = f32[3,24,128]{2,1,0:T(8,128)S(1)} collective-permute-done((f32[3,24,128]{2,1,0:T(8,128)S(1)}, f32[3,24,128]{2,1,0:T(8,128)S(1)}, u32[]{:S(2)}, u32[]{:S(2)}) %collective-permute-start.1) | collective-permute-done | bytes 36896 | tf_op jit(solution)/shard_map/ppermute | solution.py:502
  20.5 0.0 copy-done
  20.5 0.4 %join_halo.1 = f32[16,16,128]{2,1,0:T(8,128)S(1)} custom-call(s32[1]{0:T(128)S(6)} %copy.9.live_ref, f32[3,24,128]{2,1,0:T(8,128)S(1)} %collective-permute-done.before_ref, f32[3,24,128]{2,1,0:T(8,128)S(1)} %collective-permute-done.1.after_ref, f32[24,256]{1,0:T(8,128)S(1)} %get-tuple-element.24.pm_ref, ...), custom_call_target="tpu_custom_call" | custom-call | tf_op jit(solution)/shard_map/join_halo/pallas_call | solution.py:523
  20.9 12.7 %all_to_all.5.in_ref = f32[16,16,128]{2,1,0:T(8,128)S(1)} all-to-all(f32[16,16,128]{2,1,0:T(8,128)S(1)} %join_halo.1), channel_id=1, replica_groups=mesh['grp'=2,'tile'=4,'tm'=4] {'tile','tm'}, dimensions={0} | all-to-all | bytes 262144 | tf_op jit(solution)/shard_map/all_to_all | solution.py:531
  33.6 0.0 copy-done.1
  33.6 1.2 %smooth.1 = (f32[24,64]{1,0:T(8,128)}, f32[24,64]{1,0:T(8,128)}) custom-call(f32[16,16,128]{2,1,0:T(8,128)S(1)} %all_to_all.5.in_ref, f32[1,256]{1,0:T(1,128)S(1)} %bitcast.9, f32[1,256]{1,0:T(1,128)S(1)} %bitcast.8), custom_call_target="tpu_custom_call" | custom-call | tf_op jit(solution)/shard_map/smooth/pallas_call | solution.py:532
Async XLA Ops:
  0.6 19.9 %copy-start = (f32[256]{0:T(256)S(1)}, f32[256]{0:T(256)}, u32[]{:S(2)}) copy-start(f32[256]{0:T(256)} %param.13) | copy-start | bytes 3076
  0.6 32.9 %copy-start.1 = (f32[256]{0:T(256)S(1)}, f32[256]{0:T(256)}, u32[]{:S(2)}) copy-start(f32[256]{0:T(256)} %param.12) | copy-start | bytes 3076
  9.7 8.2 %collective-permute-start = (f32[3,24,128]{2,1,0:T(8,128)S(1)}, f32[3,24,128]{2,1,0:T(8,128)S(1)}, u32[]{:S(2)}, u32[]{:S(2)}) collective-permute-start(f32[3,24,128]{2,1,0:T(8,128)S(1)} %get-tuple-element.15), channel_id=1, source_target_pairs={{0,4},{4,8},{8,12},{1,5},{5,9},{9,13},{2,6},{6,10},{10,14},{3,7},{... | collective-permute-start | bytes 110600 | tf_op jit(solution)/shard_map/ppermute | solution.py:501
  14.7 5.9 %collective-permute-start.1 = (f32[3,24,128]{2,1,0:T(8,128)S(1)}, f32[3,24,128]{2,1,0:T(8,128)S(1)}, u32[]{:S(2)}, u32[]{:S(2)}) collective-permute-start(f32[3,24,128]{2,1,0:T(8,128)S(1)} %get-tuple-element.16), channel_id=1, source_target_pairs={{4,0},{8,4},{12,8},{5,1},{9,5},{13,9},{6,2},{10,6},{14,10},{7,3},{... | collective-permute-start | bytes 110600 | tf_op jit(solution)/shard_map/ppermute | solution.py:502

commit v6 on v2

--- a/solution.py
+++ b/solution.py
@@ -99,11 +99,11 @@
         w_ref[16 * t : 16 * t + 16, :] = jnp.where(jnp.abs(d) < 10.0, value, 0.0).astype(jnp.bfloat16)
 
 
-def row_sums(row_pos, r, frames):
+def row_sums(row_pos, r, frames, first_row=0):
     plain = jnp.zeros((frames, LANES), jnp.float32)
     lines = jnp.zeros((frames, LANES), jnp.float32)
     for y in range(r.shape[0] // frames):
-        d = float(y) - row_pos
+        d = float(y + first_row) - row_pos
         inside = jnp.abs(d) < 10.0
         one = jnp.where(inside, 1.0, 0.0)
         centred = jnp.where(inside, d, 0.0)
@@ -113,68 +113,58 @@
     return plain, lines
 
 
-def block_moments(x_ref, geo_ref, w_ref, p_ref, sub_cols, frames):
-    count = len(x_ref)
-    for n in range(count):
-        for h in range(2):
-            build_weights(geo_ref[n][2 * h : 2 * h + 1, :], w_ref.at[n, h])
-    for n in range(count):
-        for h in range(2):
-            first, size = half_columns(h, sub_cols, x_ref[n].shape[1])
-            r = jnp.dot(
-                x_ref[n][:, first : first + size],
-                w_ref[n, h, 0:size, :],
-                preferred_element_type=jnp.float32,
-            )
-            plain, lines = row_sums(geo_ref[n][2 * h + 1 : 2 * h + 2, :], r, frames)
-            p_ref[n][h, 0] = plain
-            p_ref[n][h, 1] = lines
-
-
-def kernel_edge(
-    sub_rows, sub_cols, frames, x_hbm, off_hbm, mask_hbm, modes_hbm,
-    up_ref, down_ref, p_ref, geo_ref, buf, mask_ref, modes_ref,
-    w_ref, off_ref, sem, side_sem,
+def block_weights(geo_ref, w_ref):
+    for h in range(2):
+        build_weights(geo_ref[2 * h : 2 * h + 1, :], w_ref.at[h])
+
+
+def block_moments(pixels, geo_ref, w_ref, sub_cols, frames, first_row=0):
+    out = []
+    for h in range(2):
+        first, size = half_columns(h, sub_cols, pixels.shape[1])
+        r = jnp.dot(
+            pixels[:, first : first + size], w_ref[h, 0:size, :], preferred_element_type=jnp.float32
+        )
+        out.append(row_sums(geo_ref[2 * h + 1 : 2 * h + 2, :], r, frames, first_row))
+    return out
+
+
+def kernel_halo(
+    sub_rows, sub_cols, frames, x_hbm, off_hbm, up_ref, down_ref, geo_ref,
+    buf, w_ref, p_ref, off_ref, sem, off_sem,
 ):
-    sensors = x_hbm.shape[0]
-    block = SIDE * frames
+    sensors, lines, width = x_hbm.shape
+    reach = SHIFT * frames
     last = sub_rows - 1
     cols = sub_cols // 2
 
-    def copy(s, i):
+    def copy(s, e):
         return pltpu.make_async_copy(
-            x_hbm.at[s, pl.ds(i * block, block)], buf.at[s, i], sem.at[s, i]
+            x_hbm.at[s, pl.ds(e * (lines - reach), reach)], buf.at[s, e], sem.at[s, e]
         )
 
-    off_copy = pltpu.make_async_copy(off_hbm, off_ref, side_sem.at[0])
-    mask_copy = pltpu.make_async_copy(mask_hbm, mask_ref, side_sem.at[1])
-    modes_copy = pltpu.make_async_copy(modes_hbm, modes_ref, side_sem.at[2])
+    off_copy = pltpu.make_async_copy(off_hbm, off_ref, off_sem)
     off_copy.start()
     for s in range(sensors):
-        for i in (0, last):
-            copy(s, i).start()
+        for e in range(2):
+            copy(s, e).start()
+    off_copy.wait()
+    geometry(geo_ref, off_ref, sensors, sub_rows, sub_cols, width)
     for s in range(sensors):
-        for i in range(1, last):
-            copy(s, i).start()
-    mask_copy.start()
-    modes_copy.start()
-    off_copy.wait()
-    geometry(geo_ref, off_ref, sensors, sub_rows, sub_cols, x_hbm.shape[2])
-
-    def step(s, carry):
-        copy(s, 0).wait()
-        copy(s, last).wait()
-        block_moments(
-            [buf.at[s, 0], buf.at[s, last]],
-            [geo_ref.at[s, 0], geo_ref.at[s, last]],
-            w_ref,
-            [p_ref.at[s, 0], p_ref.at[s, 1]],
-            sub_cols,
-            frames,
-        )
-        return carry
-
-    lax.fori_loop(0, sensors, step, 0)
+        for e in range(2):
+            block_weights(geo_ref.at[s, e * last], w_ref.at[s, e])
+    for s in range(sensors):
+        for e in range(2):
+            copy(s, e).wait()
+    for s in range(sensors):
+        for e in range(2):
+            first_row = e * (SIDE - SHIFT)
+            out = block_moments(
+                buf.at[s, e], geo_ref.at[s, e * last], w_ref.at[s, e], sub_cols, frames, first_row
+            )
+            for h in range(2):
+                for a in range(2):
+                    p_ref[s, e, h, a] = out[h][a]
     left = lane_iota() < HALF
     for ref, e, strip in ((down_ref, 0, -1), (up_ref, 1, sub_rows)):
         pair = []
@@ -188,11 +178,6 @@
             ref[h] = both[0]
             pair.append(both[1])
         ref[2] = jnp.where(left, pair[0], pltpu.roll(pair[1], HALF, axis=1))
-    for s in range(sensors):
-        for i in range(1, last):
-            copy(s, i).wait()
-    mask_copy.wait()
-    modes_copy.wait()
 
 
 def slope_terms(plain, lines, mask):
@@ -219,39 +204,34 @@
     return jnp.concatenate(parts, axis=0).astype(jnp.bfloat16)
 
 
-def kernel_inner(
-    sub_rows, sub_cols, frames, x_ref, geo_ref, pe_ref, mask_ref, modes_ref,
+def kernel_moments(
+    sub_rows, sub_cols, frames, x_ref, geo_ref, mask_ref, modes_ref,
     pm_ref, edge_ref, em_ref, count_ref, w_ref, p_ref,
 ):
     sensors = x_ref.shape[0]
+    block = SIDE * frames
     last = sub_rows - 1
     cols = sub_cols // 2
 
     def step(s, carry):
-        block_moments(
-            [x_ref.at[s, i] for i in range(1, last)],
-            [geo_ref.at[s, i] for i in range(1, last)],
-            w_ref,
-            [p_ref.at[s, i - 1] for i in range(1, last)],
-            sub_cols,
-            frames,
-        )
+        for i in range(sub_rows):
+            block_weights(geo_ref.at[s, i], w_ref.at[i])
+        for i in range(sub_rows):
+            out = block_moments(
+                x_ref.at[s, i * block : (i + 1) * block], geo_ref.at[s, i], w_ref.at[i], sub_cols, frames
+            )
+            for h in range(2):
+                for a in range(2):
+                    p_ref[s, i, h, a] = out[h][a]
         return carry
 
     lax.fori_loop(0, sensors, step, 0)
-
-    def partial(s, i, h, a):
-        if i == 0:
-            return pe_ref[s, 0, h, a]
-        if i == last:
-            return pe_ref[s, 1, h, a]
-        return p_ref[s, i - 1, h, a]
 
     def strip_total(s, k, h, a):
         total = None
         for i in (k - 1, k, k + 1):
             if 0 <= i <= last:
-                v = partial(s, i, h, a)
+                v = p_ref[s, i, h, a]
                 total = v if total is None else total + v
         return total
 
@@ -433,11 +413,11 @@
     x = jnp.transpose(pixels, (0, 2, 1, 3)).reshape(sensors, lines * frames, width)
     off = jnp.transpose(offsets, (0, 1, 3, 2))
     msk = jnp.transpose(mask, (0, 2, 1, 3))
-    x, off, msk, slope_to_modes = (
-        pltpu.with_memory_space_constraint(v, pltpu.HBM) for v in (x, off, msk, slope_to_modes)
+    pixels_v, mask_v, modes_v = (
+        pltpu.with_memory_space_constraint(v, pltpu.VMEM) for v in (x, msk, slope_to_modes)
     )
+    x, off = (pltpu.with_memory_space_constraint(v, pltpu.HBM) for v in (x, off))
     block = SIDE * frames
-    inner = sub_rows - 2
     depth = max(half_columns(h, sub_cols, width)[1] for h in range(2))
     params = pltpu.CompilerParams(vmem_limit_bytes=VMEM_LIMIT)
 
@@ -446,51 +426,49 @@
             flops=2 * chunks * block * width * 256, bytes_accessed=chunks * block * width * 2, transcendentals=0
         )
 
-    up, down, parts, geo, buf, mask_v, modes_v = pl.pallas_call(
-        functools.partial(kernel_edge, sub_rows, sub_cols, frames),
+    up, down, geo = pl.pallas_call(
+        functools.partial(kernel_halo, sub_rows, sub_cols, frames),
         out_shape=(
             jax.ShapeDtypeStruct((3, frames, LANES), f32),
             jax.ShapeDtypeStruct((3, frames, LANES), f32),
+            pltpu.VMEM((sensors, sub_rows, 8, LANES), f32),
+        ),
+        in_specs=[HBM] * 2,
+        out_specs=(VMEM,) * 3,
+        scratch_shapes=[
+            pltpu.VMEM((sensors, 2, SHIFT * frames, width), bf16),
+            pltpu.VMEM((sensors, 2, 2, depth, LANES), bf16),
             pltpu.VMEM((sensors, 2, 2, 2, frames, LANES), f32),
-            pltpu.VMEM((sensors, sub_rows, 8, LANES), f32),
-            pltpu.VMEM((sensors, sub_rows, block, width), bf16),
-            pltpu.VMEM(msk.shape, msk.dtype),
-            pltpu.VMEM(slope_to_modes.shape, bf16),
-        ),
-        in_specs=[HBM] * 4,
-        out_specs=(VMEM,) * 7,
-        scratch_shapes=[
-            pltpu.VMEM((2, 2, depth, LANES), bf16),
             pltpu.VMEM(off.shape, off.dtype),
-            pltpu.SemaphoreType.DMA((sensors, sub_rows)),
-            pltpu.SemaphoreType.DMA((3,)),
+            pltpu.SemaphoreType.DMA((sensors, 2)),
+            pltpu.SemaphoreType.DMA,
         ],
         compiler_params=params,
-        cost_estimate=cost(2 * sensors),
-        name="edge_moments",
-    )(x, off, msk, slope_to_modes)
+        cost_estimate=cost(2),
+        name="halo_moments",
+    )(x, off)
     onward = [(i, i + 1) for i in range(tiles - 1)]
     backward = [(j, i) for i, j in onward]
     from_before = lax.ppermute(up, "tile", onward)
     from_after = lax.ppermute(down, "tile", backward)
     partial_modes, edge, edge_mask, count = pl.pallas_call(
-        functools.partial(kernel_inner, sub_rows, sub_cols, frames),
+        functools.partial(kernel_moments, sub_rows, sub_cols, frames),
         out_shape=(
             pltpu.VMEM((frames, modes), f32),
             pltpu.VMEM((2, 2, 2, frames, LANES), f32),
             pltpu.VMEM((2, 2, frames, LANES), f32),
             pltpu.VMEM((frames, LANES), f32),
         ),
-        in_specs=[VMEM] * 5,
+        in_specs=[VMEM] * 4,
         out_specs=(VMEM,) * 4,
         scratch_shapes=[
-            pltpu.VMEM((inner, 2, depth, LANES), bf16),
-            pltpu.VMEM((sensors, inner, 2, 2, frames, LANES), f32),
+            pltpu.VMEM((sub_rows, 2, depth, LANES), bf16),
+            pltpu.VMEM((sensors, sub_rows, 2, 2, frames, LANES), f32),
         ],
         compiler_params=params,
-        cost_estimate=cost(inner * sensors),
-        name="inner_moments",
-    )(buf, geo, parts, mask_v, modes_v)
+        cost_estimate=cost(sensors * sub_rows),
+        name="moments",
+    )(pixels_v, geo, mask_v, modes_v)
     gain = mode_gain.reshape(1, modes)
     packed = -(-(frames * share // LANES + 1) // 8) * 8
     payload = pl.pallas_call(

time: 34.2 us -> 34.5 us (level)
  Pallas kernels: 11.6 us -> 9.6 us
  local copies, waits for them, and re-layouts: 0.01 us -> 2 us
  waiting for transfers between devices: 0.44 us -> 0.01 us
  blocking collectives: 14.3 us -> 14.7 us
    pallas_call x2, Pallas kernels: 10.1 us -> 8.04 us  [the longest x1 5.11 us: body(): pl.pallas_call(functools.partial(kernel_moments, sub_rows, sub_cols, fram...]
    unnamed x4 -> x10, local copies, waits for them, and re-layouts: 0.01 us -> 2 us
    ppermute x1, waiting for transfers between devices: 0.44 us -> 0.01 us  [body(): from_after = lax.ppermute(down, 'tile', backward)]
    all_to_all x1, blocking collectives: 14.3 us -> 14.7 us  [body(): info = lax.all_to_all(payload, ('tile', 'tm'), 0, 0)]
  transfers between devices with their start and end apart: 2 -> 2, of which waited for: 1 -> 0; matrix products, arithmetic and copies ran while one was open for 0% -> 0% of each run, Pallas kernels for 10% -> 15%
where the time goes in v6:
time: 34.5 us; the launch traced here: 34.2 us
  blocking collectives  14.7 us (43%)
  Pallas kernels  9.6 us (28%)
  starting transfers between devices  6.49 us (19%)
  local copies, waits for them, and re-layouts  2 us (6%)
  between operations  1.39 us (4%)
    all_to_all x1, blocking collectives, body(): info = lax.all_to_all(payload, ('tile', 'tm'), 0, 0)  14.7 us
    ppermute x1, starting transfers between devices, body(): from_before = lax.ppermute(up, 'tile', onward)  5.19 us
    pallas_call x1, Pallas kernels, body(): pl.pallas_call(functools.partial(kernel_moments, sub_rows, sub_cols, fram...  5.11 us
    pallas_call x1, Pallas kernels, body(): pl.pallas_call(functools.partial(kernel_halo, sub_rows, sub_cols, frames)...  2.93 us
    unnamed x10, local copies, waits for them, and re-layouts  2 us
    ppermute x1, starting transfers between devices, body(): from_after = lax.ppermute(down, 'tile', backward)  1.29 us
    pallas_call x1, Pallas kernels, body(): pl.pallas_call(functools.partial(kernel_smooth, tiles, blocks, frames, fl...  1.19 us
  transfers between devices with their start and end apart: 2, of which 0 were waited for; matrix products, arithmetic and copies ran while one was open for 0% of the time, Pallas kernels for 15%

profile of v6, /device:TPU:0, one launch (start us, length us, event | category | flops | bytes accessed | tf_op | source)
XLA Modules:
  0.0 34.2 jit_solution(615083776920360814)
XLA Ops:
  0.6 0.0 copy-start
  0.6 0.0 copy-start.3
  0.7 0.0 copy-start.4
  0.7 2.9 %halo_moments.1 = (f32[3,24,128]{2,1,0:T(8,128)S(1)}, f32[3,24,128]{2,1,0:T(8,128)S(1)}, f32[3,5,8,128]{3,2,1,0:T(8,128)S(1)}) custom-call(bf16[3,2400,800]{2,1,0:T(8,128)(2,1)} %bitcast.7, s32[3,20,2,40]{3,2,1,0:T(2,128)} %bitcast.13), custom_call_target="tpu_custom_call" | custom-call | flops 393216000 | bytes 1536000 | tf_op jit(solution)/shard_map/halo_moments/pallas_call | solution.py:429
  3.6 5.2 %collective-permute-start = (f32[3,24,128]{2,1,0:T(8,128)S(1)}, f32[3,24,128]{2,1,0:T(8,128)S(1)}, u32[]{:S(2)}, u32[]{:S(2)}) collective-permute-start(f32[3,24,128]{2,1,0:T(8,128)S(1)} %get-tuple-element.9), channel_id=1, source_target_pairs={{0,4},{4,8},{8,12},{1,5},{5,9},{9,13},{2,6},{6,10},{10,14},{3,7},{... | collective-permute-start | bytes 110600 | tf_op jit(solution)/shard_map/ppermute | solution.py:452
  8.8 1.3 %collective-permute-start.1 = (f32[3,24,128]{2,1,0:T(8,128)S(1)}, f32[3,24,128]{2,1,0:T(8,128)S(1)}, u32[]{:S(2)}, u32[]{:S(2)}) collective-permute-start(f32[3,24,128]{2,1,0:T(8,128)S(1)} %get-tuple-element.10), channel_id=1, source_target_pairs={{4,0},{8,4},{12,8},{5,1},{9,5},{13,9},{6,2},{10,6},{14,10},{7,3},{... | collective-permute-start | bytes 110600 | tf_op jit(solution)/shard_map/ppermute | solution.py:453
  10.1 0.0 copy-done
  10.1 0.0 copy-start.1
  10.1 1.1 %copy-done.1 = bf16[2,3,5,40,256]{4,3,2,1,0:T(8,128)(2,1)S(1)} copy-done((bf16[2,3,5,40,256]{4,3,2,1,0:T(8,128)(2,1)S(1)}, bf16[2,3,5,40,256]{4,3,2,1,0:T(8,128)(2,1)}, u32[]{:S(2)}) %copy-start.1) | copy-done | bytes 614424
  11.2 0.0 copy-start.2
  11.2 0.9 %copy-done.2 = s32[3,24,5,40]{3,1,2,0:T(8,128)S(1)} copy-done((s32[3,24,5,40]{3,1,2,0:T(8,128)S(1)}, s32[3,24,5,40]{3,1,2,0:T(8,128)}, u32[]{:S(2)}) %copy-start.2) | copy-done | bytes 57624
  12.1 5.1 %moments.1 = (f32[24,256]{1,0:T(8,128)S(1)}, f32[2,2,2,24,128]{4,3,2,1,0:T(8,128)S(1)}, f32[2,2,24,128]{3,2,1,0:T(8,128)S(1)}, f32[24,128]{1,0:T(8,128)S(1)}) custom-call(bf16[3,2400,800]{2,1,0:T(8,128)(2,1)S(1)} %bitcast.8, f32[3,5,8,128]{3,2,1,0:T(8,128)S(1)} %get-tuple-element.11.geo_ref, s32[3,5,24,40]{3,2,1,0:T(8,128)S(1)} %bitcast.9, ...), custom_call_target="tpu_custom_call" | custom-call | flops 2949120000 | bytes 11520000 | tf_op jit(solution)/shard_map/moments/pallas_call | solution.py:454
  17.9 0.0 collective-permute-done.before_ref
  17.9 0.0 collective-permute-done.1.after_ref
  17.9 0.0 copy-done.3
  17.9 0.4 %join_halo.1 = f32[16,16,128]{2,1,0:T(8,128)S(1)} custom-call(s32[1]{0:T(128)S(6)} %copy.9.live_ref, f32[3,24,128]{2,1,0:T(8,128)S(1)} %collective-permute-done.before_ref, f32[3,24,128]{2,1,0:T(8,128)S(1)} %collective-permute-done.1.after_ref, f32[24,256]{1,0:T(8,128)S(1)} %get-tuple-element.12.pm_ref, ...), custom_call_target="tpu_custom_call" | custom-call | tf_op jit(solution)/shard_map/join_halo/pallas_call | solution.py:474
  18.3 14.7 %all_to_all.5.in_ref = f32[16,16,128]{2,1,0:T(8,128)S(1)} all-to-all(f32[16,16,128]{2,1,0:T(8,128)S(1)} %join_halo.1), channel_id=1, replica_groups=mesh['grp'=2,'tile'=4,'tm'=4] {'tile','tm'}, dimensions={0} | all-to-all | bytes 262144 | tf_op jit(solution)/shard_map/all_to_all | solution.py:482
  33.0 0.0 copy-done.4
  33.0 1.2 %smooth.1 = (f32[24,64]{1,0:T(8,128)}, f32[24,64]{1,0:T(8,128)}) custom-call(f32[16,16,128]{2,1,0:T(8,128)S(1)} %all_to_all.5.in_ref, f32[1,256]{1,0:T(1,128)S(1)} %bitcast.12, f32[1,256]{1,0:T(1,128)S(1)} %bitcast.11), custom_call_target="tpu_custom_call" | custom-call | tf_op jit(solution)/shard_map/smooth/pallas_call | solution.py:483
Async XLA Ops:
  0.6 9.5 %copy-start = (bf16[3,24,100,800]{3,1,2,0:T(8,128)(2,1)S(1)}, bf16[3,24,100,800]{3,1,2,0:T(8,128)(2,1)}, u32[]{:S(2)}) copy-start(bf16[3,24,100,800]{3,1,2,0:T(8,128)(2,1)} %param.7) | copy-start | bytes 34560004
  0.6 17.3 %copy-start.3 = (f32[256]{0:T(256)S(1)}, f32[256]{0:T(256)}, u32[]{:S(2)}) copy-start(f32[256]{0:T(256)} %param.13) | copy-start | bytes 3076
  0.7 32.4 %copy-start.4 = (f32[256]{0:T(256)S(1)}, f32[256]{0:T(256)}, u32[]{:S(2)}) copy-start(f32[256]{0:T(256)} %param.12) | copy-start | bytes 3076
  3.6 14.3 %collective-permute-start = (f32[3,24,128]{2,1,0:T(8,128)S(1)}, f32[3,24,128]{2,1,0:T(8,128)S(1)}, u32[]{:S(2)}, u32[]{:S(2)}) collective-permute-start(f32[3,24,128]{2,1,0:T(8,128)S(1)} %get-tuple-element.9), channel_id=1, source_target_pairs={{0,4},{4,8},{8,12},{1,5},{5,9},{9,13},{2,6},{6,10},{10,14},{3,7},{... | collective-permute-start | bytes 110600 | tf_op jit(solution)/shard_map/ppermute | solution.py:452
  8.8 9.1 %collective-permute-start.1 = (f32[3,24,128]{2,1,0:T(8,128)S(1)}, f32[3,24,128]{2,1,0:T(8,128)S(1)}, u32[]{:S(2)}, u32[]{:S(2)}) collective-permute-start(f32[3,24,128]{2,1,0:T(8,128)S(1)} %get-tuple-element.10), channel_id=1, source_target_pairs={{4,0},{8,4},{12,8},{5,1},{9,5},{13,9},{6,2},{10,6},{14,10},{7,3},{... | collective-permute-start | bytes 110600 | tf_op jit(solution)/shard_map/ppermute | solution.py:453
  10.1 1.1 %copy-start.1 = (bf16[2,3,5,40,256]{4,3,2,1,0:T(8,128)(2,1)S(1)}, bf16[2,3,5,40,256]{4,3,2,1,0:T(8,128)(2,1)}, u32[]{:S(2)}) copy-start(bf16[2,3,5,40,256]{4,3,2,1,0:T(8,128)(2,1)} %modes_ref.3) | copy-start | bytes 1843204
  11.2 0.9 %copy-start.2 = (s32[3,24,5,40]{3,1,2,0:T(8,128)S(1)}, s32[3,24,5,40]{3,1,2,0:T(8,128)}, u32[]{:S(2)}) copy-start(s32[3,24,5,40]{3,1,2,0:T(8,128)} %param.9) | copy-start | bytes 172804

commit v7 on v6

--- a/solution.py
+++ b/solution.py
@@ -130,8 +130,9 @@
 
 
 def kernel_halo(
-    sub_rows, sub_cols, frames, x_hbm, off_hbm, up_ref, down_ref, geo_ref,
-    buf, w_ref, p_ref, off_ref, sem, off_sem,
+    sub_rows, sub_cols, frames, x_hbm, off_hbm, mask_hbm, modes_hbm,
+    up_ref, down_ref, geo_ref, w_ref, mask_ref, modes_ref,
+    buf, p_ref, off_ref, sem, side_sem,
 ):
     sensors, lines, width = x_hbm.shape
     reach = SHIFT * frames
@@ -143,11 +144,15 @@
             x_hbm.at[s, pl.ds(e * (lines - reach), reach)], buf.at[s, e], sem.at[s, e]
         )
 
-    off_copy = pltpu.make_async_copy(off_hbm, off_ref, off_sem)
+    off_copy = pltpu.make_async_copy(off_hbm, off_ref, side_sem.at[0])
+    mask_copy = pltpu.make_async_copy(mask_hbm, mask_ref, side_sem.at[1])
+    modes_copy = pltpu.make_async_copy(modes_hbm, modes_ref, side_sem.at[2])
     off_copy.start()
     for s in range(sensors):
         for e in range(2):
             copy(s, e).start()
+    mask_copy.start()
+    modes_copy.start()
     off_copy.wait()
     geometry(geo_ref, off_ref, sensors, sub_rows, sub_cols, width)
     for s in range(sensors):
@@ -178,6 +183,8 @@
             ref[h] = both[0]
             pair.append(both[1])
         ref[2] = jnp.where(left, pair[0], pltpu.roll(pair[1], HALF, axis=1))
+    mask_copy.wait()
+    modes_copy.wait()
 
 
 def slope_terms(plain, lines, mask):
@@ -205,7 +212,7 @@
 
 
 def kernel_moments(
-    sub_rows, sub_cols, frames, x_ref, geo_ref, mask_ref, modes_ref,
+    sub_rows, sub_cols, frames, x_ref, geo_ref, edge_w_ref, mask_ref, modes_ref,
     pm_ref, edge_ref, em_ref, count_ref, w_ref, p_ref,
 ):
     sensors = x_ref.shape[0]
@@ -214,11 +221,12 @@
     cols = sub_cols // 2
 
     def step(s, carry):
+        for i in range(1, last):
+            block_weights(geo_ref.at[s, i], w_ref.at[i - 1])
         for i in range(sub_rows):
-            block_weights(geo_ref.at[s, i], w_ref.at[i])
-        for i in range(sub_rows):
+            weights = edge_w_ref.at[s, i // last] if i in (0, last) else w_ref.at[i - 1]
             out = block_moments(
-                x_ref.at[s, i * block : (i + 1) * block], geo_ref.at[s, i], w_ref.at[i], sub_cols, frames
+                x_ref.at[s, i * block : (i + 1) * block], geo_ref.at[s, i], weights, sub_cols, frames
             )
             for h in range(2):
                 for a in range(2):
@@ -413,10 +421,10 @@
     x = jnp.transpose(pixels, (0, 2, 1, 3)).reshape(sensors, lines * frames, width)
     off = jnp.transpose(offsets, (0, 1, 3, 2))
     msk = jnp.transpose(mask, (0, 2, 1, 3))
-    pixels_v, mask_v, modes_v = (
-        pltpu.with_memory_space_constraint(v, pltpu.VMEM) for v in (x, msk, slope_to_modes)
+    pixels_v = pltpu.with_memory_space_constraint(x, pltpu.VMEM)
+    x, off, msk, slope_to_modes = (
+        pltpu.with_memory_space_constraint(v, pltpu.HBM) for v in (x, off, msk, slope_to_modes)
     )
-    x, off = (pltpu.with_memory_space_constraint(v, pltpu.HBM) for v in (x, off))
     block = SIDE * frames
     depth = max(half_columns(h, sub_cols, width)[1] for h in range(2))
     params = pltpu.CompilerParams(vmem_limit_bytes=VMEM_LIMIT)
@@ -426,27 +434,29 @@
             flops=2 * chunks * block * width * 256, bytes_accessed=chunks * block * width * 2, transcendentals=0
         )
 
-    up, down, geo = pl.pallas_call(
+    up, down, geo, edge_weights, mask_v, modes_v = pl.pallas_call(
         functools.partial(kernel_halo, sub_rows, sub_cols, frames),
         out_shape=(
             jax.ShapeDtypeStruct((3, frames, LANES), f32),
             jax.ShapeDtypeStruct((3, frames, LANES), f32),
             pltpu.VMEM((sensors, sub_rows, 8, LANES), f32),
+            pltpu.VMEM((sensors, 2, 2, depth, LANES), bf16),
+            pltpu.VMEM(msk.shape, msk.dtype),
+            pltpu.VMEM(slope_to_modes.shape, bf16),
         ),
-        in_specs=[HBM] * 2,
-        out_specs=(VMEM,) * 3,
+        in_specs=[HBM] * 4,
+        out_specs=(VMEM,) * 6,
         scratch_shapes=[
             pltpu.VMEM((sensors, 2, SHIFT * frames, width), bf16),
-            pltpu.VMEM((sensors, 2, 2, depth, LANES), bf16),
             pltpu.VMEM((sensors, 2, 2, 2, frames, LANES), f32),
             pltpu.VMEM(off.shape, off.dtype),
             pltpu.SemaphoreType.DMA((sensors, 2)),
-            pltpu.SemaphoreType.DMA,
+            pltpu.SemaphoreType.DMA((3,)),
         ],
         compiler_params=params,
         cost_estimate=cost(2),
         name="halo_moments",
-    )(x, off)
+    )(x, off, msk, slope_to_modes)
     onward = [(i, i + 1) for i in range(tiles - 1)]
     backward = [(j, i) for i, j in onward]
     from_before = lax.ppermute(up, "tile", onward)
@@ -459,16 +469,16 @@
             pltpu.VMEM((2, 2, frames, LANES), f32),
             pltpu.VMEM((frames, LANES), f32),
         ),
-        in_specs=[VMEM] * 4,
+        in_specs=[VMEM] * 5,
         out_specs=(VMEM,) * 4,
         scratch_shapes=[
-            pltpu.VMEM((sub_rows, 2, depth, LANES), bf16),
+            pltpu.VMEM((sub_rows - 2, 2, depth, LANES), bf16),
             pltpu.VMEM((sensors, sub_rows, 2, 2, frames, LANES), f32),
         ],
         compiler_params=params,
         cost_estimate=cost(sensors * sub_rows),
         name="moments",
-    )(pixels_v, geo, mask_v, modes_v)
+    )(pixels_v, geo, edge_weights, mask_v, modes_v)
     gain = mode_gain.reshape(1, modes)
     packed = -(-(frames * share // LANES + 1) // 8) * 8
     payload = pl.pallas_call(

time: 34.5 us -> 32.1 us (0.930)
  local copies, waits for them, and re-layouts: 2 us -> 0.01 us
    unnamed x10 -> x6, local copies, waits for them, and re-layouts: 2 us -> 0.01 us
where the time goes in v7:
time: 32.1 us; the launch traced here: 31.9 us
  blocking collectives  14.7 us (46%)
  Pallas kernels  9.29 us (29%)
  starting transfers between devices  6.49 us (20%)
  between operations  1.38 us (4%)
    all_to_all x1, blocking collectives, body(): info = lax.all_to_all(payload, ('tile', 'tm'), 0, 0)  14.7 us
    ppermute x1, starting transfers between devices, body(): from_before = lax.ppermute(up, 'tile', onward)  5.19 us
    pallas_call x1, Pallas kernels, body(): pl.pallas_call(functools.partial(kernel_moments, sub_rows, sub_cols, fram...  4.91 us
    pallas_call x1, Pallas kernels, body(): pl.pallas_call(functools.partial(kernel_halo, sub_rows, sub_cols, frames)...  2.81 us
    ppermute x1, starting transfers between devices, body(): from_after = lax.ppermute(down, 'tile', backward)  1.29 us
    pallas_call x1, Pallas kernels, body(): pl.pallas_call(functools.partial(kernel_smooth, tiles, blocks, frames, fl...  1.19 us
  transfers between devices with their start and end apart: 2, of which 0 were waited for; matrix products, arithmetic and copies ran while one was open for 0% of the time, Pallas kernels for 15%

profile of v7, /device:TPU:0, one launch (start us, length us, event | category | flops | bytes accessed | tf_op | source)
XLA Modules:
  0.0 31.9 jit_solution(7030965636449957615)
XLA Ops:
  0.6 0.0 copy-start
  0.6 0.0 copy-start.1
  0.7 0.0 copy-start.2
  0.7 2.8 %halo_moments.1 = (f32[3,24,128]{2,1,0:T(8,128)S(1)}, f32[3,24,128]{2,1,0:T(8,128)S(1)}, f32[3,5,8,128]{3,2,1,0:T(8,128)S(1)}, bf16[3,2,2,416,128]{4,3,2,1,0:T(8...) custom-call(bf16[3,2400,800]{2,1,0:T(8,128)(2,1)} %bitcast.7, ...), custom_call_target="tpu_custom_call" | custom-call | flops 393216000 | bytes 1536000 | tf_op jit(solution)/shard_map/halo_moments/pallas_call | solution.py:437
  3.5 5.2 %collective-permute-start = (f32[3,24,128]{2,1,0:T(8,128)S(1)}, f32[3,24,128]{2,1,0:T(8,128)S(1)}, u32[]{:S(2)}, u32[]{:S(2)}) collective-permute-start(f32[3,24,128]{2,1,0:T(8,128)S(1)} %get-tuple-element.12), channel_id=1, source_target_pairs={{0,4},{4,8},{8,12},{1,5},{5,9},{9,13},{2,6},{6,10},{10,14},{3,7},{... | collective-permute-start | bytes 110600 | tf_op jit(solution)/shard_map/ppermute | solution.py:462
  8.7 1.3 %collective-permute-start.1 = (f32[3,24,128]{2,1,0:T(8,128)S(1)}, f32[3,24,128]{2,1,0:T(8,128)S(1)}, u32[]{:S(2)}, u32[]{:S(2)}) collective-permute-start(f32[3,24,128]{2,1,0:T(8,128)S(1)} %get-tuple-element.13), channel_id=1, source_target_pairs={{4,0},{8,4},{12,8},{5,1},{9,5},{13,9},{6,2},{10,6},{14,10},{7,3},{... | collective-permute-start | bytes 110600 | tf_op jit(solution)/shard_map/ppermute | solution.py:463
  10.0 0.0 copy-done
  10.0 4.9 %moments.1 = (f32[24,256]{1,0:T(8,128)S(1)}, f32[2,2,2,24,128]{4,3,2,1,0:T(8,128)S(1)}, f32[2,2,24,128]{3,2,1,0:T(8,128)S(1)}, f32[24,128]{1,0:T(8,128)S(1)}) custom-call(bf16[3,2400,800]{2,1,0:T(8,128)(2,1)S(1)} %bitcast.8, f32[3,5,8,128]{3,2,1,0:T(8,128)S(1)} %get-tuple-element.14.geo_ref, bf16[3,2,2,416,128]{4,3,2,1,0:T(8,128)(2,1)S(1)} %get-tuple-element.15.edge_w_ref, ...), custom_call_target="tpu_custom_call" | custom-call | flops 2949120000 | bytes 11520000 | tf_op jit(solution)/shard_map/moments/pallas_call | solution.py:464
  15.6 0.0 collective-permute-done.before_ref
  15.6 0.0 collective-permute-done.1.after_ref
  15.6 0.0 copy-done.1
  15.6 0.4 %join_halo.1 = f32[16,16,128]{2,1,0:T(8,128)S(1)} custom-call(s32[1]{0:T(128)S(6)} %copy.9.live_ref, f32[3,24,128]{2,1,0:T(8,128)S(1)} %collective-permute-done.before_ref, f32[3,24,128]{2,1,0:T(8,128)S(1)} %collective-permute-done.1.after_ref, f32[24,256]{1,0:T(8,128)S(1)} %get-tuple-element.18.pm_ref, ...), custom_call_target="tpu_custom_call" | custom-call | tf_op jit(solution)/shard_map/join_halo/pallas_call | solution.py:484
  16.0 14.7 %all_to_all.5.in_ref = f32[16,16,128]{2,1,0:T(8,128)S(1)} all-to-all(f32[16,16,128]{2,1,0:T(8,128)S(1)} %join_halo.1), channel_id=1, replica_groups=mesh['grp'=2,'tile'=4,'tm'=4] {'tile','tm'}, dimensions={0} | all-to-all | bytes 262144 | tf_op jit(solution)/shard_map/all_to_all | solution.py:492
  30.7 0.0 copy-done.2
  30.7 1.2 %smooth.1 = (f32[24,64]{1,0:T(8,128)}, f32[24,64]{1,0:T(8,128)}) custom-call(f32[16,16,128]{2,1,0:T(8,128)S(1)} %all_to_all.5.in_ref, f32[1,256]{1,0:T(1,128)S(1)} %bitcast.11, f32[1,256]{1,0:T(1,128)S(1)} %bitcast.10), custom_call_target="tpu_custom_call" | custom-call | tf_op jit(solution)/shard_map/smooth/pallas_call | solution.py:493
Async XLA Ops:
  0.6 9.4 %copy-start = (bf16[3,24,100,800]{3,1,2,0:T(8,128)(2,1)S(1)}, bf16[3,24,100,800]{3,1,2,0:T(8,128)(2,1)}, u32[]{:S(2)}) copy-start(bf16[3,24,100,800]{3,1,2,0:T(8,128)(2,1)} %param.7) | copy-start | bytes 34560004
  0.6 14.9 %copy-start.1 = (f32[256]{0:T(256)S(1)}, f32[256]{0:T(256)}, u32[]{:S(2)}) copy-start(f32[256]{0:T(256)} %param.13) | copy-start | bytes 3076
  0.7 30.1 %copy-start.2 = (f32[256]{0:T(256)S(1)}, f32[256]{0:T(256)}, u32[]{:S(2)}) copy-start(f32[256]{0:T(256)} %param.12) | copy-start | bytes 3076
  3.5 12.1 %collective-permute-start = (f32[3,24,128]{2,1,0:T(8,128)S(1)}, f32[3,24,128]{2,1,0:T(8,128)S(1)}, u32[]{:S(2)}, u32[]{:S(2)}) collective-permute-start(f32[3,24,128]{2,1,0:T(8,128)S(1)} %get-tuple-element.12), channel_id=1, source_target_pairs={{0,4},{4,8},{8,12},{1,5},{5,9},{9,13},{2,6},{6,10},{10,14},{3,7},{... | collective-permute-start | bytes 110600 | tf_op jit(solution)/shard_map/ppermute | solution.py:462
  8.7 6.9 %collective-permute-start.1 = (f32[3,24,128]{2,1,0:T(8,128)S(1)}, f32[3,24,128]{2,1,0:T(8,128)S(1)}, u32[]{:S(2)}, u32[]{:S(2)}) collective-permute-start(f32[3,24,128]{2,1,0:T(8,128)S(1)} %get-tuple-element.13), channel_id=1, source_target_pairs={{4,0},{8,4},{12,8},{5,1},{9,5},{13,9},{6,2},{10,6},{14,10},{7,3},{... | collective-permute-start | bytes 110600 | tf_op jit(solution)/shard_map/ppermute | solution.py:463

commit v8 on v7

--- a/solution.py
+++ b/solution.py
@@ -12,6 +12,7 @@
 CENTRE = (SIDE - 1) / 2.0
 LANES = 128
 HALF = LANES // 2
+TILE = 2 * LANES
 VMEM_LIMIT = 24 * 1024 * 1024
 VMEM = pl.BlockSpec(memory_space=pltpu.VMEM)
 HBM = pl.BlockSpec(memory_space=pl.ANY)
@@ -48,8 +49,8 @@
 
 def side_by_side(pieces):
     rows, cols = pieces[0].shape
-    pad = jnp.zeros((rows, HALF - 3 * cols), pieces[0].dtype)
-    return jnp.concatenate([*pieces, pad, *pieces, pad], axis=1)
+    group = jnp.concatenate([*pieces, jnp.zeros((rows, HALF - 3 * cols), pieces[0].dtype)], axis=1)
+    return jnp.concatenate([group, group], axis=1)
 
 
 def rotate(x, slots, cols):
@@ -61,7 +62,7 @@
     return jnp.where(half_lane() >= shift, near, far)
 
 
-def geometry(geo_ref, off_ref, sensors, sub_rows, sub_cols, width):
+def geometry(geo_ref, off_ref, table_ref, spread_ref, sensors, sub_rows, sub_cols, width):
     cols = sub_cols // 2
     lane = half_lane()
     index = lane - cols * (lane >= cols).astype(jnp.int32)
@@ -70,11 +71,14 @@
     tile = lax.axis_index("tile")
     total_rows = off_ref.shape[1]
     for s in range(sensors):
-        spread_rows = []
         for k in range(-1, sub_rows + 1):
             row = jnp.clip(tile * sub_rows + k, 0, total_rows - 1)
-            v = off_ref[s, row].astype(jnp.float32)
-            spread_rows.append([side_by_side([v[:, h * cols : (h + 1) * cols]] * 3) for h in range(2)])
+            n = 2 * (s * (sub_rows + 2) + k + 1)
+            table_ref[n : n + 2, :] = off_ref[s, row].astype(jnp.float32)
+    table = table_ref[...]
+    for h in range(2):
+        spread_ref[h] = side_by_side([table[:, h * cols : (h + 1) * cols]] * 3)
+    for s in range(sensors):
         for i in range(sub_rows):
             for h in range(2):
                 first, _ = half_columns(h, sub_cols, width)
@@ -83,56 +87,85 @@
                 rs = [None] * 3
                 for k in (i - 1, i, i + 1):
                     q = slot_of(k, s)
-                    v = spread_rows[k + 1][h]
-                    cs[q] = v[1:2] + col_base
-                    rs[q] = v[0:1] + (SIDE * (k - i) + CENTRE)
-                geo_ref[s, i, 2 * h : 2 * h + 1, :] = jnp.where(used, by_slot(cs, cols), -1000.0)
+                    n = 2 * (s * (sub_rows + 2) + k + 1)
+                    cs[q] = spread_ref[h, n + 1 : n + 2, :]
+                    rs[q] = spread_ref[h, n : n + 1, :] + (SIDE * (k - i) + CENTRE)
+                geo_ref[s, i, 2 * h : 2 * h + 1, :] = jnp.where(used, by_slot(cs, cols) + col_base, -1000.0)
                 geo_ref[s, i, 2 * h + 1 : 2 * h + 2, :] = jnp.where(used, by_slot(rs, cols), -1000.0)
 
 
-def build_weights(col_pos, w_ref):
+def window_weights(col_pos, first, count):
     base = lax.broadcasted_iota(jnp.int32, (16, LANES), 0).astype(jnp.float32) - col_pos
     left = lane_iota(16) < HALF
-    for t in range(w_ref.shape[0] // 16):
+    for t in range(count // 16):
         d = base + float(16 * t)
         value = jnp.where(left, 1.0, d)
-        w_ref[16 * t : 16 * t + 16, :] = jnp.where(jnp.abs(d) < 10.0, value, 0.0).astype(jnp.bfloat16)
-
-
-def row_sums(row_pos, r, frames, first_row=0):
-    plain = jnp.zeros((frames, LANES), jnp.float32)
-    lines = jnp.zeros((frames, LANES), jnp.float32)
-    for y in range(r.shape[0] // frames):
-        d = float(y + first_row) - row_pos
-        inside = jnp.abs(d) < 10.0
-        one = jnp.where(inside, 1.0, 0.0)
-        centred = jnp.where(inside, d, 0.0)
-        piece = r[y * frames : (y + 1) * frames, :]
-        plain = plain + one * piece
-        lines = lines + centred * piece
-    return plain, lines
-
-
-def block_weights(geo_ref, w_ref):
+        yield first + 16 * t, jnp.where(jnp.abs(d) < 10.0, value, 0.0).astype(jnp.bfloat16)
+
+
+def clear_weights(wide_ref, rest):
+    zero = jnp.zeros((16, LANES), jnp.bfloat16)
+    for n in range(wide_ref.shape[0]):
+        for t in range(0, TILE, 16):
+            wide_ref[n, t : t + 16, 0:LANES] = zero
+            wide_ref[n, t : t + 16, LANES:] = zero
+        for t in range(0, rest, 16):
+            wide_ref[n, TILE + t : TILE + t + 16, LANES:] = zero
+            wide_ref[n, TILE + rest + t : TILE + rest + t + 16, 0:LANES] = zero
+
+
+def block_weights(geo_ref, narrow_ref, wide_ref, sub_cols, width):
+    rest = width - 3 * TILE
     for h in range(2):
-        build_weights(geo_ref[2 * h : 2 * h + 1, :], w_ref.at[h])
-
-
-def block_moments(pixels, geo_ref, w_ref, sub_cols, frames, first_row=0):
-    out = []
-    for h in range(2):
-        first, size = half_columns(h, sub_cols, pixels.shape[1])
-        r = jnp.dot(
-            pixels[:, first : first + size], w_ref[h, 0:size, :], preferred_element_type=jnp.float32
-        )
-        out.append(row_sums(geo_ref[2 * h + 1 : 2 * h + 2, :], r, frames, first_row))
+        first, count = half_columns(h, sub_cols, width)
+        lanes = slice(h * LANES, (h + 1) * LANES)
+        for c, piece in window_weights(geo_ref[2 * h : 2 * h + 1, :], first, count):
+            if c < TILE:
+                narrow_ref[0, c : c + 16, :] = piece
+            elif c < 2 * TILE:
+                wide_ref[c - TILE : c - TILE + 16, lanes] = piece
+            elif c < 3 * TILE:
+                narrow_ref[1, c - 2 * TILE : c - 2 * TILE + 16, :] = piece
+            else:
+                at = c - 2 * TILE
+                wide_ref[at : at + 16, 0:LANES] = piece
+                wide_ref[at + rest : at + rest + 16, LANES:] = piece
+
+
+def block_moments(pixels, geo_ref, narrow_ref, wide_ref, frames, first_row=0):
+    f32 = jnp.float32
+    rows, width = pixels.shape
+    rest = width - 3 * TILE
+    a = jnp.dot(pixels[:, 0:TILE], narrow_ref[0], preferred_element_type=f32)
+    m = jnp.dot(pixels[:, TILE : 2 * TILE], wide_ref[0:TILE, :], preferred_element_type=f32)
+    b = jnp.dot(pixels[:, 2 * TILE : 3 * TILE], narrow_ref[1], preferred_element_type=f32)
+    split = rows // 2 if (rows // 2) % 16 == 0 else rows
+    tail = pixels[0:split, 3 * TILE :]
+    if split < rows:
+        tail = jnp.concatenate([tail, pixels[split:, 3 * TILE :]], axis=1)
+        r = jnp.dot(tail, wide_ref[TILE:, :], preferred_element_type=f32)
+    else:
+        r = jnp.dot(tail, wide_ref[TILE : TILE + rest, 0:LANES], preferred_element_type=f32)
+    out = [[jnp.zeros((frames, LANES), f32) for _ in range(2)] for _ in range(2)]
+    for y in range(rows // frames):
+        at = slice(y * frames, (y + 1) * frames)
+        if y * frames < split:
+            extra = r[at, 0:LANES]
+        else:
+            extra = r[y * frames - split : (y + 1) * frames - split, LANES:]
+        pieces = (a[at] + m[at, 0:LANES], m[at, LANES:] + b[at] + extra)
+        for h in range(2):
+            d = float(y + first_row) - geo_ref[2 * h + 1 : 2 * h + 2, :]
+            inside = jnp.abs(d) < 10.0
+            out[h][0] = out[h][0] + jnp.where(inside, 1.0, 0.0) * pieces[h]
+            out[h][1] = out[h][1] + jnp.where(inside, d, 0.0) * pieces[h]
     return out
 
 
 def kernel_halo(
     sub_rows, sub_cols, frames, x_hbm, off_hbm, mask_hbm, modes_hbm,
-    up_ref, down_ref, geo_ref, w_ref, mask_ref, modes_ref,
-    buf, p_ref, off_ref, sem, side_sem,
+    up_ref, down_ref, geo_ref, narrow_ref, wide_ref, mask_ref, modes_ref,
+    buf, p_ref, off_ref, table_ref, spread_ref, sem, side_sem,
 ):
     sensors, lines, width = x_hbm.shape
     reach = SHIFT * frames
@@ -153,11 +186,13 @@
             copy(s, e).start()
     mask_copy.start()
     modes_copy.start()
+    for s in range(sensors):
+        clear_weights(wide_ref.at[s], width - 3 * TILE)
     off_copy.wait()
-    geometry(geo_ref, off_ref, sensors, sub_rows, sub_cols, width)
+    geometry(geo_ref, off_ref, table_ref, spread_ref, sensors, sub_rows, sub_cols, width)
     for s in range(sensors):
         for e in range(2):
-            block_weights(geo_ref.at[s, e * last], w_ref.at[s, e])
+            block_weights(geo_ref.at[s, e * last], narrow_ref.at[s, e], wide_ref.at[s, e], sub_cols, width)
     for s in range(sensors):
         for e in range(2):
             copy(s, e).wait()
@@ -165,7 +200,7 @@
         for e in range(2):
             first_row = e * (SIDE - SHIFT)
             out = block_moments(
-                buf.at[s, e], geo_ref.at[s, e * last], w_ref.at[s, e], sub_cols, frames, first_row
+                buf.at[s, e], geo_ref.at[s, e * last], narrow_ref.at[s, e], wide_ref.at[s, e], frames, first_row
             )
             for h in range(2):
                 for a in range(2):
@@ -212,21 +247,27 @@
 
 
 def kernel_moments(
-    sub_rows, sub_cols, frames, x_ref, geo_ref, edge_w_ref, mask_ref, modes_ref,
-    pm_ref, edge_ref, em_ref, count_ref, w_ref, p_ref,
+    sub_rows, sub_cols, frames, x_ref, geo_ref, edge_narrow_ref, edge_wide_ref, mask_ref, modes_ref,
+    pm_ref, edge_ref, em_ref, count_ref, narrow_ref, wide_ref, p_ref,
 ):
     sensors = x_ref.shape[0]
     block = SIDE * frames
     last = sub_rows - 1
     cols = sub_cols // 2
 
+    width = x_ref.shape[2]
+    clear_weights(wide_ref, width - 3 * TILE)
+
     def step(s, carry):
         for i in range(1, last):
-            block_weights(geo_ref.at[s, i], w_ref.at[i - 1])
+            block_weights(geo_ref.at[s, i], narrow_ref.at[i - 1], wide_ref.at[i - 1], sub_cols, width)
         for i in range(sub_rows):
-            weights = edge_w_ref.at[s, i // last] if i in (0, last) else w_ref.at[i - 1]
+            if i in (0, last):
+                weights = (edge_narrow_ref.at[s, i // last], edge_wide_ref.at[s, i // last])
+            else:
+                weights = (narrow_ref.at[i - 1], wide_ref.at[i - 1])
             out = block_moments(
-                x_ref.at[s, i * block : (i + 1) * block], geo_ref.at[s, i], weights, sub_cols, frames
+                x_ref.at[s, i * block : (i + 1) * block], geo_ref.at[s, i], *weights, frames
             )
             for h in range(2):
                 for a in range(2):
@@ -336,76 +377,113 @@
     return jnp.where(row >= by, pltpu.roll(x, by, axis=0), fill)
 
 
+def filter_join(early, late):
+    a1, b1, c1, e1, j1 = early
+    a, b, c, e, j = late
+    damp = 1.0 / (1.0 + c1 * j)
+    left = a * damp
+    right = a1 * damp
+    return (
+        left * a1,
+        left * (b1 + c1 * e) + b,
+        left * a * c1 + c,
+        right * (e - j * b1) + e1,
+        right * a1 * j + j1,
+    )
+
+
+def smoother_join(late, early):
+    g1, m1, v1 = late
+    g, m, v = early
+    return g * g1, g * m1 + m, g * g * v1 + v
+
+
+def scan_lanes(values, ident, join, back, share):
+    rows = values[0].shape[0]
+    by = 1
+    while by < rows:
+        values = join(tuple(shifted(x, by, i, back) for x, i in zip(values, ident)), values)
+        by *= 2
+    edge = slice(0, 1) if back else slice(rows - 1, rows)
+    ends = tuple(x[edge] for x in values)
+    lane = lane_iota()
+
+    def over(x, groups, i):
+        step = groups * share
+        if back:
+            return jnp.where(lane < LANES - step, pltpu.roll(x, LANES - step, axis=1), i)
+        return jnp.where(lane >= step, pltpu.roll(x, step, axis=1), i)
+
+    groups = 1
+    while groups * share < LANES - share:
+        ends = join(tuple(over(x, groups, i) for x, i in zip(ends, ident)), ends)
+        groups *= 2
+    return join(tuple(over(x, 1, i) for x, i in zip(ends, ident)), values)
+
+
 def kernel_smooth(
     tiles, blocks, frames, total_subaps, in_ref, noise_ref, gain_ref, mean_ref, var_ref, mean_scr, var_scr
 ):
     share = mean_ref.shape[1]
-    total = blocks * frames
     tile = lax.axis_index("tile")
     time = lax.axis_index("tm")
     pack = LANES // share
     rows = frames // pack
+    per_group = blocks // pack
+    lane = lane_iota()
 
     def own_modes(v):
         out = v[:, 0:share]
         for t in range(1, tiles):
             out = jnp.where(tile == t, v[:, t * share : (t + 1) * share], out)
-        return out
+        return jnp.concatenate([out] * pack, axis=1)
 
     q = own_modes(noise_ref[...])
     gain = own_modes(gain_ref[...])
     own = lane_iota(frames) == lax.broadcasted_iota(jnp.int32, (frames, LANES), 0)
-    infos = []
-    counts = []
+    infos = [None] * per_group
+    counts = [None] * per_group
     for b in range(blocks):
         v = in_ref[b]
         for t in range(1, tiles):
             v = v + in_ref[t * blocks + b]
+        group, place = divmod(b, per_group)
+        parts = []
         for g in range(pack):
-            infos.append(v[0:rows, g * share : (g + 1) * share])
-        counts.append(jnp.sum(jnp.where(own, v[rows : rows + 1], 0.0), axis=1, keepdims=True))
+            turn = (group - g) % pack * share
+            parts.append(pltpu.roll(v, turn, axis=1)[0:rows] if turn else v[0:rows])
+        info = jnp.concatenate(parts, axis=0)
+        count = jnp.sum(jnp.where(own, v[rows : rows + 1], 0.0), axis=1, keepdims=True)
+        if group == 0:
+            infos[place] = info
+            counts[place] = jnp.broadcast_to(count, (frames, LANES))
+        else:
+            infos[place] = jnp.where(lane >= group * share, info, infos[place])
+            counts[place] = jnp.where(lane >= group * share, count, counts[place])
     info_mean = jnp.concatenate(infos, axis=0)
     prec = gain * jnp.concatenate(counts, axis=0) / total_subaps
-    row = lax.broadcasted_iota(jnp.int32, (total, 1), 0)
-    first = row == 0
+    length = per_group * frames
+    row = lax.broadcasted_iota(jnp.int32, (length, LANES), 0)
+    wide_lane = lane_iota(length)
+    first = (row == 0) & (wide_lane < share)
+    last = (row == length - 1) & (wide_lane >= LANES - share)
     retain = 1.0 / (1.0 + q * prec)
     a = jnp.where(first, 0.0, retain)
     c = jnp.where(first, 1.0 / (1.0 + prec), q * retain)
-    b = c * info_mean
-    e = a * info_mean
-    j = a * prec
-    by = 1
-    while by < total:
-        a1 = shifted(a, by, 1.0, False)
-        b1 = shifted(b, by, 0.0, False)
-        c1 = shifted(c, by, 0.0, False)
-        e1 = shifted(e, by, 0.0, False)
-        j1 = shifted(j, by, 0.0, False)
-        damp = 1.0 / (1.0 + c1 * j)
-        left = a * damp
-        right = a1 * damp
-        b = left * (b1 + c1 * e) + b
-        c = left * a * c1 + c
-        e, j = right * (e - j * b1) + e1, right * a1 * j + j1
-        a = left * a1
-        by *= 2
-    g = jnp.where(row == total - 1, 0.0, c / (c + q))
-    m = (1.0 - g) * b
-    v = c * (1.0 - g)
-    by = 1
-    while by < total:
-        g1 = shifted(g, by, 1.0, True)
-        m1 = shifted(m, by, 0.0, True)
-        v1 = shifted(v, by, 0.0, True)
-        m = g * m1 + m
-        v = g * g * v1 + v
-        g = g * g1
-        by *= 2
+    _, b, c, _, _ = scan_lanes(
+        (a, c * info_mean, c, a * info_mean, a * prec), (1.0, 0.0, 0.0, 0.0, 0.0), filter_join, False, share
+    )
+    g = jnp.where(last, 0.0, c / (c + q))
+    _, m, v = scan_lanes((g, (1.0 - g) * b, c * (1.0 - g)), (1.0, 0.0, 0.0), smoother_join, True, share)
     mean_scr[...] = m
     var_scr[...] = v
-    start = pl.multiple_of(time * frames, 8)
-    mean_ref[...] = mean_scr[pl.ds(start, frames), :]
-    var_ref[...] = var_scr[pl.ds(start, frames), :]
+    start = pl.multiple_of(time % per_group * frames, 8)
+    for scr, out_ref in ((mean_scr, mean_ref), (var_scr, var_ref)):
+        piece = scr[pl.ds(start, frames), :]
+        out = piece[:, 0:share]
+        for g in range(1, pack):
+            out = jnp.where(time // per_group == g, piece[:, g * share : (g + 1) * share], out)
+        out_ref[...] = out
 
 
 def body(pixels, offsets, mask, frame_count, slope_to_modes, process_noise, mode_gain):
@@ -426,7 +504,9 @@
         pltpu.with_memory_space_constraint(v, pltpu.HBM) for v in (x, off, msk, slope_to_modes)
     )
     block = SIDE * frames
-    depth = max(half_columns(h, sub_cols, width)[1] for h in range(2))
+    narrow = (2, TILE, LANES)
+    wide = (TILE + 2 * (width - 3 * TILE), 2 * LANES)
+    table_rows = -(-2 * sensors * (sub_rows + 2) // 8) * 8
     params = pltpu.CompilerParams(vmem_limit_bytes=VMEM_LIMIT)
 
     def cost(chunks):
@@ -434,22 +514,25 @@
             flops=2 * chunks * block * width * 256, bytes_accessed=chunks * block * width * 2, transcendentals=0
         )
 
-    up, down, geo, edge_weights, mask_v, modes_v = pl.pallas_call(
+    up, down, geo, edge_narrow, edge_wide, mask_v, modes_v = pl.pallas_call(
         functools.partial(kernel_halo, sub_rows, sub_cols, frames),
         out_shape=(
             jax.ShapeDtypeStruct((3, frames, LANES), f32),
             jax.ShapeDtypeStruct((3, frames, LANES), f32),
             pltpu.VMEM((sensors, sub_rows, 8, LANES), f32),
-            pltpu.VMEM((sensors, 2, 2, depth, LANES), bf16),
+            pltpu.VMEM((sensors, 2, *narrow), bf16),
+            pltpu.VMEM((sensors, 2, *wide), bf16),
             pltpu.VMEM(msk.shape, msk.dtype),
             pltpu.VMEM(slope_to_modes.shape, bf16),
         ),
         in_specs=[HBM] * 4,
-        out_specs=(VMEM,) * 6,
+        out_specs=(VMEM,) * 7,
         scratch_shapes=[
             pltpu.VMEM((sensors, 2, SHIFT * frames, width), bf16),
             pltpu.VMEM((sensors, 2, 2, 2, frames, LANES), f32),
             pltpu.VMEM(off.shape, off.dtype),
+            pltpu.VMEM((table_rows, sub_cols), f32),
+            pltpu.VMEM((2, table_rows, LANES), f32),
             pltpu.SemaphoreType.DMA((sensors, 2)),
             pltpu.SemaphoreType.DMA((3,)),
         ],
@@ -469,16 +552,17 @@
             pltpu.VMEM((2, 2, frames, LANES), f32),
             pltpu.VMEM((frames, LANES), f32),
         ),
-        in_specs=[VMEM] * 5,
+        in_specs=[VMEM] * 6,
         out_specs=(VMEM,) * 4,
         scratch_shapes=[
-            pltpu.VMEM((sub_rows - 2, 2, depth, LANES), bf16),
+            pltpu.VMEM((sub_rows - 2, *narrow), bf16),
+            pltpu.VMEM((sub_rows - 2, *wide), bf16),
             pltpu.VMEM((sensors, sub_rows, 2, 2, frames, LANES), f32),
         ],
         compiler_params=params,
         cost_estimate=cost(sensors * sub_rows),
         name="moments",
-    )(pixels_v, geo, edge_weights, mask_v, modes_v)
+    )(pixels_v, geo, edge_narrow, edge_wide, mask_v, modes_v)
     gain = mode_gain.reshape(1, modes)
     packed = -(-(frames * share // LANES + 1) // 8) * 8
     payload = pl.pallas_call(
@@ -499,8 +583,8 @@
         in_specs=[VMEM] * 3,
         out_specs=(VMEM, VMEM),
         scratch_shapes=[
-            pltpu.VMEM((blocks * frames, share), f32),
-            pltpu.VMEM((blocks * frames, share), f32),
+            pltpu.VMEM((blocks * frames * share // LANES, LANES), f32),
+            pltpu.VMEM((blocks * frames * share // LANES, LANES), f32),
         ],
         compiler_params=params,
         name="smooth",

time: 32.1 us -> 32.1 us (level)
  no operation moved by 1% of the time
where the time goes in v8:
time: 32.1 us; the launch traced here: 31.9 us
  blocking collectives  14.7 us (46%)
  Pallas kernels  9.26 us (29%)
  starting transfers between devices  6.49 us (20%)
  between operations  1.38 us (4%)
    all_to_all x1, blocking collectives, body(): info = lax.all_to_all(payload, ('tile', 'tm'), 0, 0)  14.7 us
    ppermute x1, starting transfers between devices, body(): from_before = lax.ppermute(up, 'tile', onward)  5.19 us
    pallas_call x1, Pallas kernels, body(): pl.pallas_call(functools.partial(kernel_moments, sub_rows, sub_cols, fram...  4.73 us
    pallas_call x1, Pallas kernels, body(): pl.pallas_call(functools.partial(kernel_halo, sub_rows, sub_cols, frames)...  2.84 us
    pallas_call x1, Pallas kernels, body(): pl.pallas_call(functools.partial(kernel_smooth, tiles, blocks, frames, fl...  1.31 us
    ppermute x1, starting transfers between devices, body(): from_after = lax.ppermute(down, 'tile', backward)  1.29 us
  transfers between devices with their start and end apart: 2, of which 0 were waited for; matrix products, arithmetic and copies ran while one was open for 0% of the time, Pallas kernels for 15%

profile of v8, /device:TPU:0, one launch (start us, length us, event | category | flops | bytes accessed | tf_op | source)
XLA Modules:
  0.0 31.9 jit_solution(1136209748244175609)
XLA Ops:
  0.6 0.0 copy-start
  0.6 0.0 copy-start.1
  0.7 0.0 copy-start.2
  0.7 2.8 %halo_moments.1 = (f32[3,24,128]{2,1,0:T(8,128)S(1)}, f32[3,24,128]{2,1,0:T(8,128)S(1)}, f32[3,5,8,128]{3,2,1,0:T(8,128)S(1)}, bf16[3,2,2,256,128]{4,3,2,1,0:T(8...) custom-call(bf16[3,2400,800]{2,1,0:T(8,128)(2,1)} %bitcast.7, ...), custom_call_target="tpu_custom_call" | custom-call | flops 393216000 | bytes 1536000 | tf_op jit(solution)/shard_map/halo_moments/pallas_call | solution.py:517
  3.5 5.2 %collective-permute-start = (f32[3,24,128]{2,1,0:T(8,128)S(1)}, f32[3,24,128]{2,1,0:T(8,128)S(1)}, u32[]{:S(2)}, u32[]{:S(2)}) collective-permute-start(f32[3,24,128]{2,1,0:T(8,128)S(1)} %get-tuple-element.13), channel_id=1, source_target_pairs={{0,4},{4,8},{8,12},{1,5},{5,9},{9,13},{2,6},{6,10},{10,14},{3,7},{... | collective-permute-start | bytes 110600 | tf_op jit(solution)/shard_map/ppermute | solution.py:545
  8.7 1.3 %collective-permute-start.1 = (f32[3,24,128]{2,1,0:T(8,128)S(1)}, f32[3,24,128]{2,1,0:T(8,128)S(1)}, u32[]{:S(2)}, u32[]{:S(2)}) collective-permute-start(f32[3,24,128]{2,1,0:T(8,128)S(1)} %get-tuple-element.14), channel_id=1, source_target_pairs={{4,0},{8,4},{12,8},{5,1},{9,5},{13,9},{6,2},{10,6},{14,10},{7,3},{... | collective-permute-start | bytes 110600 | tf_op jit(solution)/shard_map/ppermute | solution.py:546
  10.0 0.0 copy-done
  10.0 4.7 %moments.1 = (f32[24,256]{1,0:T(8,128)S(1)}, f32[2,2,2,24,128]{4,3,2,1,0:T(8,128)S(1)}, f32[2,2,24,128]{3,2,1,0:T(8,128)S(1)}, f32[24,128]{1,0:T(8,128)S(1)}) custom-call(bf16[3,2400,800]{2,1,0:T(8,128)(2,1)S(1)} %bitcast.8, f32[3,5,8,128]{3,2,1,0:T(8,128)S(1)} %get-tuple-element.15.geo_ref, ...), custom_call_target="tpu_custom_call" | custom-call | flops 2949120000 | bytes 11520000 | tf_op jit(solution)/shard_map/moments/pallas_call | solution.py:547
  15.4 0.0 collective-permute-done.before_ref
  15.4 0.0 collective-permute-done.1.after_ref
  15.4 0.0 copy-done.1
  15.4 0.4 %join_halo.1 = f32[16,16,128]{2,1,0:T(8,128)S(1)} custom-call(s32[1]{0:T(128)S(6)} %copy.9.live_ref, f32[3,24,128]{2,1,0:T(8,128)S(1)} %collective-permute-done.before_ref, f32[3,24,128]{2,1,0:T(8,128)S(1)} %collective-permute-done.1.after_ref, f32[24,256]{1,0:T(8,128)S(1)} %get-tuple-element.20.pm_ref, ...), custom_call_target="tpu_custom_call" | custom-call | tf_op jit(solution)/shard_map/join_halo/pallas_call | solution.py:568
  15.8 14.7 %all_to_all.5.in_ref = f32[16,16,128]{2,1,0:T(8,128)S(1)} all-to-all(f32[16,16,128]{2,1,0:T(8,128)S(1)} %join_halo.1), channel_id=1, replica_groups=mesh['grp'=2,'tile'=4,'tm'=4] {'tile','tm'}, dimensions={0} | all-to-all | bytes 262144 | tf_op jit(solution)/shard_map/all_to_all | solution.py:576
  30.6 0.0 copy-done.2
  30.6 1.3 %smooth.1 = (f32[24,64]{1,0:T(8,128)}, f32[24,64]{1,0:T(8,128)}) custom-call(f32[16,16,128]{2,1,0:T(8,128)S(1)} %all_to_all.5.in_ref, f32[1,256]{1,0:T(1,128)S(1)} %bitcast.11, f32[1,256]{1,0:T(1,128)S(1)} %bitcast.10), custom_call_target="tpu_custom_call" | custom-call | tf_op jit(solution)/shard_map/smooth/pallas_call | solution.py:577
Async XLA Ops:
  0.6 9.4 %copy-start = (bf16[3,24,100,800]{3,1,2,0:T(8,128)(2,1)S(1)}, bf16[3,24,100,800]{3,1,2,0:T(8,128)(2,1)}, u32[]{:S(2)}) copy-start(bf16[3,24,100,800]{3,1,2,0:T(8,128)(2,1)} %param.7) | copy-start | bytes 34560004
  0.6 14.8 %copy-start.1 = (f32[256]{0:T(256)S(1)}, f32[256]{0:T(256)}, u32[]{:S(2)}) copy-start(f32[256]{0:T(256)} %param.13) | copy-start | bytes 3076
  0.7 29.9 %copy-start.2 = (f32[256]{0:T(256)S(1)}, f32[256]{0:T(256)}, u32[]{:S(2)}) copy-start(f32[256]{0:T(256)} %param.12) | copy-start | bytes 3076
  3.5 11.9 %collective-permute-start = (f32[3,24,128]{2,1,0:T(8,128)S(1)}, f32[3,24,128]{2,1,0:T(8,128)S(1)}, u32[]{:S(2)}, u32[]{:S(2)}) collective-permute-start(f32[3,24,128]{2,1,0:T(8,128)S(1)} %get-tuple-element.13), channel_id=1, source_target_pairs={{0,4},{4,8},{8,12},{1,5},{5,9},{9,13},{2,6},{6,10},{10,14},{3,7},{... | collective-permute-start | bytes 110600 | tf_op jit(solution)/shard_map/ppermute | solution.py:545
  8.7 6.7 %collective-permute-start.1 = (f32[3,24,128]{2,1,0:T(8,128)S(1)}, f32[3,24,128]{2,1,0:T(8,128)S(1)}, u32[]{:S(2)}, u32[]{:S(2)}) collective-permute-start(f32[3,24,128]{2,1,0:T(8,128)S(1)} %get-tuple-element.14), channel_id=1, source_target_pairs={{4,0},{8,4},{12,8},{5,1},{9,5},{13,9},{6,2},{10,6},{14,10},{7,3},{... | collective-permute-start | bytes 110600 | tf_op jit(solution)/shard_map/ppermute | solution.py:546

commit v9 on v8

--- a/solution.py
+++ b/solution.py
@@ -196,8 +196,6 @@
     for s in range(sensors):
         for e in range(2):
             copy(s, e).wait()
-    for s in range(sensors):
-        for e in range(2):
             first_row = e * (SIDE - SHIFT)
             out = block_moments(
                 buf.at[s, e], geo_ref.at[s, e * last], narrow_ref.at[s, e], wide_ref.at[s, e], frames, first_row
@@ -347,7 +345,7 @@
                 preferred_element_type=jnp.float32,
             )
     frame = lax.broadcasted_iota(jnp.int32, (frames, 1), 0)
-    live = (frame < live_ref[0]).astype(jnp.float32)
+    live = (frame < live_ref[0:1, 0:1]).astype(jnp.float32)
     info = gain_ref[...] * modes * live
     own = lane_iota(frames) == lax.broadcasted_iota(jnp.int32, (frames, LANES), 0)
     counts = jnp.sum(jnp.where(own, count_ref[...] * live, 0.0), axis=0, keepdims=True)
@@ -377,113 +375,76 @@
     return jnp.where(row >= by, pltpu.roll(x, by, axis=0), fill)
 
 
-def filter_join(early, late):
-    a1, b1, c1, e1, j1 = early
-    a, b, c, e, j = late
-    damp = 1.0 / (1.0 + c1 * j)
-    left = a * damp
-    right = a1 * damp
-    return (
-        left * a1,
-        left * (b1 + c1 * e) + b,
-        left * a * c1 + c,
-        right * (e - j * b1) + e1,
-        right * a1 * j + j1,
-    )
-
-
-def smoother_join(late, early):
-    g1, m1, v1 = late
-    g, m, v = early
-    return g * g1, g * m1 + m, g * g * v1 + v
-
-
-def scan_lanes(values, ident, join, back, share):
-    rows = values[0].shape[0]
-    by = 1
-    while by < rows:
-        values = join(tuple(shifted(x, by, i, back) for x, i in zip(values, ident)), values)
-        by *= 2
-    edge = slice(0, 1) if back else slice(rows - 1, rows)
-    ends = tuple(x[edge] for x in values)
-    lane = lane_iota()
-
-    def over(x, groups, i):
-        step = groups * share
-        if back:
-            return jnp.where(lane < LANES - step, pltpu.roll(x, LANES - step, axis=1), i)
-        return jnp.where(lane >= step, pltpu.roll(x, step, axis=1), i)
-
-    groups = 1
-    while groups * share < LANES - share:
-        ends = join(tuple(over(x, groups, i) for x, i in zip(ends, ident)), ends)
-        groups *= 2
-    return join(tuple(over(x, 1, i) for x, i in zip(ends, ident)), values)
-
-
 def kernel_smooth(
     tiles, blocks, frames, total_subaps, in_ref, noise_ref, gain_ref, mean_ref, var_ref, mean_scr, var_scr
 ):
     share = mean_ref.shape[1]
+    total = blocks * frames
     tile = lax.axis_index("tile")
     time = lax.axis_index("tm")
     pack = LANES // share
     rows = frames // pack
-    per_group = blocks // pack
-    lane = lane_iota()
 
     def own_modes(v):
         out = v[:, 0:share]
         for t in range(1, tiles):
             out = jnp.where(tile == t, v[:, t * share : (t + 1) * share], out)
-        return jnp.concatenate([out] * pack, axis=1)
+        return out
 
     q = own_modes(noise_ref[...])
     gain = own_modes(gain_ref[...])
     own = lane_iota(frames) == lax.broadcasted_iota(jnp.int32, (frames, LANES), 0)
-    infos = [None] * per_group
-    counts = [None] * per_group
+    infos = []
+    counts = []
     for b in range(blocks):
         v = in_ref[b]
         for t in range(1, tiles):
             v = v + in_ref[t * blocks + b]
-        group, place = divmod(b, per_group)
-        parts = []
         for g in range(pack):
-            turn = (group - g) % pack * share
-            parts.append(pltpu.roll(v, turn, axis=1)[0:rows] if turn else v[0:rows])
-        info = jnp.concatenate(parts, axis=0)
-        count = jnp.sum(jnp.where(own, v[rows : rows + 1], 0.0), axis=1, keepdims=True)
-        if group == 0:
-            infos[place] = info
-            counts[place] = jnp.broadcast_to(count, (frames, LANES))
-        else:
-            infos[place] = jnp.where(lane >= group * share, info, infos[place])
-            counts[place] = jnp.where(lane >= group * share, count, counts[place])
+            infos.append(v[0:rows, g * share : (g + 1) * share])
+        counts.append(jnp.sum(jnp.where(own, v[rows : rows + 1], 0.0), axis=1, keepdims=True))
     info_mean = jnp.concatenate(infos, axis=0)
     prec = gain * jnp.concatenate(counts, axis=0) / total_subaps
-    length = per_group * frames
-    row = lax.broadcasted_iota(jnp.int32, (length, LANES), 0)
-    wide_lane = lane_iota(length)
-    first = (row == 0) & (wide_lane < share)
-    last = (row == length - 1) & (wide_lane >= LANES - share)
+    row = lax.broadcasted_iota(jnp.int32, (total, 1), 0)
+    first = row == 0
     retain = 1.0 / (1.0 + q * prec)
     a = jnp.where(first, 0.0, retain)
     c = jnp.where(first, 1.0 / (1.0 + prec), q * retain)
-    _, b, c, _, _ = scan_lanes(
-        (a, c * info_mean, c, a * info_mean, a * prec), (1.0, 0.0, 0.0, 0.0, 0.0), filter_join, False, share
-    )
-    g = jnp.where(last, 0.0, c / (c + q))
-    _, m, v = scan_lanes((g, (1.0 - g) * b, c * (1.0 - g)), (1.0, 0.0, 0.0), smoother_join, True, share)
+    b = c * info_mean
+    e = a * info_mean
+    j = a * prec
+    by = 1
+    while by < total:
+        a1 = shifted(a, by, 1.0, False)
+        b1 = shifted(b, by, 0.0, False)
+        c1 = shifted(c, by, 0.0, False)
+        e1 = shifted(e, by, 0.0, False)
+        j1 = shifted(j, by, 0.0, False)
+        damp = 1.0 / (1.0 + c1 * j)
+        left = a * damp
+        right = a1 * damp
+        b = left * (b1 + c1 * e) + b
+        c = left * a * c1 + c
+        e, j = right * (e - j * b1) + e1, right * a1 * j + j1
+        a = left * a1
+        by *= 2
+    g = jnp.where(row == total - 1, 0.0, c / (c + q))
+    m = (1.0 - g) * b
+    v = c * (1.0 - g)
+    by = 1
+    while by < total:
+        g1 = shifted(g, by, 1.0, True)
+        m1 = shifted(m, by, 0.0, True)
+        v1 = shifted(v, by, 0.0, True)
+        m = g * m1 + m
+        v = g * g * v1 + v
+        g = g * g1
+        by *= 2
     mean_scr[...] = m
     var_scr[...] = v
-    start = pl.multiple_of(time % per_group * frames, 8)
-    for scr, out_ref in ((mean_scr, mean_ref), (var_scr, var_ref)):
-        piece = scr[pl.ds(start, frames), :]
-        out = piece[:, 0:share]
-        for g in range(1, pack):
-            out = jnp.where(time // per_group == g, piece[:, g * share : (g + 1) * share], out)
-        out_ref[...] = out
+    start = pl.multiple_of(time * frames, 8)
+    mean_ref[...] = mean_scr[pl.ds(start, frames), :]
+    var_ref[...] = var_scr[pl.ds(start, frames), :]
 
 
 def body(pixels, offsets, mask, frame_count, slope_to_modes, process_noise, mode_gain):
@@ -568,11 +529,13 @@
     payload = pl.pallas_call(
         functools.partial(kernel_join, sub_rows, sub_cols, frames, tiles, blocks),
         out_shape=jax.ShapeDtypeStruct((tiles * blocks, packed, LANES), f32),
-        in_specs=[pl.BlockSpec(memory_space=pltpu.SMEM)] + [VMEM] * 8,
+        in_specs=[VMEM] * 9,
         out_specs=VMEM,
-        compiler_params=params,
+        compiler_params=pltpu.CompilerParams(
+            vmem_limit_bytes=VMEM_LIMIT, allow_input_fusion=[True] + [False] * 8
+        ),
         name="join_halo",
-    )(frame_count, from_before, from_after, partial_modes, edge, edge_mask, count, modes_v, gain)
+    )(jnp.broadcast_to(frame_count[:, None], (8, LANES)), from_before, from_after, partial_modes, edge, edge_mask, count, modes_v, gain)
     info = lax.all_to_all(payload, ("tile", "tm"), 0, 0)
     return pl.pallas_call(
         functools.partial(kernel_smooth, tiles, blocks, frames, float(total_subaps)),
@@ -583,8 +546,8 @@
         in_specs=[VMEM] * 3,
         out_specs=(VMEM, VMEM),
         scratch_shapes=[
-            pltpu.VMEM((blocks * frames * share // LANES, LANES), f32),
-            pltpu.VMEM((blocks * frames * share // LANES, LANES), f32),
+            pltpu.VMEM((blocks * frames, share), f32),
+            pltpu.VMEM((blocks * frames, share), f32),
         ],
         compiler_params=params,
         name="smooth",

time: 32.1 us -> 32.8 us (1.022)
  Pallas kernels: 9.26 us -> 9.93 us
    pallas_call x1, Pallas kernels: 2.84 us -> 3.63 us  [body(): pl.pallas_call(functools.partial(kernel_halo, sub_rows, sub_cols, frames)...]
where the time goes in v9:
time: 32.8 us; the launch traced here: 32.6 us
  blocking collectives  14.7 us (45%)
  Pallas kernels  9.93 us (30%)
  starting transfers between devices  6.48 us (20%)
  between operations  1.39 us (4%)
    all_to_all x1, blocking collectives, body(): info = lax.all_to_all(payload, ('tile', 'tm'), 0, 0)  14.7 us
    ppermute x1, starting transfers between devices, body(): from_before = lax.ppermute(up, 'tile', onward)  5.19 us
    pallas_call x1, Pallas kernels, body(): pl.pallas_call(functools.partial(kernel_moments, sub_rows, sub_cols, fram...  4.73 us
    pallas_call x1, Pallas kernels, body(): pl.pallas_call(functools.partial(kernel_halo, sub_rows, sub_cols, frames)...  3.63 us
    ppermute x1, starting transfers between devices, body(): from_after = lax.ppermute(down, 'tile', backward)  1.29 us
    pallas_call x1, Pallas kernels, body(): pl.pallas_call(functools.partial(kernel_smooth, tiles, blocks, frames, fl...  1.19 us
  transfers between devices with their start and end apart: 2, of which 0 were waited for; matrix products, arithmetic and copies ran while one was open for 0% of the time, Pallas kernels for 15%

profile of v9, /device:TPU:0, one launch (start us, length us, event | category | flops | bytes accessed | tf_op | source)
XLA Modules:
  0.0 32.6 jit_solution(11283615258698221007)
XLA Ops:
  0.6 0.0 copy-start
  0.6 0.0 copy-start.1
  0.7 0.0 copy-start.2
  0.7 3.6 %halo_moments.1 = (f32[3,24,128]{2,1,0:T(8,128)S(1)}, f32[3,24,128]{2,1,0:T(8,128)S(1)}, f32[3,5,8,128]{3,2,1,0:T(8,128)S(1)}, bf16[3,2,2,256,128]{4,3,2,1,0:T(8...) custom-call(bf16[3,2400,800]{2,1,0:T(8,128)(2,1)} %bitcast.9, ...), custom_call_target="tpu_custom_call" | custom-call | flops 393216000 | bytes 1536000 | tf_op jit(solution)/shard_map/halo_moments/pallas_call | solution.py:478
  4.3 5.2 %collective-permute-start = (f32[3,24,128]{2,1,0:T(8,128)S(1)}, f32[3,24,128]{2,1,0:T(8,128)S(1)}, u32[]{:S(2)}, u32[]{:S(2)}) collective-permute-start(f32[3,24,128]{2,1,0:T(8,128)S(1)} %get-tuple-element.13), channel_id=1, source_target_pairs={{0,4},{4,8},{8,12},{1,5},{5,9},{9,13},{2,6},{6,10},{10,14},{3,7},{... | collective-permute-start | bytes 110600 | tf_op jit(solution)/shard_map/ppermute | solution.py:506
  9.5 1.3 %collective-permute-start.1 = (f32[3,24,128]{2,1,0:T(8,128)S(1)}, f32[3,24,128]{2,1,0:T(8,128)S(1)}, u32[]{:S(2)}, u32[]{:S(2)}) collective-permute-start(f32[3,24,128]{2,1,0:T(8,128)S(1)} %get-tuple-element.14), channel_id=1, source_target_pairs={{4,0},{8,4},{12,8},{5,1},{9,5},{13,9},{6,2},{10,6},{14,10},{7,3},{... | collective-permute-start | bytes 110600 | tf_op jit(solution)/shard_map/ppermute | solution.py:507
  10.8 0.0 copy-done
  10.8 4.7 %moments.1 = (f32[24,256]{1,0:T(8,128)S(1)}, f32[2,2,2,24,128]{4,3,2,1,0:T(8,128)S(1)}, f32[2,2,24,128]{3,2,1,0:T(8,128)S(1)}, f32[24,128]{1,0:T(8,128)S(1)}) custom-call(bf16[3,2400,800]{2,1,0:T(8,128)(2,1)S(1)} %bitcast.10, f32[3,5,8,128]{3,2,1,0:T(8,128)S(1)} %get-tuple-element.15.geo_ref, ...), custom_call_target="tpu_custom_call" | custom-call | flops 2949120000 | bytes 11520000 | tf_op jit(solution)/shard_map/moments/pallas_call | solution.py:508
  16.2 0.0 collective-permute-done.before_ref
  16.2 0.0 collective-permute-done.1.after_ref
  16.2 0.0 copy-done.1
  16.2 0.4 %join_halo.1 = f32[16,16,128]{2,1,0:T(8,128)S(1)} custom-call(s32[8,128]{1,0:T(8,128)S(1)} %broadcast_in_dim.9.live_ref, f32[3,24,128]{2,1,0:T(8,128)S(1)} %collective-permute-done.before_ref, f32[3,24,128]{2,1,0:T(8,128)S(1)} %collective-permute-done.1.after_ref, f32[24,256]{1,0:T(8,128)S(1)} %get-tuple-element.20.pm_ref, ...), custom_call_target="tpu_custom_call" | custom-call | tf_op jit(solution)/shard_map/join_halo/pallas_call | solution.py:529
  16.6 14.7 %all_to_all.5.in_ref = f32[16,16,128]{2,1,0:T(8,128)S(1)} all-to-all(f32[16,16,128]{2,1,0:T(8,128)S(1)} %join_halo.1), channel_id=1, replica_groups=mesh['grp'=2,'tile'=4,'tm'=4] {'tile','tm'}, dimensions={0} | all-to-all | bytes 262144 | tf_op jit(solution)/shard_map/all_to_all | solution.py:539
  31.4 0.0 copy-done.2
  31.4 1.2 %smooth.1 = (f32[24,64]{1,0:T(8,128)}, f32[24,64]{1,0:T(8,128)}) custom-call(f32[16,16,128]{2,1,0:T(8,128)S(1)} %all_to_all.5.in_ref, f32[1,256]{1,0:T(1,128)S(1)} %bitcast.13, f32[1,256]{1,0:T(1,128)S(1)} %bitcast.12), custom_call_target="tpu_custom_call" | custom-call | tf_op jit(solution)/shard_map/smooth/pallas_call | solution.py:540
  (1 shorter events, 0.0 us)
Async XLA Ops:
  0.6 10.2 %copy-start = (bf16[3,24,100,800]{3,1,2,0:T(8,128)(2,1)S(1)}, bf16[3,24,100,800]{3,1,2,0:T(8,128)(2,1)}, u32[]{:S(2)}) copy-start(bf16[3,24,100,800]{3,1,2,0:T(8,128)(2,1)} %param.7) | copy-start | bytes 34560004
  0.6 15.6 %copy-start.1 = (f32[256]{0:T(256)S(1)}, f32[256]{0:T(256)}, u32[]{:S(2)}) copy-start(f32[256]{0:T(256)} %param.13) | copy-start | bytes 3076
  0.7 30.7 %copy-start.2 = (f32[256]{0:T(256)S(1)}, f32[256]{0:T(256)}, u32[]{:S(2)}) copy-start(f32[256]{0:T(256)} %param.12) | copy-start | bytes 3076
  4.3 11.9 %collective-permute-start = (f32[3,24,128]{2,1,0:T(8,128)S(1)}, f32[3,24,128]{2,1,0:T(8,128)S(1)}, u32[]{:S(2)}, u32[]{:S(2)}) collective-permute-start(f32[3,24,128]{2,1,0:T(8,128)S(1)} %get-tuple-element.13), channel_id=1, source_target_pairs={{0,4},{4,8},{8,12},{1,5},{5,9},{9,13},{2,6},{6,10},{10,14},{3,7},{... | collective-permute-start | bytes 110600 | tf_op jit(solution)/shard_map/ppermute | solution.py:506
  9.5 6.7 %collective-permute-start.1 = (f32[3,24,128]{2,1,0:T(8,128)S(1)}, f32[3,24,128]{2,1,0:T(8,128)S(1)}, u32[]{:S(2)}, u32[]{:S(2)}) collective-permute-start(f32[3,24,128]{2,1,0:T(8,128)S(1)} %get-tuple-element.14), channel_id=1, source_target_pairs={{4,0},{8,4},{12,8},{5,1},{9,5},{13,9},{6,2},{10,6},{14,10},{7,3},{... | collective-permute-start | bytes 110600 | tf_op jit(solution)/shard_map/ppermute | solution.py:507

commit v10 on v9

--- a/solution.py
+++ b/solution.py
@@ -103,11 +103,15 @@
         yield first + 16 * t, jnp.where(jnp.abs(d) < 10.0, value, 0.0).astype(jnp.bfloat16)
 
 
-def clear_weights(wide_ref, rest):
+def clear_weights(wide_ref, sub_cols, width):
     zero = jnp.zeros((16, LANES), jnp.bfloat16)
+    rest = width - 3 * TILE
+    end = sum(half_columns(0, sub_cols, width)) - TILE
+    begin = half_columns(1, sub_cols, width)[0] - TILE
     for n in range(wide_ref.shape[0]):
-        for t in range(0, TILE, 16):
+        for t in range(end, TILE, 16):
             wide_ref[n, t : t + 16, 0:LANES] = zero
+        for t in range(0, begin, 16):
             wide_ref[n, t : t + 16, LANES:] = zero
         for t in range(0, rest, 16):
             wide_ref[n, TILE + t : TILE + t + 16, LANES:] = zero
@@ -187,7 +191,7 @@
     mask_copy.start()
     modes_copy.start()
     for s in range(sensors):
-        clear_weights(wide_ref.at[s], width - 3 * TILE)
+        clear_weights(wide_ref.at[s], sub_cols, width)
     off_copy.wait()
     geometry(geo_ref, off_ref, table_ref, spread_ref, sensors, sub_rows, sub_cols, width)
     for s in range(sensors):
@@ -196,6 +200,8 @@
     for s in range(sensors):
         for e in range(2):
             copy(s, e).wait()
+    for s in range(sensors):
+        for e in range(2):
             first_row = e * (SIDE - SHIFT)
             out = block_moments(
                 buf.at[s, e], geo_ref.at[s, e * last], narrow_ref.at[s, e], wide_ref.at[s, e], frames, first_row
@@ -254,25 +260,22 @@
     cols = sub_cols // 2
 
     width = x_ref.shape[2]
-    clear_weights(wide_ref, width - 3 * TILE)
-
-    def step(s, carry):
+    for s in range(sensors):
+        clear_weights(wide_ref.at[s], sub_cols, width)
         for i in range(1, last):
-            block_weights(geo_ref.at[s, i], narrow_ref.at[i - 1], wide_ref.at[i - 1], sub_cols, width)
+            block_weights(geo_ref.at[s, i], narrow_ref.at[s, i - 1], wide_ref.at[s, i - 1], sub_cols, width)
+    for s in range(sensors):
         for i in range(sub_rows):
             if i in (0, last):
                 weights = (edge_narrow_ref.at[s, i // last], edge_wide_ref.at[s, i // last])
             else:
-                weights = (narrow_ref.at[i - 1], wide_ref.at[i - 1])
+                weights = (narrow_ref.at[s, i - 1], wide_ref.at[s, i - 1])
             out = block_moments(
                 x_ref.at[s, i * block : (i + 1) * block], geo_ref.at[s, i], *weights, frames
             )
             for h in range(2):
                 for a in range(2):
                     p_ref[s, i, h, a] = out[h][a]
-        return carry
-
-    lax.fori_loop(0, sensors, step, 0)
 
     def strip_total(s, k, h, a):
         total = None
@@ -345,7 +348,7 @@
                 preferred_element_type=jnp.float32,
             )
     frame = lax.broadcasted_iota(jnp.int32, (frames, 1), 0)
-    live = (frame < live_ref[0:1, 0:1]).astype(jnp.float32)
+    live = (frame < live_ref[0]).astype(jnp.float32)
     info = gain_ref[...] * modes * live
     own = lane_iota(frames) == lax.broadcasted_iota(jnp.int32, (frames, LANES), 0)
     counts = jnp.sum(jnp.where(own, count_ref[...] * live, 0.0), axis=0, keepdims=True)
@@ -516,8 +519,8 @@
         in_specs=[VMEM] * 6,
         out_specs=(VMEM,) * 4,
         scratch_shapes=[
-            pltpu.VMEM((sub_rows - 2, *narrow), bf16),
-            pltpu.VMEM((sub_rows - 2, *wide), bf16),
+            pltpu.VMEM((sensors, sub_rows - 2, *narrow), bf16),
+            pltpu.VMEM((sensors, sub_rows - 2, *wide), bf16),
             pltpu.VMEM((sensors, sub_rows, 2, 2, frames, LANES), f32),
         ],
         compiler_params=params,
@@ -529,13 +532,11 @@
     payload = pl.pallas_call(
         functools.partial(kernel_join, sub_rows, sub_cols, frames, tiles, blocks),
         out_shape=jax.ShapeDtypeStruct((tiles * blocks, packed, LANES), f32),
-        in_specs=[VMEM] * 9,
+        in_specs=[pl.BlockSpec(memory_space=pltpu.SMEM)] + [VMEM] * 8,
         out_specs=VMEM,
-        compiler_params=pltpu.CompilerParams(
-            vmem_limit_bytes=VMEM_LIMIT, allow_input_fusion=[True] + [False] * 8
-        ),
+        compiler_params=params,
         name="join_halo",
-    )(jnp.broadcast_to(frame_count[:, None], (8, LANES)), from_before, from_after, partial_modes, edge, edge_mask, count, modes_v, gain)
+    )(frame_count, from_before, from_after, partial_modes, edge, edge_mask, count, modes_v, gain)
     info = lax.all_to_all(payload, ("tile", "tm"), 0, 0)
     return pl.pallas_call(
         functools.partial(kernel_smooth, tiles, blocks, frames, float(total_subaps)),

time: 32.8 us -> 31.6 us (0.963)
  Pallas kernels: 9.93 us -> 8.79 us
    pallas_call x1, Pallas kernels: 3.63 us -> 2.84 us  [body(): pl.pallas_call(functools.partial(kernel_halo, sub_rows, sub_cols, frames)...]
    pallas_call x1, Pallas kernels: 4.73 us -> 4.38 us  [body(): pl.pallas_call(functools.partial(kernel_moments, sub_rows, sub_cols, fram...]
  transfers between devices with their start and end apart: 2 -> 2, of which waited for: 0 -> 0; matrix products, arithmetic and copies ran while one was open for 0% -> 0% of each run, Pallas kernels for 15% -> 14%
where the time goes in v10:
time: 31.6 us; the launch traced here: 31.4 us
  blocking collectives  14.8 us (47%)
  Pallas kernels  8.79 us (28%)
  starting transfers between devices  6.49 us (21%)
  between operations  1.38 us (4%)
    all_to_all x1, blocking collectives, body(): info = lax.all_to_all(payload, ('tile', 'tm'), 0, 0)  14.8 us
    ppermute x1, starting transfers between devices, body(): from_before = lax.ppermute(up, 'tile', onward)  5.19 us
    pallas_call x1, Pallas kernels, body(): pl.pallas_call(functools.partial(kernel_moments, sub_rows, sub_cols, fram...  4.38 us
    pallas_call x1, Pallas kernels, body(): pl.pallas_call(functools.partial(kernel_halo, sub_rows, sub_cols, frames)...  2.84 us
    ppermute x1, starting transfers between devices, body(): from_after = lax.ppermute(down, 'tile', backward)  1.29 us
    pallas_call x1, Pallas kernels, body(): pl.pallas_call(functools.partial(kernel_smooth, tiles, blocks, frames, fl...  1.19 us
  transfers between devices with their start and end apart: 2, of which 0 were waited for; matrix products, arithmetic and copies ran while one was open for 0% of the time, Pallas kernels for 14%

profile of v10, /device:TPU:0, one launch (start us, length us, event | category | flops | bytes accessed | tf_op | source)
XLA Modules:
  0.0 31.4 jit_solution(14913634200418810231)
XLA Ops:
  0.6 0.0 copy-start
  0.6 0.0 copy-start.1
  0.7 0.0 copy-start.2
  0.7 2.8 %halo_moments.1 = (f32[3,24,128]{2,1,0:T(8,128)S(1)}, f32[3,24,128]{2,1,0:T(8,128)S(1)}, f32[3,5,8,128]{3,2,1,0:T(8,128)S(1)}, bf16[3,2,2,256,128]{4,3,2,1,0:T(8...) custom-call(bf16[3,2400,800]{2,1,0:T(8,128)(2,1)} %bitcast.7, ...), custom_call_target="tpu_custom_call" | custom-call | flops 393216000 | bytes 1536000 | tf_op jit(solution)/shard_map/halo_moments/pallas_call | solution.py:481
  3.5 5.2 %collective-permute-start = (f32[3,24,128]{2,1,0:T(8,128)S(1)}, f32[3,24,128]{2,1,0:T(8,128)S(1)}, u32[]{:S(2)}, u32[]{:S(2)}) collective-permute-start(f32[3,24,128]{2,1,0:T(8,128)S(1)} %get-tuple-element.13), channel_id=1, source_target_pairs={{0,4},{4,8},{8,12},{1,5},{5,9},{9,13},{2,6},{6,10},{10,14},{3,7},{... | collective-permute-start | bytes 110600 | tf_op jit(solution)/shard_map/ppermute | solution.py:509
  8.7 1.3 %collective-permute-start.1 = (f32[3,24,128]{2,1,0:T(8,128)S(1)}, f32[3,24,128]{2,1,0:T(8,128)S(1)}, u32[]{:S(2)}, u32[]{:S(2)}) collective-permute-start(f32[3,24,128]{2,1,0:T(8,128)S(1)} %get-tuple-element.14), channel_id=1, source_target_pairs={{4,0},{8,4},{12,8},{5,1},{9,5},{13,9},{6,2},{10,6},{14,10},{7,3},{... | collective-permute-start | bytes 110600 | tf_op jit(solution)/shard_map/ppermute | solution.py:510
  10.0 0.0 copy-done
  10.0 4.4 %moments.1 = (f32[24,256]{1,0:T(8,128)S(1)}, f32[2,2,2,24,128]{4,3,2,1,0:T(8,128)S(1)}, f32[2,2,24,128]{3,2,1,0:T(8,128)S(1)}, f32[24,128]{1,0:T(8,128)S(1)}) custom-call(bf16[3,2400,800]{2,1,0:T(8,128)(2,1)S(1)} %bitcast.8, f32[3,5,8,128]{3,2,1,0:T(8,128)S(1)} %get-tuple-element.15.geo_ref, ...), custom_call_target="tpu_custom_call" | custom-call | flops 2949120000 | bytes 11520000 | tf_op jit(solution)/shard_map/moments/pallas_call | solution.py:511
  15.1 0.0 collective-permute-done.before_ref
  15.1 0.0 collective-permute-done.1.after_ref
  15.1 0.0 copy-done.1
  15.1 0.4 %join_halo.1 = f32[16,16,128]{2,1,0:T(8,128)S(1)} custom-call(s32[1]{0:T(128)S(6)} %copy.9.live_ref, f32[3,24,128]{2,1,0:T(8,128)S(1)} %collective-permute-done.before_ref, f32[3,24,128]{2,1,0:T(8,128)S(1)} %collective-permute-done.1.after_ref, f32[24,256]{1,0:T(8,128)S(1)} %get-tuple-element.20.pm_ref, ...), custom_call_target="tpu_custom_call" | custom-call | tf_op jit(solution)/shard_map/join_halo/pallas_call | solution.py:532
  15.5 14.8 %all_to_all.5.in_ref = f32[16,16,128]{2,1,0:T(8,128)S(1)} all-to-all(f32[16,16,128]{2,1,0:T(8,128)S(1)} %join_halo.1), channel_id=1, replica_groups=mesh['grp'=2,'tile'=4,'tm'=4] {'tile','tm'}, dimensions={0} | all-to-all | bytes 262144 | tf_op jit(solution)/shard_map/all_to_all | solution.py:540
  30.2 0.0 copy-done.2
  30.2 1.2 %smooth.1 = (f32[24,64]{1,0:T(8,128)}, f32[24,64]{1,0:T(8,128)}) custom-call(f32[16,16,128]{2,1,0:T(8,128)S(1)} %all_to_all.5.in_ref, f32[1,256]{1,0:T(1,128)S(1)} %bitcast.11, f32[1,256]{1,0:T(1,128)S(1)} %bitcast.10), custom_call_target="tpu_custom_call" | custom-call | tf_op jit(solution)/shard_map/smooth/pallas_call | solution.py:541
Async XLA Ops:
  0.6 9.4 %copy-start = (bf16[3,24,100,800]{3,1,2,0:T(8,128)(2,1)S(1)}, bf16[3,24,100,800]{3,1,2,0:T(8,128)(2,1)}, u32[]{:S(2)}) copy-start(bf16[3,24,100,800]{3,1,2,0:T(8,128)(2,1)} %param.7) | copy-start | bytes 34560004
  0.6 14.4 %copy-start.1 = (f32[256]{0:T(256)S(1)}, f32[256]{0:T(256)}, u32[]{:S(2)}) copy-start(f32[256]{0:T(256)} %param.13) | copy-start | bytes 3076
  0.7 29.6 %copy-start.2 = (f32[256]{0:T(256)S(1)}, f32[256]{0:T(256)}, u32[]{:S(2)}) copy-start(f32[256]{0:T(256)} %param.12) | copy-start | bytes 3076
  3.5 11.5 %collective-permute-start = (f32[3,24,128]{2,1,0:T(8,128)S(1)}, f32[3,24,128]{2,1,0:T(8,128)S(1)}, u32[]{:S(2)}, u32[]{:S(2)}) collective-permute-start(f32[3,24,128]{2,1,0:T(8,128)S(1)} %get-tuple-element.13), channel_id=1, source_target_pairs={{0,4},{4,8},{8,12},{1,5},{5,9},{9,13},{2,6},{6,10},{10,14},{3,7},{... | collective-permute-start | bytes 110600 | tf_op jit(solution)/shard_map/ppermute | solution.py:509
  8.7 6.4 %collective-permute-start.1 = (f32[3,24,128]{2,1,0:T(8,128)S(1)}, f32[3,24,128]{2,1,0:T(8,128)S(1)}, u32[]{:S(2)}, u32[]{:S(2)}) collective-permute-start(f32[3,24,128]{2,1,0:T(8,128)S(1)} %get-tuple-element.14), channel_id=1, source_target_pairs={{4,0},{8,4},{12,8},{5,1},{9,5},{13,9},{6,2},{10,6},{14,10},{7,3},{... | collective-permute-start | bytes 110600 | tf_op jit(solution)/shard_map/ppermute | solution.py:510

commit v11 on v10

--- a/solution.py
+++ b/solution.py
@@ -136,7 +136,17 @@
                 wide_ref[at + rest : at + rest + 16, LANES:] = piece
 
 
-def block_moments(pixels, geo_ref, narrow_ref, wide_ref, frames, first_row=0):
+def row_weights(geo_ref, line_ref):
+    count = line_ref.shape[2]
+    row = lax.broadcasted_iota(jnp.int32, (count, LANES), 0).astype(jnp.float32)
+    for h in range(2):
+        d = row - geo_ref[2 * h + 1 : 2 * h + 2, :]
+        inside = jnp.abs(d) < 10.0
+        line_ref[h, 0] = jnp.where(inside, 1.0, 0.0)
+        line_ref[h, 1] = jnp.where(inside, d, 0.0)
+
+
+def block_moments(pixels, line_ref, narrow_ref, wide_ref, frames, first_row=0):
     f32 = jnp.float32
     rows, width = pixels.shape
     rest = width - 3 * TILE
@@ -159,17 +169,16 @@
             extra = r[y * frames - split : (y + 1) * frames - split, LANES:]
         pieces = (a[at] + m[at, 0:LANES], m[at, LANES:] + b[at] + extra)
         for h in range(2):
-            d = float(y + first_row) - geo_ref[2 * h + 1 : 2 * h + 2, :]
-            inside = jnp.abs(d) < 10.0
-            out[h][0] = out[h][0] + jnp.where(inside, 1.0, 0.0) * pieces[h]
-            out[h][1] = out[h][1] + jnp.where(inside, d, 0.0) * pieces[h]
+            at_row = slice(first_row + y, first_row + y + 1)
+            out[h][0] = out[h][0] + line_ref[h, 0, at_row, :] * pieces[h]
+            out[h][1] = out[h][1] + line_ref[h, 1, at_row, :] * pieces[h]
     return out
 
 
 def kernel_halo(
     sub_rows, sub_cols, frames, x_hbm, off_hbm, mask_hbm, modes_hbm,
     up_ref, down_ref, geo_ref, narrow_ref, wide_ref, mask_ref, modes_ref,
-    buf, p_ref, off_ref, table_ref, spread_ref, sem, side_sem,
+    buf, p_ref, line_ref, off_ref, table_ref, spread_ref, sem, side_sem,
 ):
     sensors, lines, width = x_hbm.shape
     reach = SHIFT * frames
@@ -197,6 +206,7 @@
     for s in range(sensors):
         for e in range(2):
             block_weights(geo_ref.at[s, e * last], narrow_ref.at[s, e], wide_ref.at[s, e], sub_cols, width)
+            row_weights(geo_ref.at[s, e * last], line_ref.at[s, e])
     for s in range(sensors):
         for e in range(2):
             copy(s, e).wait()
@@ -204,7 +214,7 @@
         for e in range(2):
             first_row = e * (SIDE - SHIFT)
             out = block_moments(
-                buf.at[s, e], geo_ref.at[s, e * last], narrow_ref.at[s, e], wide_ref.at[s, e], frames, first_row
+                buf.at[s, e], line_ref.at[s, e], narrow_ref.at[s, e], wide_ref.at[s, e], frames, first_row
             )
             for h in range(2):
                 for a in range(2):
@@ -252,7 +262,7 @@
 
 def kernel_moments(
     sub_rows, sub_cols, frames, x_ref, geo_ref, edge_narrow_ref, edge_wide_ref, mask_ref, modes_ref,
-    pm_ref, edge_ref, em_ref, count_ref, narrow_ref, wide_ref, p_ref,
+    pm_ref, edge_ref, em_ref, count_ref, narrow_ref, wide_ref, p_ref, line_ref,
 ):
     sensors = x_ref.shape[0]
     block = SIDE * frames
@@ -262,6 +272,8 @@
     width = x_ref.shape[2]
     for s in range(sensors):
         clear_weights(wide_ref.at[s], sub_cols, width)
+        for i in range(sub_rows):
+            row_weights(geo_ref.at[s, i], line_ref.at[s, i])
         for i in range(1, last):
             block_weights(geo_ref.at[s, i], narrow_ref.at[s, i - 1], wide_ref.at[s, i - 1], sub_cols, width)
     for s in range(sensors):
@@ -271,7 +283,7 @@
             else:
                 weights = (narrow_ref.at[s, i - 1], wide_ref.at[s, i - 1])
             out = block_moments(
-                x_ref.at[s, i * block : (i + 1) * block], geo_ref.at[s, i], *weights, frames
+                x_ref.at[s, i * block : (i + 1) * block], line_ref.at[s, i], *weights, frames
             )
             for h in range(2):
                 for a in range(2):
@@ -355,12 +367,11 @@
     share = modes.shape[1] // tiles
     pack = LANES // share
     rows = frames // pack
-    pad = jnp.zeros((out_ref.shape[1] - rows - 1, LANES), jnp.float32)
     for t in range(tiles):
         piece = jnp.concatenate(
             [info[g * rows : (g + 1) * rows, t * share : (t + 1) * share] for g in range(pack)], axis=1
         )
-        piece = jnp.concatenate([piece, counts, pad], axis=0)
+        piece = jnp.concatenate([piece, counts], axis=0).reshape(rows + 1, 1, LANES)
         for b in range(blocks):
             out_ref[t * blocks + b] = piece
 
@@ -403,6 +414,7 @@
         v = in_ref[b]
         for t in range(1, tiles):
             v = v + in_ref[t * blocks + b]
+        v = v.reshape(rows + 1, LANES)
         for g in range(pack):
             infos.append(v[0:rows, g * share : (g + 1) * share])
         counts.append(jnp.sum(jnp.where(own, v[rows : rows + 1], 0.0), axis=1, keepdims=True))
@@ -469,6 +481,7 @@
     )
     block = SIDE * frames
     narrow = (2, TILE, LANES)
+    line_rows = -(-SIDE // 8) * 8
     wide = (TILE + 2 * (width - 3 * TILE), 2 * LANES)
     table_rows = -(-2 * sensors * (sub_rows + 2) // 8) * 8
     params = pltpu.CompilerParams(vmem_limit_bytes=VMEM_LIMIT)
@@ -494,6 +507,7 @@
         scratch_shapes=[
             pltpu.VMEM((sensors, 2, SHIFT * frames, width), bf16),
             pltpu.VMEM((sensors, 2, 2, 2, frames, LANES), f32),
+            pltpu.VMEM((sensors, 2, 2, 2, line_rows, LANES), f32),
             pltpu.VMEM(off.shape, off.dtype),
             pltpu.VMEM((table_rows, sub_cols), f32),
             pltpu.VMEM((2, table_rows, LANES), f32),
@@ -522,16 +536,17 @@
             pltpu.VMEM((sensors, sub_rows - 2, *narrow), bf16),
             pltpu.VMEM((sensors, sub_rows - 2, *wide), bf16),
             pltpu.VMEM((sensors, sub_rows, 2, 2, frames, LANES), f32),
+            pltpu.VMEM((sensors, sub_rows, 2, 2, line_rows, LANES), f32),
         ],
         compiler_params=params,
         cost_estimate=cost(sensors * sub_rows),
         name="moments",
     )(pixels_v, geo, edge_narrow, edge_wide, mask_v, modes_v)
     gain = mode_gain.reshape(1, modes)
-    packed = -(-(frames * share // LANES + 1) // 8) * 8
+    packed = frames * share // LANES + 1
     payload = pl.pallas_call(
         functools.partial(kernel_join, sub_rows, sub_cols, frames, tiles, blocks),
-        out_shape=jax.ShapeDtypeStruct((tiles * blocks, packed, LANES), f32),
+        out_shape=jax.ShapeDtypeStruct((tiles * blocks, packed, 1, LANES), f32),
         in_specs=[pl.BlockSpec(memory_space=pltpu.SMEM)] + [VMEM] * 8,
         out_specs=VMEM,
         compiler_params=params,

time: 31.6 us -> 31.3 us (level)
  blocking collectives: 14.8 us -> 14.4 us
    all_to_all x1, blocking collectives: 14.8 us -> 14.4 us  [body(): info = lax.all_to_all(payload, ('tile', 'tm'), 0, 0)]
where the time goes in v11:
time: 31.3 us; the launch traced here: 31 us
  blocking collectives  14.4 us (46%)
  Pallas kernels  8.8 us (28%)
  starting transfers between devices  6.49 us (21%)
  between operations  1.38 us (4%)
    all_to_all x1, blocking collectives, body(): info = lax.all_to_all(payload, ('tile', 'tm'), 0, 0)  14.4 us
    ppermute x1, starting transfers between devices, body(): from_before = lax.ppermute(up, 'tile', onward)  5.19 us
    pallas_call x1, Pallas kernels, body(): pl.pallas_call(functools.partial(kernel_moments, sub_rows, sub_cols, fram...  4.31 us
    pallas_call x1, Pallas kernels, body(): pl.pallas_call(functools.partial(kernel_halo, sub_rows, sub_cols, frames)...  2.87 us
    ppermute x1, starting transfers between devices, body(): from_after = lax.ppermute(down, 'tile', backward)  1.29 us
    pallas_call x1, Pallas kernels, body(): pl.pallas_call(functools.partial(kernel_smooth, tiles, blocks, frames, fl...  1.2 us
  transfers between devices with their start and end apart: 2, of which 0 were waited for; matrix products, arithmetic and copies ran while one was open for 0% of the time, Pallas kernels for 14%

profile of v11, /device:TPU:0, one launch (start us, length us, event | category | flops | bytes accessed | tf_op | source)
XLA Modules:
  0.0 31.0 jit_solution(6687428899206616182)
XLA Ops:
  0.6 0.0 copy-start
  0.6 0.0 copy-start.1
  0.7 0.0 copy-start.2
  0.7 2.9 %halo_moments.1 = (f32[3,24,128]{2,1,0:T(8,128)S(1)}, f32[3,24,128]{2,1,0:T(8,128)S(1)}, f32[3,5,8,128]{3,2,1,0:T(8,128)S(1)}, bf16[3,2,2,256,128]{4,3,2,1,0:T(8...) custom-call(bf16[3,2400,800]{2,1,0:T(8,128)(2,1)} %bitcast.7, ...), custom_call_target="tpu_custom_call" | custom-call | flops 393216000 | bytes 1536000 | tf_op jit(solution)/shard_map/halo_moments/pallas_call | solution.py:494
  3.5 5.2 %collective-permute-start = (f32[3,24,128]{2,1,0:T(8,128)S(1)}, f32[3,24,128]{2,1,0:T(8,128)S(1)}, u32[]{:S(2)}, u32[]{:S(2)}) collective-permute-start(f32[3,24,128]{2,1,0:T(8,128)S(1)} %get-tuple-element.13), channel_id=1, source_target_pairs={{0,4},{4,8},{8,12},{1,5},{5,9},{9,13},{2,6},{6,10},{10,14},{3,7},{... | collective-permute-start | bytes 110600 | tf_op jit(solution)/shard_map/ppermute | solution.py:523
  8.7 1.3 %collective-permute-start.1 = (f32[3,24,128]{2,1,0:T(8,128)S(1)}, f32[3,24,128]{2,1,0:T(8,128)S(1)}, u32[]{:S(2)}, u32[]{:S(2)}) collective-permute-start(f32[3,24,128]{2,1,0:T(8,128)S(1)} %get-tuple-element.14), channel_id=1, source_target_pairs={{4,0},{8,4},{12,8},{5,1},{9,5},{13,9},{6,2},{10,6},{14,10},{7,3},{... | collective-permute-start | bytes 110600 | tf_op jit(solution)/shard_map/ppermute | solution.py:524
  10.0 0.0 copy-done
  10.0 4.3 %moments.1 = (f32[24,256]{1,0:T(8,128)S(1)}, f32[2,2,2,24,128]{4,3,2,1,0:T(8,128)S(1)}, f32[2,2,24,128]{3,2,1,0:T(8,128)S(1)}, f32[24,128]{1,0:T(8,128)S(1)}) custom-call(bf16[3,2400,800]{2,1,0:T(8,128)(2,1)S(1)} %bitcast.8, f32[3,5,8,128]{3,2,1,0:T(8,128)S(1)} %get-tuple-element.15.geo_ref, ...), custom_call_target="tpu_custom_call" | custom-call | flops 2949120000 | bytes 11520000 | tf_op jit(solution)/shard_map/moments/pallas_call | solution.py:525
  15.0 0.0 collective-permute-done.before_ref
  15.0 0.0 collective-permute-done.1.after_ref
  15.0 0.0 copy-done.1
  15.0 0.4 %join_halo.1 = f32[16,13,1,128]{3,2,1,0:T(1,128)S(1)} custom-call(s32[1]{0:T(128)S(6)} %copy.9.live_ref, f32[3,24,128]{2,1,0:T(8,128)S(1)} %collective-permute-done.before_ref, f32[3,24,128]{2,1,0:T(8,128)S(1)} %collective-permute-done.1.after_ref, f32[24,256]{1,0:T(8,128)S(1)} %get-tuple-element.20.pm_ref, ...), custom_call_target="tpu_custom_call" | custom-call | tf_op jit(solution)/shard_map/join_halo/pallas_call | solution.py:547
  15.5 14.4 %all_to_all.5.in_ref = f32[16,13,1,128]{3,2,1,0:T(1,128)S(1)} all-to-all(f32[16,13,1,128]{3,2,1,0:T(1,128)S(1)} %join_halo.1), channel_id=1, replica_groups=mesh['grp'=2,'tile'=4,'tm'=4] {'tile','tm'}, dimensions={0} | all-to-all | bytes 212992 | tf_op jit(solution)/shard_map/all_to_all | solution.py:555
  29.8 0.0 copy-done.2
  29.8 1.2 %smooth.1 = (f32[24,64]{1,0:T(8,128)}, f32[24,64]{1,0:T(8,128)}) custom-call(f32[16,13,1,128]{3,2,1,0:T(1,128)S(1)} %all_to_all.5.in_ref, f32[1,256]{1,0:T(1,128)S(1)} %bitcast.11, f32[1,256]{1,0:T(1,128)S(1)} %bitcast.10), custom_call_target="tpu_custom_call" | custom-call | tf_op jit(solution)/shard_map/smooth/pallas_call | solution.py:556
Async XLA Ops:
  0.6 9.4 %copy-start = (bf16[3,24,100,800]{3,1,2,0:T(8,128)(2,1)S(1)}, bf16[3,24,100,800]{3,1,2,0:T(8,128)(2,1)}, u32[]{:S(2)}) copy-start(bf16[3,24,100,800]{3,1,2,0:T(8,128)(2,1)} %param.7) | copy-start | bytes 34560004
  0.6 14.4 %copy-start.1 = (f32[256]{0:T(256)S(1)}, f32[256]{0:T(256)}, u32[]{:S(2)}) copy-start(f32[256]{0:T(256)} %param.13) | copy-start | bytes 3076
  0.7 29.2 %copy-start.2 = (f32[256]{0:T(256)S(1)}, f32[256]{0:T(256)}, u32[]{:S(2)}) copy-start(f32[256]{0:T(256)} %param.12) | copy-start | bytes 3076
  3.5 11.5 %collective-permute-start = (f32[3,24,128]{2,1,0:T(8,128)S(1)}, f32[3,24,128]{2,1,0:T(8,128)S(1)}, u32[]{:S(2)}, u32[]{:S(2)}) collective-permute-start(f32[3,24,128]{2,1,0:T(8,128)S(1)} %get-tuple-element.13), channel_id=1, source_target_pairs={{0,4},{4,8},{8,12},{1,5},{5,9},{9,13},{2,6},{6,10},{10,14},{3,7},{... | collective-permute-start | bytes 110600 | tf_op jit(solution)/shard_map/ppermute | solution.py:523
  8.7 6.3 %collective-permute-start.1 = (f32[3,24,128]{2,1,0:T(8,128)S(1)}, f32[3,24,128]{2,1,0:T(8,128)S(1)}, u32[]{:S(2)}, u32[]{:S(2)}) collective-permute-start(f32[3,24,128]{2,1,0:T(8,128)S(1)} %get-tuple-element.14), channel_id=1, source_target_pairs={{4,0},{8,4},{12,8},{5,1},{9,5},{13,9},{6,2},{10,6},{14,10},{7,3},{... | collective-permute-start | bytes 110600 | tf_op jit(solution)/shard_map/ppermute | solution.py:524

commit v12 on v11

--- a/solution.py
+++ b/solution.py
@@ -96,11 +96,14 @@
 
 def window_weights(col_pos, first, count):
     base = lax.broadcasted_iota(jnp.int32, (16, LANES), 0).astype(jnp.float32) - col_pos
+    bf16 = jnp.bfloat16
     left = lane_iota(16) < HALF
+    plain = jnp.where(left, 1.0, 0.0).astype(bf16)
+    plain_lane = plain > jnp.bfloat16(0.5)
     for t in range(count // 16):
-        d = base + float(16 * t)
-        value = jnp.where(left, 1.0, d)
-        yield first + 16 * t, jnp.where(jnp.abs(d) < 10.0, value, 0.0).astype(jnp.bfloat16)
+        d = (base + float(16 * t)).astype(bf16)
+        value = jnp.where(plain_lane, jnp.bfloat16(1.0), d)
+        yield first + 16 * t, jnp.where(jnp.abs(d) < jnp.bfloat16(10.0), value, jnp.bfloat16(0.0))
 
 
 def clear_weights(wide_ref, sub_cols, width):
@@ -276,8 +279,7 @@
             row_weights(geo_ref.at[s, i], line_ref.at[s, i])
         for i in range(1, last):
             block_weights(geo_ref.at[s, i], narrow_ref.at[s, i - 1], wide_ref.at[s, i - 1], sub_cols, width)
-    for s in range(sensors):
-        for i in range(sub_rows):
+        for i in (0, last, *range(1, last)):
             if i in (0, last):
                 weights = (edge_narrow_ref.at[s, i // last], edge_wide_ref.at[s, i // last])
             else:

time: 31.3 us -> 31.1 us (level)
  no operation moved by 1% of the time
where the time goes in v12:
time: 31.1 us; the launch traced here: 30.9 us
  blocking collectives  14.3 us (46%)
  Pallas kernels  8.71 us (28%)
  starting transfers between devices  6.49 us (21%)
  between operations  1.38 us (4%)
    all_to_all x1, blocking collectives, body(): info = lax.all_to_all(payload, ('tile', 'tm'), 0, 0)  14.3 us
    ppermute x1, starting transfers between devices, body(): from_before = lax.ppermute(up, 'tile', onward)  5.19 us
    pallas_call x1, Pallas kernels, body(): pl.pallas_call(functools.partial(kernel_moments, sub_rows, sub_cols, fram...  4.28 us
    pallas_call x1, Pallas kernels, body(): pl.pallas_call(functools.partial(kernel_halo, sub_rows, sub_cols, frames)...  2.81 us
    ppermute x1, starting transfers between devices, body(): from_after = lax.ppermute(down, 'tile', backward)  1.29 us
    pallas_call x1, Pallas kernels, body(): pl.pallas_call(functools.partial(kernel_smooth, tiles, blocks, frames, fl...  1.2 us
  transfers between devices with their start and end apart: 2, of which 0 were waited for; matrix products, arithmetic and copies ran while one was open for 0% of the time, Pallas kernels for 14%

profile of v12, /device:TPU:0, one launch (start us, length us, event | category | flops | bytes accessed | tf_op | source)
XLA Modules:
  0.0 30.9 jit_solution(9709600793862446104)
XLA Ops:
  0.6 0.0 copy-start
  0.6 0.0 copy-start.1
  0.7 0.0 copy-start.2
  0.7 2.8 %halo_moments.1 = (f32[3,24,128]{2,1,0:T(8,128)S(1)}, f32[3,24,128]{2,1,0:T(8,128)S(1)}, f32[3,5,8,128]{3,2,1,0:T(8,128)S(1)}, bf16[3,2,2,256,128]{4,3,2,1,0:T(8...) custom-call(bf16[3,2400,800]{2,1,0:T(8,128)(2,1)} %bitcast.7, ...), custom_call_target="tpu_custom_call" | custom-call | flops 393216000 | bytes 1536000 | tf_op jit(solution)/shard_map/halo_moments/pallas_call | solution.py:496
  3.5 5.2 %collective-permute-start = (f32[3,24,128]{2,1,0:T(8,128)S(1)}, f32[3,24,128]{2,1,0:T(8,128)S(1)}, u32[]{:S(2)}, u32[]{:S(2)}) collective-permute-start(f32[3,24,128]{2,1,0:T(8,128)S(1)} %get-tuple-element.13), channel_id=1, source_target_pairs={{0,4},{4,8},{8,12},{1,5},{5,9},{9,13},{2,6},{6,10},{10,14},{3,7},{... | collective-permute-start | bytes 110600 | tf_op jit(solution)/shard_map/ppermute | solution.py:525
  8.7 1.3 %collective-permute-start.1 = (f32[3,24,128]{2,1,0:T(8,128)S(1)}, f32[3,24,128]{2,1,0:T(8,128)S(1)}, u32[]{:S(2)}, u32[]{:S(2)}) collective-permute-start(f32[3,24,128]{2,1,0:T(8,128)S(1)} %get-tuple-element.14), channel_id=1, source_target_pairs={{4,0},{8,4},{12,8},{5,1},{9,5},{13,9},{6,2},{10,6},{14,10},{7,3},{... | collective-permute-start | bytes 110600 | tf_op jit(solution)/shard_map/ppermute | solution.py:526
  10.0 0.0 copy-done
  10.0 4.3 %moments.1 = (f32[24,256]{1,0:T(8,128)S(1)}, f32[2,2,2,24,128]{4,3,2,1,0:T(8,128)S(1)}, f32[2,2,24,128]{3,2,1,0:T(8,128)S(1)}, f32[24,128]{1,0:T(8,128)S(1)}) custom-call(bf16[3,2400,800]{2,1,0:T(8,128)(2,1)S(1)} %bitcast.8, f32[3,5,8,128]{3,2,1,0:T(8,128)S(1)} %get-tuple-element.15.geo_ref, ...), custom_call_target="tpu_custom_call" | custom-call | flops 2949120000 | bytes 11520000 | tf_op jit(solution)/shard_map/moments/pallas_call | solution.py:527
  14.9 0.0 collective-permute-done.before_ref
  14.9 0.0 collective-permute-done.1.after_ref
  14.9 0.0 copy-done.1
  15.0 0.4 %join_halo.1 = f32[16,13,1,128]{3,2,1,0:T(1,128)S(1)} custom-call(s32[1]{0:T(128)S(6)} %copy.9.live_ref, f32[3,24,128]{2,1,0:T(8,128)S(1)} %collective-permute-done.before_ref, f32[3,24,128]{2,1,0:T(8,128)S(1)} %collective-permute-done.1.after_ref, f32[24,256]{1,0:T(8,128)S(1)} %get-tuple-element.20.pm_ref, ...), custom_call_target="tpu_custom_call" | custom-call | tf_op jit(solution)/shard_map/join_halo/pallas_call | solution.py:549
  15.4 14.3 %all_to_all.5.in_ref = f32[16,13,1,128]{3,2,1,0:T(1,128)S(1)} all-to-all(f32[16,13,1,128]{3,2,1,0:T(1,128)S(1)} %join_halo.1), channel_id=1, replica_groups=mesh['grp'=2,'tile'=4,'tm'=4] {'tile','tm'}, dimensions={0} | all-to-all | bytes 212992 | tf_op jit(solution)/shard_map/all_to_all | solution.py:557
  29.7 0.0 copy-done.2
  29.7 1.2 %smooth.1 = (f32[24,64]{1,0:T(8,128)}, f32[24,64]{1,0:T(8,128)}) custom-call(f32[16,13,1,128]{3,2,1,0:T(1,128)S(1)} %all_to_all.5.in_ref, f32[1,256]{1,0:T(1,128)S(1)} %bitcast.11, f32[1,256]{1,0:T(1,128)S(1)} %bitcast.10), custom_call_target="tpu_custom_call" | custom-call | tf_op jit(solution)/shard_map/smooth/pallas_call | solution.py:558
Async XLA Ops:
  0.6 9.3 %copy-start = (bf16[3,24,100,800]{3,1,2,0:T(8,128)(2,1)S(1)}, bf16[3,24,100,800]{3,1,2,0:T(8,128)(2,1)}, u32[]{:S(2)}) copy-start(bf16[3,24,100,800]{3,1,2,0:T(8,128)(2,1)} %param.7) | copy-start | bytes 34560004
  0.6 14.3 %copy-start.1 = (f32[256]{0:T(256)S(1)}, f32[256]{0:T(256)}, u32[]{:S(2)}) copy-start(f32[256]{0:T(256)} %param.13) | copy-start | bytes 3076
  0.7 29.1 %copy-start.2 = (f32[256]{0:T(256)S(1)}, f32[256]{0:T(256)}, u32[]{:S(2)}) copy-start(f32[256]{0:T(256)} %param.12) | copy-start | bytes 3076
  3.5 11.5 %collective-permute-start = (f32[3,24,128]{2,1,0:T(8,128)S(1)}, f32[3,24,128]{2,1,0:T(8,128)S(1)}, u32[]{:S(2)}, u32[]{:S(2)}) collective-permute-start(f32[3,24,128]{2,1,0:T(8,128)S(1)} %get-tuple-element.13), channel_id=1, source_target_pairs={{0,4},{4,8},{8,12},{1,5},{5,9},{9,13},{2,6},{6,10},{10,14},{3,7},{... | collective-permute-start | bytes 110600 | tf_op jit(solution)/shard_map/ppermute | solution.py:525
  8.7 6.3 %collective-permute-start.1 = (f32[3,24,128]{2,1,0:T(8,128)S(1)}, f32[3,24,128]{2,1,0:T(8,128)S(1)}, u32[]{:S(2)}, u32[]{:S(2)}) collective-permute-start(f32[3,24,128]{2,1,0:T(8,128)S(1)} %get-tuple-element.14), channel_id=1, source_target_pairs={{4,0},{8,4},{12,8},{5,1},{9,5},{13,9},{6,2},{10,6},{14,10},{7,3},{... | collective-permute-start | bytes 110600 | tf_op jit(solution)/shard_map/ppermute | solution.py:526

commit v13 on v12

--- a/solution.py
+++ b/solution.py
@@ -272,6 +272,19 @@
     last = sub_rows - 1
     cols = sub_cols // 2
 
+    def strip_total(s, k, h, a):
+        total = None
+        for i in (k - 1, k, k + 1):
+            if 0 <= i <= last:
+                v = p_ref[s, i, h, a]
+                total = v if total is None else total + v
+        return total
+
+    def mask_of(s, k, h):
+        return mask_ref[s, k].astype(jnp.float32)[:, h * cols : (h + 1) * cols]
+
+    modes = jnp.zeros((frames, modes_ref.shape[-1]), jnp.float32)
+    count = jnp.zeros((frames, LANES), jnp.float32)
     width = x_ref.shape[2]
     for s in range(sensors):
         clear_weights(wide_ref.at[s], sub_cols, width)
@@ -290,31 +303,6 @@
             for h in range(2):
                 for a in range(2):
                     p_ref[s, i, h, a] = out[h][a]
-
-    def strip_total(s, k, h, a):
-        total = None
-        for i in (k - 1, k, k + 1):
-            if 0 <= i <= last:
-                v = p_ref[s, i, h, a]
-                total = v if total is None else total + v
-        return total
-
-    def mask_of(s, k, h):
-        return mask_ref[s, k].astype(jnp.float32)[:, h * cols : (h + 1) * cols]
-
-    count = jnp.zeros((frames, LANES), jnp.float32)
-    for e, k in enumerate((0, last)):
-        order = [None] * 3
-        for s in range(sensors):
-            order[slot_of(k, s)] = s
-        for h in range(2):
-            m = side_by_side([mask_of(s, k, h) for s in order])
-            em_ref[e, h] = m
-            count = count + m
-            for a in range(2):
-                edge_ref[e, h, a] = by_slot([strip_total(s, k, h, a) for s in order], cols)
-    modes = jnp.zeros((frames, modes_ref.shape[-1]), jnp.float32)
-    for s in range(sensors):
         for g in range(1, last, 3):
             order = [None] * 3
             for k in range(g, min(g + 3, last)):
@@ -332,6 +320,16 @@
                     stacked(modes_ref, [None if k is None else (s, k) for k in order], h, cols),
                     preferred_element_type=jnp.float32,
                 )
+    for e, k in enumerate((0, last)):
+        order = [None] * 3
+        for s in range(sensors):
+            order[slot_of(k, s)] = s
+        for h in range(2):
+            m = side_by_side([mask_of(s, k, h) for s in order])
+            em_ref[e, h] = m
+            count = count + m
+            for a in range(2):
+                edge_ref[e, h, a] = by_slot([strip_total(s, k, h, a) for s in order], cols)
     pm_ref[...] = modes
     count_ref[...] = jnp.broadcast_to(0.5 * jnp.sum(count, axis=1, keepdims=True), count_ref.shape)
 

time: 31.1 us -> 31.7 us (1.019)
  Pallas kernels: 8.71 us -> 9.26 us
    pallas_call x1, Pallas kernels: 4.28 us -> 4.82 us  [body(): pl.pallas_call(functools.partial(kernel_moments, sub_rows, sub_cols, fram...]
  transfers between devices with their start and end apart: 2 -> 2, of which waited for: 0 -> 0; matrix products, arithmetic and copies ran while one was open for 0% -> 0% of each run, Pallas kernels for 14% -> 15%
where the time goes in v13:
time: 31.7 us; the launch traced here: 31.5 us
  blocking collectives  14.3 us (45%)
  Pallas kernels  9.26 us (29%)
  starting transfers between devices  6.49 us (20%)
  between operations  1.38 us (4%)
    all_to_all x1, blocking collectives, body(): info = lax.all_to_all(payload, ('tile', 'tm'), 0, 0)  14.3 us
    ppermute x1, starting transfers between devices, body(): from_before = lax.ppermute(up, 'tile', onward)  5.19 us
    pallas_call x1, Pallas kernels, body(): pl.pallas_call(functools.partial(kernel_moments, sub_rows, sub_cols, fram...  4.82 us
    pallas_call x1, Pallas kernels, body(): pl.pallas_call(functools.partial(kernel_halo, sub_rows, sub_cols, frames)...  2.81 us
    ppermute x1, starting transfers between devices, body(): from_after = lax.ppermute(down, 'tile', backward)  1.29 us
    pallas_call x1, Pallas kernels, body(): pl.pallas_call(functools.partial(kernel_smooth, tiles, blocks, frames, fl...  1.2 us
  transfers between devices with their start and end apart: 2, of which 0 were waited for; matrix products, arithmetic and copies ran while one was open for 0% of the time, Pallas kernels for 15%

profile of v13, /device:TPU:0, one launch (start us, length us, event | category | flops | bytes accessed | tf_op | source)
XLA Modules:
  0.0 31.5 jit_solution(4674218774688731823)
XLA Ops:
  0.6 0.0 copy-start
  0.6 0.0 copy-start.1
  0.7 0.0 copy-start.2
  0.7 2.8 %halo_moments.1 = (f32[3,24,128]{2,1,0:T(8,128)S(1)}, f32[3,24,128]{2,1,0:T(8,128)S(1)}, f32[3,5,8,128]{3,2,1,0:T(8,128)S(1)}, bf16[3,2,2,256,128]{4,3,2,1,0:T(8...) custom-call(bf16[3,2400,800]{2,1,0:T(8,128)(2,1)} %bitcast.7, ...), custom_call_target="tpu_custom_call" | custom-call | flops 393216000 | bytes 1536000 | tf_op jit(solution)/shard_map/halo_moments/pallas_call | solution.py:494
  3.5 5.2 %collective-permute-start = (f32[3,24,128]{2,1,0:T(8,128)S(1)}, f32[3,24,128]{2,1,0:T(8,128)S(1)}, u32[]{:S(2)}, u32[]{:S(2)}) collective-permute-start(f32[3,24,128]{2,1,0:T(8,128)S(1)} %get-tuple-element.13), channel_id=1, source_target_pairs={{0,4},{4,8},{8,12},{1,5},{5,9},{9,13},{2,6},{6,10},{10,14},{3,7},{... | collective-permute-start | bytes 110600 | tf_op jit(solution)/shard_map/ppermute | solution.py:523
  8.7 1.3 %collective-permute-start.1 = (f32[3,24,128]{2,1,0:T(8,128)S(1)}, f32[3,24,128]{2,1,0:T(8,128)S(1)}, u32[]{:S(2)}, u32[]{:S(2)}) collective-permute-start(f32[3,24,128]{2,1,0:T(8,128)S(1)} %get-tuple-element.14), channel_id=1, source_target_pairs={{4,0},{8,4},{12,8},{5,1},{9,5},{13,9},{6,2},{10,6},{14,10},{7,3},{... | collective-permute-start | bytes 110600 | tf_op jit(solution)/shard_map/ppermute | solution.py:524
  10.0 0.0 copy-done
  10.0 4.8 %moments.1 = (f32[24,256]{1,0:T(8,128)S(1)}, f32[2,2,2,24,128]{4,3,2,1,0:T(8,128)S(1)}, f32[2,2,24,128]{3,2,1,0:T(8,128)S(1)}, f32[24,128]{1,0:T(8,128)S(1)}) custom-call(bf16[3,2400,800]{2,1,0:T(8,128)(2,1)S(1)} %bitcast.8, f32[3,5,8,128]{3,2,1,0:T(8,128)S(1)} %get-tuple-element.15.geo_ref, ...), custom_call_target="tpu_custom_call" | custom-call | flops 2949120000 | bytes 11520000 | tf_op jit(solution)/shard_map/moments/pallas_call | solution.py:525
  15.5 0.0 collective-permute-done.before_ref
  15.5 0.0 collective-permute-done.1.after_ref
  15.5 0.0 copy-done.1
  15.5 0.4 %join_halo.1 = f32[16,13,1,128]{3,2,1,0:T(1,128)S(1)} custom-call(s32[1]{0:T(128)S(6)} %copy.9.live_ref, f32[3,24,128]{2,1,0:T(8,128)S(1)} %collective-permute-done.before_ref, f32[3,24,128]{2,1,0:T(8,128)S(1)} %collective-permute-done.1.after_ref, f32[24,256]{1,0:T(8,128)S(1)} %get-tuple-element.20.pm_ref, ...), custom_call_target="tpu_custom_call" | custom-call | tf_op jit(solution)/shard_map/join_halo/pallas_call | solution.py:547
  15.9 14.3 %all_to_all.5.in_ref = f32[16,13,1,128]{3,2,1,0:T(1,128)S(1)} all-to-all(f32[16,13,1,128]{3,2,1,0:T(1,128)S(1)} %join_halo.1), channel_id=1, replica_groups=mesh['grp'=2,'tile'=4,'tm'=4] {'tile','tm'}, dimensions={0} | all-to-all | bytes 212992 | tf_op jit(solution)/shard_map/all_to_all | solution.py:555
  30.3 0.0 copy-done.2
  30.3 1.2 %smooth.1 = (f32[24,64]{1,0:T(8,128)}, f32[24,64]{1,0:T(8,128)}) custom-call(f32[16,13,1,128]{3,2,1,0:T(1,128)S(1)} %all_to_all.5.in_ref, f32[1,256]{1,0:T(1,128)S(1)} %bitcast.11, f32[1,256]{1,0:T(1,128)S(1)} %bitcast.10), custom_call_target="tpu_custom_call" | custom-call | tf_op jit(solution)/shard_map/smooth/pallas_call | solution.py:556
Async XLA Ops:
  0.6 9.3 %copy-start = (bf16[3,24,100,800]{3,1,2,0:T(8,128)(2,1)S(1)}, bf16[3,24,100,800]{3,1,2,0:T(8,128)(2,1)}, u32[]{:S(2)}) copy-start(bf16[3,24,100,800]{3,1,2,0:T(8,128)(2,1)} %param.7) | copy-start | bytes 34560004
  0.6 14.8 %copy-start.1 = (f32[256]{0:T(256)S(1)}, f32[256]{0:T(256)}, u32[]{:S(2)}) copy-start(f32[256]{0:T(256)} %param.13) | copy-start | bytes 3076
  0.7 29.6 %copy-start.2 = (f32[256]{0:T(256)S(1)}, f32[256]{0:T(256)}, u32[]{:S(2)}) copy-start(f32[256]{0:T(256)} %param.12) | copy-start | bytes 3076
  3.5 12.0 %collective-permute-start = (f32[3,24,128]{2,1,0:T(8,128)S(1)}, f32[3,24,128]{2,1,0:T(8,128)S(1)}, u32[]{:S(2)}, u32[]{:S(2)}) collective-permute-start(f32[3,24,128]{2,1,0:T(8,128)S(1)} %get-tuple-element.13), channel_id=1, source_target_pairs={{0,4},{4,8},{8,12},{1,5},{5,9},{9,13},{2,6},{6,10},{10,14},{3,7},{... | collective-permute-start | bytes 110600 | tf_op jit(solution)/shard_map/ppermute | solution.py:523
  8.7 6.8 %collective-permute-start.1 = (f32[3,24,128]{2,1,0:T(8,128)S(1)}, f32[3,24,128]{2,1,0:T(8,128)S(1)}, u32[]{:S(2)}, u32[]{:S(2)}) collective-permute-start(f32[3,24,128]{2,1,0:T(8,128)S(1)} %get-tuple-element.14), channel_id=1, source_target_pairs={{4,0},{8,4},{12,8},{5,1},{9,5},{13,9},{6,2},{10,6},{14,10},{7,3},{... | collective-permute-start | bytes 110600 | tf_op jit(solution)/shard_map/ppermute | solution.py:524
